TPU v7x, 32 devices: a whole 2x2x4 slice. The times are simulated.
32 devices in a mesh: groups: 2 (over x), pos: 16 (over z, y, core).
Axes of the slice: x: 2, y: 2, z: 4, core: 2. Of those that a mesh axis runs over, the one named last changes fastest.
Arguments:
- activations: bfloat16 [32768, 512], P(('groups', 'pos')), parts along dimension 0, may hold values from -6 to 6
- kernel: bfloat16 [512, 5, 608], P('pos'), may hold values from -0.125 to 0.125
- cotangent: bfloat16 [16384, 608], P(('groups', 'pos')), parts along dimension 0, may hold values from -6 to 6
Outputs:
- pooled: bfloat16 [16384, 608], P(('groups', 'pos')), parts along dimension 0
- input_grad: bfloat16 [32768, 512], P(('groups', 'pos')), parts along dimension 0
- kernel_grad: float32 [1024, 5, 608], P(('groups', 'pos')), parts along dimension 0
There are 2 independent parts, one for each index of `groups`. A program takes and returns all parts, laid end to end along the dimension named above; an argument that names none is the same for every part. Nothing has to cross between parts.
All inputs are finite; a program needn't handle non-finite values.
Results may differ from a plain program's by a relative error of at most 0.0041.
Values may be sent and summed in bfloat16 or wider, within the bound.
No kernel may reach another device: no remote copies, remote signals or barrier semaphores. Data moves between devices by JAX's collectives and lax.ppermute only.
A program may use at most 128 MiB of HBM per device.

v0:
```python
import jax
import jax.numpy as jnp
from jax import lax
from jax.sharding import PartitionSpec as P

DILATION_STEP = 4


def extended(cells, sides, width):
    for axis, dim in sides:
        count = lax.axis_size(axis)
        ends = count - 1
        head = lax.slice_in_dim(cells, 0, width, axis=dim)
        tail = lax.slice_in_dim(cells, cells.shape[dim] - width, cells.shape[dim], axis=dim)
        cells = jnp.concatenate(
            [
                lax.ppermute(tail, axis, [(i, (i + 1) % count) for i in range(ends)]),
                cells,
                lax.ppermute(head, axis, [((i + 1) % count, i) for i in range(ends)]),
            ],
            axis=dim,
        )
    return cells


def gelu_value(v):
    return 0.5 * v * (1.0 + jax.scipy.special.erf(v * 0.7071067811865476))


def gelu_slope(v):
    return (
        0.5 * (1.0 + jax.scipy.special.erf(v * 0.7071067811865476))
        + v * jnp.exp(-0.5 * v * v) * 0.3989422804014327
    )


def on_device(activations, kernel, cotangent):
    window_length = activations.shape[0]
    kernel_taps = kernel.shape[1]
    out_width = kernel.shape[2]
    reach_row_count = (kernel_taps - 1) // 2 * DILATION_STEP
    values = activations.astype(jnp.float32)
    gelu = gelu_value(values).astype(jnp.bfloat16)
    padded_activation = extended(gelu, (("pos", 0),), reach_row_count)
    gelu_taps = jnp.stack(
        [
            padded_activation[
                tap_offset * DILATION_STEP : tap_offset * DILATION_STEP + window_length
            ]
            for tap_offset in range(kernel_taps)
        ]
    )
    kernel_full = lax.all_gather(kernel, "pos", axis=0, tiled=True)
    columns = gelu_taps
    dilated_output = jnp.einsum(
        "kpc,cko->po", columns, kernel_full, preferred_element_type=jnp.float32
    )
    pooled = (0.5 * dilated_output.reshape(window_length // 2, 2, out_width).sum(axis=1)).astype(
        jnp.bfloat16
    )
    convolution_gradient = (0.5 * jnp.repeat(cotangent.astype(jnp.float32), 2, axis=0)).astype(
        jnp.bfloat16
    )
    columns = gelu_taps
    kernel_grad = lax.psum_scatter(
        jnp.einsum(
            "kpc,po->cko", columns, convolution_gradient, preferred_element_type=jnp.float32
        ),
        "pos",
        scatter_dimension=0,
        tiled=True,
    )
    padded_gradient = extended(convolution_gradient, (("pos", 0),), reach_row_count)
    grad_taps = jnp.stack(
        [
            padded_gradient[
                (kernel_taps - 1 - tap_offset)
                * DILATION_STEP : (kernel_taps - 1 - tap_offset)
                * DILATION_STEP
                + window_length
            ]
            for tap_offset in range(kernel_taps)
        ]
    )
    block = jnp.einsum("kpo,cko->pc", grad_taps, kernel_full, preferred_element_type=jnp.float32)
    input_grad = (block * gelu_slope(values)).astype(jnp.bfloat16)
    return (pooled, input_grad, kernel_grad)


def solution(mesh):
    placed = (P(("groups", "pos"), None), P("pos", None, None), P(("groups", "pos"), None))
    return jax.shard_map(
        on_device,
        mesh=mesh,
        in_specs=placed,
        out_specs=(
            P(("groups", "pos"), None),
            P(("groups", "pos"), None),
            P(("groups", "pos"), None, None),
        ),
        check_vma=False,
    )
```

profile of v0, /device:TPU:9, one launch (start us, length us, event | category | flops | bytes accessed | tf_op | source)
XLA Modules:
  0.0 189.8 jit_solution(12694590104552449113)
XLA Ops:
  8.0 1.7 fusion.1
  9.6 2.6 %collective-permute-start.1 = (bf16[8,512]{1,0:T(8,128)(2,1)S(1)}, bf16[8,512]{1,0:T(8,128)(2,1)S(1)}, u32[]{:S(2)}, u32[]{:S(2)}) collective-permute-start(bf16[8,512]{1,0:T(8,128)(2,1)S(1)} %get-tuple-element.12), channel_id=1, source_target_pairs={{1,0},{2,1},{3,2},{4,3},{5,4},{6,5},{7,6},{8,7},{9,8},{10,9},{11,1... | collective-permute-start | bytes 24584 | tf_op jit(solution)/shard_map/ppermute | solution.py:19
  12.2 3.0 %collective-permute-start = (bf16[8,512]{1,0:T(8,128)(2,1)S(1)}, bf16[8,512]{1,0:T(8,128)(2,1)S(1)}, u32[]{:S(2)}, u32[]{:S(2)}) collective-permute-start(bf16[8,512]{1,0:T(8,128)(2,1)S(1)} %get-tuple-element.13), channel_id=1, source_target_pairs={{0,1},{1,2},{2,3},{3,4},{4,5},{5,6},{6,7},{7,8},{8,9},{9,10},{10,1... | collective-permute-start | bytes 24584 | tf_op jit(solution)/shard_map/ppermute | solution.py:17
  16.4 1.9 convert_element_type.38
  20.4 2.3 %copy-done.5 = bf16[5,1024,512]{2,1,0:T(8,128)(2,1)} copy-done((bf16[5,1024,512]{2,1,0:T(8,128)(2,1)}, bf16[5,1024,512]{2,1,0:T(8,128)(2,1)S(1)}, u32[]{:S(2)}) %copy-start.5) | copy-done | bytes 5242904
  22.7 5.4 %convolution_bitcast_fusion = f32[512,5,608]{0,2,1:T(8,128)} fusion(bf16[5,1024,512]{2,1,0:T(8,128)(2,1)S(1)} %fusion.27, bf16[1024,608]{1,0:T(8,128)(2,1)S(1)} %copy-done), kind=kOutput, calls=%fused_computation.5 | convolution fusion | flops 3187671040 | bytes 12713984 | tf_op jit(solution)/shard_map/kpc,po->cko/dot_general | solution.py:66
  28.1 10.9 %copy.26 = f32[512,5,608]{2,1,0:T(8,128)} copy(f32[512,5,608]{0,2,1:T(8,128)} %convolution_bitcast_fusion) | data formatting | bytes 12451840 | tf_op jit(solution)/shard_map/kpc,po->cko/transpose | solution.py:66
  39.8 1.9 %collective-permute-start.2 = (bf16[8,608]{0,1:T(8,128)(2,1)}, bf16[8,608]{0,1:T(8,128)(2,1)}, u32[]{:S(2)}, u32[]{:S(2)}) collective-permute-start(bf16[8,608]{0,1:T(8,128)(2,1)} %copy.20), channel_id=1, source_target_pairs={{1,0},{2,1},{3,2},{4,3},{5,4},{6,5},{7,6},{8,7},{9,8},{10,9},{11,1... | collective-permute-start | bytes 29192 | tf_op jit(solution)/shard_map/ppermute | solution.py:19
  42.6 3.8 %collective-permute-start.3 = (bf16[8,608]{0,1:T(8,128)(2,1)}, bf16[8,608]{0,1:T(8,128)(2,1)S(1)}, u32[]{:S(2)}, u32[]{:S(2)}) collective-permute-start(bf16[8,608]{0,1:T(8,128)(2,1)} %copy.22), channel_id=1, source_target_pairs={{0,1},{1,2},{2,3},{3,4},{4,5},{5,6},{6,7},{7,8},{8,9},{9,10},{10,1... | collective-permute-start | bytes 29192 | tf_op jit(solution)/shard_map/ppermute | solution.py:17
  46.4 1.9 convert_element_type.39
  48.9 1.6 copy.24
  50.5 2.6 %fusion.15 = bf16[5,1024,608]{1,2,0:T(8,128)(2,1)} fusion(bf16[1024,608]{0,1:T(8,128)(2,1)S(1)} %copy.21, bf16[8,608]{0,1:T(8,128)(2,1)} %collective-permute-done.2), kind=kLoop, calls=%fused_computation.28 | loop fusion | flops 2490367 | bytes 2500096
  53.1 2.7 %fusion.19 = bf16[5,1024,608]{1,2,0:T(8,128)(2,1)} fusion(bf16[5,1024,608]{1,2,0:T(8,128)(2,1)} %fusion.15, bf16[8,608]{0,1:T(8,128)(2,1)} %collective-permute-done.2, bf16[1024,608]{0,1:T(8,128)(2,1)S(1)} %copy.21), kind=kLoop, calls=%fused_computation.34 | loop fusion | flops 2490368 | bytes 2646016
  55.8 1.1 constant_dynamic-update-slice_fusion
  56.9 1.7 fusion.12
  58.6 1.7 fusion.17
  60.3 9.3 %convolution_bitcast_fusion.1 = f32[1024,608]{1,0:T(8,128)} fusion(bf16[5,1024,512]{2,1,0:T(8,128)(2,1)} %copy-done.5, bf16[512,5,608]{2,0,1:T(8,128)(2,1)} %all-gather.2.cloned.1.call-done), kind=kOutput, calls=%fused_computation.15 | convolution fusion | flops 3187671040 | bytes 10846208 | tf_op jit(solution)/shard_map/kpc,cko->po/dot_general | solution.py:55
  69.5 3.7 %reshape.31 = f32[512,2,608]{2,1,0:T(2,128)S(1)} reshape(f32[1024,608]{1,0:T(8,128)} %convolution_bitcast_fusion.1) | data formatting | bytes 4980736 | tf_op jit(solution)/shard_map/reshape | solution.py:58
  73.2 4.6 %reduce_sum.9 = f32[512,608]{1,0:T(8,128)} reduce(f32[512,2,608]{2,1,0:T(2,128)S(1)} %reshape.31, f32[]{:T(128)} %constant.1.clone.1), dimensions={1}, to_apply=%region_0.0 | reduce | flops 311296 | bytes 3735556 | tf_op jit(solution)/shard_map/reduce_sum | solution.py:58
  77.8 1.7 multiply_convert_fusion.1
  79.5 1.1 copy.27
  80.5 10.1 %fusion.8 = bf16[1024,512]{1,0:T(8,128)(2,1)} fusion(bf16[1024,512]{1,0:T(8,128)(2,1)S(1)} %copy-done.3, bf16[5,1024,608]{1,2,0:T(8,128)(2,1)} %fusion.17, bf16[512,5,608]{2,0,1:T(8,128)(2,1)} %all-gather.2.cloned.1.call-done), kind=kOutput, calls=%fused_computation.14 | convolution fusion | flops 3193438208 | bytes 11436032 | tf_op jit(solution)/shard_map/kpo,cko->pc/dot_general | solution.py:85
  90.7 90.4 %reduce-scatter.2.cloned.1.call-done = f32[32,5,608]{2,1,0:T(8,128)} async-done(((f32[512,5,608]{2,1,0:T(8,128)}), f32[32,5,608]{2,1,0:T(8,128)}) %reduce-scatter.2.cloned.1.call-update) | async-done | bytes 389136 | tf_op jit(solution)/shard_map/reduce_scatter | solution.py:65
  181.1 1.9 %copy.28 = f32[32,5,608]{2,0,1:T(8,128)} copy(f32[32,5,608]{2,1,0:T(8,128)} %reduce-scatter.2.cloned.1.call-done) | data formatting | bytes 778240
  (37 shorter events, 6.2 us)
Async XLA Ops:
  7.2 8.1 %copy-start.4 = (bf16[512,608]{0,1:T(8,128)(2,1)S(1)}, bf16[512,608]{0,1:T(8,128)(2,1)}, u32[]{:S(2)}) copy-start(bf16[512,608]{0,1:T(8,128)(2,1)} %param.5) | copy-start | bytes 1867780
  7.2 53.1 %all-gather.2.cloned.1.call-start = ((), (), s32[]{:S(2)}) async-start(), calls=%async_computation.1 | async-start | bytes 3481600 | tf_op jit(solution)/shard_map/all_gather | solution.py:53
  7.9 173.2 %reduce-scatter.2.cloned.1.call-start = ((), (), s32[]{:S(2)}) async-start(), calls=%async_computation.2 | async-start | bytes 11141120 | tf_op jit(solution)/shard_map/reduce_scatter | solution.py:65
  9.6 10.4 %collective-permute-start.1 = (bf16[8,512]{1,0:T(8,128)(2,1)S(1)}, bf16[8,512]{1,0:T(8,128)(2,1)S(1)}, u32[]{:S(2)}, u32[]{:S(2)}) collective-permute-start(bf16[8,512]{1,0:T(8,128)(2,1)S(1)} %get-tuple-element.12), channel_id=1, source_target_pairs={{1,0},{2,1},{3,2},{4,3},{5,4},{6,5},{7,6},{8,7},{9,8},{10,9},{11,1... | collective-permute-start | bytes 24584 | tf_op jit(solution)/shard_map/ppermute | solution.py:19
  12.2 6.1 %collective-permute-start = (bf16[8,512]{1,0:T(8,128)(2,1)S(1)}, bf16[8,512]{1,0:T(8,128)(2,1)S(1)}, u32[]{:S(2)}, u32[]{:S(2)}) collective-permute-start(bf16[8,512]{1,0:T(8,128)(2,1)S(1)} %get-tuple-element.13), channel_id=1, source_target_pairs={{0,1},{1,2},{2,3},{3,4},{4,5},{5,6},{6,7},{7,8},{8,9},{9,10},{10,1... | collective-permute-start | bytes 24584 | tf_op jit(solution)/shard_map/ppermute | solution.py:17
  18.3 1.3 copy-start.2
  20.0 2.7 %copy-start = (bf16[1024,608]{1,0:T(8,128)(2,1)S(1)}, bf16[1024,608]{1,0:T(8,128)(2,1)}, u32[]{:S(2)}) copy-start(bf16[1024,608]{1,0:T(8,128)(2,1)} %convert_element_type.38) | copy-start | bytes 3735556
  20.3 2.3 %copy-start.5 = (bf16[5,1024,512]{2,1,0:T(8,128)(2,1)}, bf16[5,1024,512]{2,1,0:T(8,128)(2,1)S(1)}, u32[]{:S(2)}) copy-start(bf16[5,1024,512]{2,1,0:T(8,128)(2,1)S(1)} %fusion.27) | copy-start | bytes 15728644
  38.9 9.3 %copy-start.1 = (bf16[1024,608]{1,0:T(8,128)(2,1)S(1)}, bf16[1024,608]{1,0:T(8,128)(2,1)}, u32[]{:S(2)}) copy-start(bf16[1024,608]{1,0:T(8,128)(2,1)} %convert_element_type.38) | copy-start | bytes 3735556
  39.8 10.7 %collective-permute-start.2 = (bf16[8,608]{0,1:T(8,128)(2,1)}, bf16[8,608]{0,1:T(8,128)(2,1)}, u32[]{:S(2)}, u32[]{:S(2)}) collective-permute-start(bf16[8,608]{0,1:T(8,128)(2,1)} %copy.20), channel_id=1, source_target_pairs={{1,0},{2,1},{3,2},{4,3},{5,4},{6,5},{7,6},{8,7},{9,8},{10,9},{11,1... | collective-permute-start | bytes 29192 | tf_op jit(solution)/shard_map/ppermute | solution.py:19
  42.6 14.3 %collective-permute-start.3 = (bf16[8,608]{0,1:T(8,128)(2,1)}, bf16[8,608]{0,1:T(8,128)(2,1)S(1)}, u32[]{:S(2)}, u32[]{:S(2)}) collective-permute-start(bf16[8,608]{0,1:T(8,128)(2,1)} %copy.22), channel_id=1, source_target_pairs={{0,1},{1,2},{2,3},{3,4},{4,5},{5,6},{6,7},{7,8},{8,9},{9,10},{10,1... | collective-permute-start | bytes 29192 | tf_op jit(solution)/shard_map/ppermute | solution.py:17
  77.8 2.7 %copy-start.3 = (bf16[1024,512]{1,0:T(8,128)(2,1)S(1)}, bf16[1024,512]{1,0:T(8,128)(2,1)}, u32[]{:S(2)}) copy-start(bf16[1024,512]{1,0:T(8,128)(2,1)} %param.3) | copy-start | bytes 3145732
Sparse Core Ops, SparseCore 0:
  10.3 49.3 all-gather.1
  63.7 117.3 reduce-scatter.1
where the time goes:
time: 192 us; the launch traced here: 190 us
  waiting for transfers between devices  91.1 us (47%)
  local copies, waits for them, and re-layouts  30.5 us (16%)
  matrix products  24.8 us (13%)
  other arithmetic  17.7 us (9%)
  between operations  14.3 us (7%)
  starting transfers between devices  11.4 us (6%)
    reduce_scatter x1, waiting for transfers between devices, on_device(): lax.psum_scatter(jnp.einsum('kpc,po->cko', columns, convolution_gradient,...  90.4 us
    transpose x1, local copies, waits for them, and re-layouts, on_device(): jnp.einsum('kpc,po->cko', columns, convolution_gradient, preferred_elemen...  10.9 us
    dot_general x1, matrix products, on_device(): jnp.einsum('kpo,cko->pc', grad_taps, kernel_full, preferred_element_type=...  10.1 us
    dot_general x1, matrix products, on_device(): jnp.einsum('kpc,cko->po', columns, kernel_full, preferred_element_type=jn...  9.26 us
    unnamed x7, other arithmetic  7.92 us
    unnamed x16, local copies, waits for them, and re-layouts  7.66 us
    ppermute x2, starting transfers between devices, extended(): lax.ppermute(tail, axis, [(i, (i + 1) % count) for i in range(ends)])  6.86 us
    convert_element_type x4, local copies, waits for them, and re-layouts, on_device(): (0.5 * jnp.repeat(cotangent.astype(jnp.float32), 2, axis=0)).astype(jnp.b...  6 us
  transfers between devices with their start and end apart: 6, of which 1 were waited for; matrix products, arithmetic and copies ran while one was open for 36% of the time, Pallas kernels for 0%

commit v1 on v0

v1 whole, which is shorter than its diff:
```python
import functools

import jax
import jax.numpy as jnp
from jax import lax
from jax.experimental import pallas as pl
from jax.experimental.pallas import tpu as pltpu
from jax.sharding import PartitionSpec as P

STEP = 4
TAPS = 5
HALO = 16
TEAM = 4
EXT = 8
VMEM = pl.BlockSpec(memory_space=pltpu.VMEM)
SMEM = pl.BlockSpec(memory_space=pltpu.SMEM)
F32 = jnp.float32
BF16 = jnp.bfloat16


def params(mib):
    return pltpu.CompilerParams(vmem_limit_bytes=mib * 2**20)


def gelu_value(v):
    return 0.5 * v * (1.0 + lax.erf(v * 0.7071067811865476))


def gelu_slope(v):
    return (
        0.5 * (1.0 + lax.erf(v * 0.7071067811865476))
        + v * jnp.exp(-0.5 * v * v) * 0.3989422804014327
    )


def relative_order(place, rows, channels, transposed):
    shape = (channels, channels)
    chan = lax.broadcasted_iota(jnp.int32, shape, 1 if transposed else 0)
    col = lax.broadcasted_iota(jnp.int32, shape, 0 if transposed else 1)
    quarter = channels // TEAM
    mate = lax.div(col, quarter)
    within = lax.rem(col, quarter)
    level = lax.div(within, rows)
    row = lax.rem(within, rows)
    want = rows * (TEAM * (level ^ place[0]) + (mate ^ place[1])) + row
    return jnp.where(chan == want, 1.0, 0.0).astype(BF16)


def pool_kernel(rows, place, act, low, high, own, near, far):
    channels = act.shape[1]
    quarter = channels // TEAM
    order = relative_order(place, rows, channels, False)

    def pooled(g):
        t = g.shape[0]
        u = lax.broadcasted_iota(jnp.int32, (t // 2, t), 0)
        v = lax.broadcasted_iota(jnp.int32, (t // 2, t), 1)
        halves = jnp.where(lax.div(v, 2) == u, 0.5, 0.0).astype(BF16)
        s = jnp.dot(halves, g, preferred_element_type=F32).astype(BF16)
        return jnp.dot(s, order, preferred_element_type=F32).astype(BF16)

    def put(at, s):
        n = s.shape[0]
        own[at : at + n, :] = s[:, :quarter]
        near[at : at + n, :] = s[:, quarter : 2 * quarter]
        far[at : at + n, :] = s[:, 2 * quarter :]

    def gelu(v):
        return gelu_value(v.astype(F32)).astype(BF16)

    window = act.shape[0]
    block = 256
    g_prev = gelu(low[...])
    for at in range(0, window, block):
        g = gelu(act[at : at + block, :])
        joined = jnp.concatenate([g_prev, g[: block - HALO]], axis=0)
        put(at // 2, pooled(joined))
        g_prev = g[block - HALO :]
    put(window // 2, pooled(jnp.concatenate([g_prev, gelu(high[...])], axis=0)))


def wgrad_kernel(rows, s0, s1, s2, s3, c0, c1, c2, c3, *refs):
    *outs, left = refs
    positions = c0.shape[1]
    quarter = s0.shape[1]
    total = None
    for s, c in ((s0, c0), (s1, c1), (s2, c2), (s3, c3)):
        for k in range(TAPS):
            at = EXT + 2 * (k - 2)
            left[k * quarter : (k + 1) * quarter, :] = s[at : at + positions, :].T
        term = lax.dot_general(
            left[...], c[...], (((1,), (1,)), ((), ())), preferred_element_type=F32
        )
        total = term if total is None else total + term
    if len(outs) == 1:
        for k in range(TAPS):
            outs[0][k] = total[k * quarter : (k + 1) * quarter]
    else:
        for k in range(TAPS):
            for m, out in enumerate(outs):
                at = k * quarter + m * rows
                out[k] = total[at : at + rows].astype(out.dtype)


def fill_ext(ext, cot, low, high):
    positions = cot.shape[0]
    ext[:HALO, :] = low[...]
    ext[HALO : HALO + positions, :] = cot[...]
    ext[HALO + positions :, :] = high[...]


def pair_products(s_pair, k_pair, ext, positions):
    acc = None
    grad = None
    for k in range(TAPS):
        at = EXT + 2 * (k - 2)
        weights = k_pair(k)
        term = jnp.dot(s_pair(at), weights, preferred_element_type=F32)
        acc = term if acc is None else acc + term
        back = HALO - 2 * (k - 2)
        term = lax.dot_general(
            ext[back : back + positions, :],
            weights,
            (((1,), (1,)), ((), ())),
            preferred_element_type=F32,
        )
        grad = term if grad is None else grad + term
    return acc, grad


def first_kernel(rows, place, own, near, k0, k1, cot, low, high, act, acc, grad, slope, ext):
    positions = cot.shape[0]
    fill_ext(ext, cot, low, high)
    acc[...], grad[...] = pair_products(
        lambda at: jnp.concatenate([own[at : at + positions], near[at : at + positions]], axis=1),
        lambda k: jnp.concatenate([k0[k], k1[k]], axis=0),
        ext,
        positions,
    )
    order = relative_order(place, rows, act.shape[1], False)
    block = 256
    for at in range(0, act.shape[0], block):
        v = jnp.dot(act[at : at + block, :], order, preferred_element_type=F32)
        slope[at : at + block, :] = 0.5 * gelu_slope(v)


def second_kernel(
    rows, place, far, k2, k3, cot, low, high, acc1, grad1, slope, pooled, out, ext, doubled
):
    positions = cot.shape[0]
    channels = out.shape[1]
    half = channels // 2
    fill_ext(ext, cot, low, high)
    acc, grad = pair_products(
        lambda at: far[at : at + positions, :],
        lambda k: jnp.concatenate([k2[k], k3[k]], axis=0),
        ext,
        positions,
    )
    pooled[...] = (acc + acc1[...]).T.astype(BF16)
    lanes = doubled.shape[2]
    for j in range(channels // lanes):
        g = grad1[:, j * lanes : (j + 1) * lanes] if j * lanes < half else grad[:, j * lanes - half : (j + 1) * lanes - half]
        doubled[j, pl.ds(0, positions, 2), :] = g
        doubled[j, pl.ds(1, positions, 2), :] = g
    back = relative_order(place, rows, channels, True)
    block = 256
    for at in range(0, 2 * positions, block):
        pieces = [
            (doubled[j, at : at + block, :] * slope[at : at + block, j * lanes : (j + 1) * lanes]).astype(BF16)
            for j in range(channels // lanes)
        ]
        mixed = jnp.concatenate(pieces, axis=1)
        out[at : at + block, :] = jnp.dot(mixed, back, preferred_element_type=F32).astype(BF16)


def flip(x, bit):
    n = lax.axis_size("pos")
    return lax.ppermute(x, "pos", [(i, i ^ bit) for i in range(n)])


def on_device(activations, kernel, cotangent):
    window, channels = activations.shape
    positions, width = cotangent.shape
    rows = kernel.shape[0]
    n = lax.axis_size("pos")
    levels = n // TEAM
    quarter = channels // TEAM
    me = lax.axis_index("pos")
    place = jnp.stack([me // TEAM, me % TEAM]).astype(jnp.int32)

    cot_t = cotangent.T
    shard = kernel.transpose(1, 0, 2)

    cot_y = flip(cot_t, 2)
    shards = [shard] + [flip(shard, TEAM * m) for m in range(1, levels)]
    edge_low = jnp.concatenate([activations[-HALO:], cotangent[-HALO:]], axis=1)
    edge_high = jnp.concatenate([activations[:HALO], cotangent[:HALO]], axis=1)
    low = lax.ppermute(edge_low, "pos", [(i, i + 1) for i in range(n - 1)])
    high = lax.ppermute(edge_high, "pos", [(i + 1, i) for i in range(n - 1)])
    cot_c = flip(cot_t, 1)

    ext_rows = positions + 2 * EXT
    own, near, far = pl.pallas_call(
        functools.partial(pool_kernel, rows),
        out_shape=[
            jax.ShapeDtypeStruct((ext_rows, quarter), BF16),
            jax.ShapeDtypeStruct((ext_rows, quarter), BF16),
            jax.ShapeDtypeStruct((ext_rows, 2 * quarter), BF16),
        ],
        in_specs=[SMEM, VMEM, VMEM, VMEM],
        out_specs=[VMEM] * 3,
        compiler_params=params(32),
        name="pool",
    )(place, activations, low[:, :channels], high[:, :channels])

    far_y = flip(far, 2)
    near_c = flip(near, 1)
    cot_yc = flip(cot_y, 1)
    far_yc = flip(far_y, 1)

    split = rows % 16 == 0
    if split:
        grad_shape = [
            jax.ShapeDtypeStruct((TAPS, rows, width), F32 if m == 0 else BF16)
            for m in range(levels)
        ]
    else:
        grad_shape = [jax.ShapeDtypeStruct((TAPS, quarter, width), F32)]
    grads = pl.pallas_call(
        functools.partial(wgrad_kernel, rows),
        out_shape=grad_shape,
        in_specs=[VMEM] * 8,
        out_specs=[VMEM] * len(grad_shape),
        scratch_shapes=[pltpu.VMEM((TAPS * quarter, positions), BF16)],
        compiler_params=params(48),
        name="wgrad",
    )(own, near_c, far_y[:, :quarter], far_yc[:, quarter:], cot_t, cot_c, cot_y, cot_yc)
    if not split:
        parts = [grads[0][:, m * rows : (m + 1) * rows] for m in range(levels)]
        grads = [parts[0]] + [p.astype(BF16) for p in parts[1:]]
    total = grads[0]
    for m in range(1, levels):
        total = total + flip(grads[m], TEAM * m).astype(F32)
    kernel_grad = total.transpose(1, 0, 2)

    k0 = jnp.concatenate(shards, axis=1)
    k2 = flip(k0, 2)
    k1 = flip(k0, 1)
    k3 = flip(k2, 1)

    low_cot, high_cot = low[:, channels:], high[:, channels:]
    acc, grad, slope = pl.pallas_call(
        functools.partial(first_kernel, rows),
        out_shape=[
            jax.ShapeDtypeStruct((positions, width), F32),
            jax.ShapeDtypeStruct((positions, channels // 2), F32),
            jax.ShapeDtypeStruct((window, channels), F32),
        ],
        in_specs=[SMEM] + [VMEM] * 8,
        out_specs=[VMEM] * 3,
        scratch_shapes=[pltpu.VMEM((positions + 2 * HALO, width), BF16)],
        compiler_params=params(48),
        name="first",
    )(place, own, near, k0, k1, cotangent, low_cot, high_cot, activations)
    pooled_t, input_grad = pl.pallas_call(
        functools.partial(second_kernel, rows),
        out_shape=[
            jax.ShapeDtypeStruct((width, positions), BF16),
            jax.ShapeDtypeStruct((window, channels), BF16),
        ],
        in_specs=[SMEM] + [VMEM] * 9,
        out_specs=[VMEM] * 2,
        scratch_shapes=[
            pltpu.VMEM((positions + 2 * HALO, width), BF16),
            pltpu.VMEM((channels // 128, window, 128), F32),
        ],
        compiler_params=params(48),
        name="second",
    )(place, far, k2, k3, cotangent, low_cot, high_cot, acc, grad, slope)
    return pooled_t.T, input_grad, kernel_grad


def solution(mesh):
    placed = (P(("groups", "pos"), None), P("pos", None, None), P(("groups", "pos"), None))
    return jax.shard_map(
        on_device,
        mesh=mesh,
        in_specs=placed,
        out_specs=(
            P(("groups", "pos"), None),
            P(("groups", "pos"), None),
            P(("groups", "pos"), None, None),
        ),
        check_vma=False,
    )
```

time: 192 us -> 94 us (0.49)
  the two profiles are of different devices: /device:TPU:9 before, /device:TPU:0 now
where the time goes in v1:
time: 94 us; the launch traced here: 93.5 us
  starting transfers between devices  30 us (32%)
  waiting for transfers between devices  28.3 us (30%)
  Pallas kernels  17.2 us (18%)
  local copies, waits for them, and re-layouts  14.1 us (15%)
  other arithmetic  3.06 us (3%)
    ppermute x15, starting transfers between devices, flip(): return lax.ppermute(x, 'pos', [(i, i ^ bit) for i in range(n)])  27.4 us
    ppermute x15, waiting for transfers between devices, flip(): return lax.ppermute(x, 'pos', [(i, i ^ bit) for i in range(n)])  25.8 us
    pallas_call x1, Pallas kernels, on_device(): pl.pallas_call(functools.partial(second_kernel, rows), out_shape=[jax.Sha...  6.51 us
    unnamed x29, local copies, waits for them, and re-layouts  6.25 us
    ppermute x3, local copies, waits for them, and re-layouts, flip(): return lax.ppermute(x, 'pos', [(i, i ^ bit) for i in range(n)])  5.51 us
    pallas_call x1, Pallas kernels, on_device(): pl.pallas_call(functools.partial(first_kernel, rows), out_shape=[jax.Shap...  4.74 us
    pallas_call x1, Pallas kernels, on_device(): pl.pallas_call(functools.partial(wgrad_kernel, rows), out_shape=grad_shap...  4.17 us
    ppermute x1, waiting for transfers between devices, on_device(): high = lax.ppermute(edge_high, 'pos', [(i + 1, i) for i in range(n - 1)])  2.45 us
  transfers between devices with their start and end apart: 17, of which 7 were waited for; matrix products, arithmetic and copies ran while one was open for 11% of the time, Pallas kernels for 11%

profile of v1, /device:TPU:0, one launch (start us, length us, event | category | flops | bytes accessed | tf_op | source)
XLA Modules:
  0.0 93.5 jit_solution(4935377639007678396)
XLA Ops:
  0.6 5.1 %collective-permute-start.4 = (bf16[5,32,608]{2,1,0:T(8,128)(2,1)}, bf16[5,32,608]{2,1,0:T(8,128)(2,1)S(1)}, u32[]{:S(2)}, u32[]{:S(2)}) collective-permute-start(bf16[5,32,608]{2,1,0:T(8,128)(2,1)} %bitcast.10), channel_id=1, source_target_pairs={{0,12},{1,13},{2,14},{3,15},{4,8},{5,9},{6,10},{7,11},{8,4},{9,5},... | collective-permute-start | bytes 583688 | tf_op jit(solution)/shard_map/ppermute | solution.py:179
  6.4 1.7 %collective-permute-start.12 = (bf16[608,512]{1,0:T(8,128)(2,1)}, bf16[608,512]{1,0:T(8,128)(2,1)}, u32[]{:S(2)}, u32[]{:S(2)}) collective-permute-start(bf16[608,512]{1,0:T(8,128)(2,1)} %bitcast.7), channel_id=1, source_target_pairs={{0,2},{1,3},{2,0},{3,1},{4,6},{5,7},{6,4},{7,5},{8,10},{9,11},{10,... | collective-permute-start | bytes 1867784 | tf_op jit(solution)/shard_map/ppermute | solution.py:179
  8.1 1.4 %copy.10.cot = bf16[512,608]{1,0:T(8,128)(2,1)S(1)} copy(bf16[512,608]{0,1:T(8,128)(2,1)} %param.5) | data formatting | bytes 1245184 | tf_op args[2]
  10.2 1.8 %collective-permute-done.4 = bf16[5,32,608]{2,1,0:T(8,128)(2,1)S(1)} collective-permute-done((bf16[5,32,608]{2,1,0:T(8,128)(2,1)}, bf16[5,32,608]{2,1,0:T(8,128)(2,1)S(1)}, u32[]{:S(2)}, u32[]{:S(2)}) %collective-permute-start.4) | collective-permute-done | bytes 194592 | tf_op jit(solution)/shard_map/ppermute | solution.py:179
  12.0 11.3 %collective-permute-done.3 = bf16[5,32,608]{2,1,0:T(8,128)(2,1)S(1)} collective-permute-done((bf16[5,32,608]{2,1,0:T(8,128)(2,1)}, bf16[5,32,608]{2,1,0:T(8,128)(2,1)S(1)}, u32[]{:S(2)}, u32[]{:S(2)}) %collective-permute-start.3) | collective-permute-done | bytes 194592 | tf_op jit(solution)/shard_map/ppermute | solution.py:179
  24.4 1.5 %copy.12 = bf16[5,128,608]{1,2,0:T(8,128)(2,1)} copy(bf16[5,128,608]{2,1,0:T(8,128)(2,1)S(1)} %pad_maximum_fusion.k0) | data formatting | bytes 1556480 | tf_op jit(solution)/shard_map/concatenate | solution.py:247
  25.9 1.5 %collective-permute-start.5 = (bf16[5,128,608]{1,2,0:T(8,128)(2,1)}, bf16[5,128,608]{1,2,0:T(8,128)(2,1)}, u32[]{:S(2)}, u32[]{:S(2)}) collective-permute-start(bf16[5,128,608]{1,2,0:T(8,128)(2,1)} %copy.12), channel_id=1, source_target_pairs={{0,2},{1,3},{2,0},{3,1},{4,6},{5,7},{6,4},{7,5},{8,10},{9,11},{10,... | collective-permute-start | bytes 2334728 | tf_op jit(solution)/shard_map/ppermute | solution.py:179
  27.4 1.3 %collective-permute-start = (bf16[16,1120]{1,0:T(8,128)(2,1)S(1)}, bf16[16,1120]{1,0:T(8,128)(2,1)S(1)}, u32[]{:S(2)}, u32[]{:S(2)}) collective-permute-start(bf16[16,1120]{1,0:T(8,128)(2,1)S(1)} %pad_maximum_fusion.1), channel_id=1, source_target_pairs={{0,1},{1,2},{2,3},{3,4},{4,5},{5,6},{6,7},{7,8},{8,9},{9,10},{10,1... | collective-permute-start | bytes 107528 | tf_op jit(solution)/shard_map/ppermute | solution.py:199
  28.7 1.3 %collective-permute-start.1 = (bf16[16,1120]{1,0:T(8,128)(2,1)S(1)}, bf16[16,1120]{1,0:T(8,128)(2,1)S(1)}, u32[]{:S(2)}, u32[]{:S(2)}) collective-permute-start(bf16[16,1120]{1,0:T(8,128)(2,1)S(1)} %pad_maximum_fusion.2), channel_id=1, source_target_pairs={{1,0},{2,1},{3,2},{4,3},{5,4},{6,5},{7,6},{8,7},{9,8},{10,9},{11,1... | collective-permute-start | bytes 107528 | tf_op jit(solution)/shard_map/ppermute | solution.py:200
  30.1 2.4 %collective-permute-done.1 = bf16[16,1120]{1,0:T(8,128)(2,1)S(1)} collective-permute-done((bf16[16,1120]{1,0:T(8,128)(2,1)S(1)}, bf16[16,1120]{1,0:T(8,128)(2,1)S(1)}, u32[]{:S(2)}, u32[]{:S(2)}) %collective-permute-start.1) | collective-permute-done | bytes 35872 | tf_op jit(solution)/shard_map/ppermute | solution.py:200
  32.6 1.8 %pool.1 = (bf16[528,128]{1,0:T(8,128)(2,1)S(1)}, bf16[528,128]{1,0:T(8,128)(2,1)S(1)}, bf16[528,256]{1,0:T(8,128)(2,1)S(1)}) custom-call(s32[2]{0:T(128)S(1)} %pad_add_fusion.place, bf16[1024,512]{1,0:T(8,128)(2,1)S(1)} %copy-done, bf16[16,512]{1,0:T(8,128)(2,1)S(1)} %slice.41.low, bf16[16,512]{1,0:T(8,128)(2,1)S(1)} %slice.43.high), custom_call_target="tpu_custom_call" | custom-call | tf_op jit(solution)/shard_map/pool/pallas_call | solution.py:204
  34.4 12.8 %collective-permute-start.9 = (bf16[528,256]{1,0:T(8,128)(2,1)S(1)}, bf16[528,256]{1,0:T(8,128)(2,1)S(1)}, u32[]{:S(2)}, u32[]{:S(2)}) collective-permute-start(bf16[528,256]{1,0:T(8,128)(2,1)S(1)} %get-tuple-element.15.far), channel_id=1, source_target_pairs={{0,2},{1,3},{2,0},{3,1},{4,6},{5,7},{6,4},{7,5},{8,10},{9,11},{10,... | collective-permute-start | bytes 811016 | tf_op jit(solution)/shard_map/ppermute | solution.py:179
  47.8 6.4 %collective-permute-done.9 = bf16[528,256]{1,0:T(8,128)(2,1)S(1)} collective-permute-done((bf16[528,256]{1,0:T(8,128)(2,1)S(1)}, bf16[528,256]{1,0:T(8,128)(2,1)S(1)}, u32[]{:S(2)}, u32[]{:S(2)}) %collective-permute-start.9) | collective-permute-done | bytes 270368 | tf_op jit(solution)/shard_map/ppermute | solution.py:179
  57.1 4.2 %wgrad.1 = (f32[5,32,608]{2,1,0:T(8,128)S(1)}, bf16[5,32,608]{2,1,0:T(8,128)(2,1)}, bf16[5,32,608]{2,1,0:T(8,128)(2,1)}, bf16[5,32,608]{2,1,0:T(8,128)(2,1)}) custom-call(bf16[528,128]{1,0:T(8,128)(2,1)S(1)} %get-tuple-element.16.own.s0, bf16[528,128]{1,0:T(8,128)(2,1)S(1)} %collective-permute-done.8.s1, bf16[528,128]{1,0:T(8,128)(2,1)S(1)} %slice.46.s2, ...), custom_call_target="tpu_custom_call" | custom-call | tf_op jit(solution)/shard_map/wgrad/pallas_call | solution.py:230
  62.0 1.9 %collective-permute-start.16 = (bf16[5,32,608]{2,1,0:T(8,128)(2,1)}, bf16[5,32,608]{2,1,0:T(8,128)(2,1)}, u32[]{:S(2)}, u32[]{:S(2)}) collective-permute-start(bf16[5,32,608]{2,1,0:T(8,128)(2,1)} %get-tuple-element.26), channel_id=1, source_target_pairs={{0,12},{1,13},{2,14},{3,15},{4,8},{5,9},{6,10},{7,11},{8,4},{9,5},... | collective-permute-start | bytes 583688 | tf_op jit(solution)/shard_map/ppermute | solution.py:179
  64.0 2.5 %collective-permute-start.14 = (bf16[5,32,608]{2,1,0:T(8,128)(2,1)}, bf16[5,32,608]{2,1,0:T(8,128)(2,1)}, u32[]{:S(2)}, u32[]{:S(2)}) collective-permute-start(bf16[5,32,608]{2,1,0:T(8,128)(2,1)} %get-tuple-element.24), channel_id=1, source_target_pairs={{0,4},{1,5},{2,6},{3,7},{4,0},{5,1},{6,2},{7,3},{8,12},{9,13},{10,... | collective-permute-start | bytes 583688 | tf_op jit(solution)/shard_map/ppermute | solution.py:179
  66.5 1.8 %copy.14.k1 = bf16[5,128,608]{2,1,0:T(8,128)(2,1)S(1)} copy(bf16[5,128,608]{1,2,0:T(8,128)(2,1)} %collective-permute-done.7) | data formatting | bytes 1556480 | tf_op jit(solution)/shard_map/ppermute | solution.py:179
  69.2 4.7 %first.1 = (f32[512,608]{1,0:T(8,128)S(1)}, f32[512,256]{1,0:T(8,128)S(1)}, f32[1024,512]{1,0:T(8,128)}) custom-call(s32[2]{0:T(128)S(1)} %pad_add_fusion.place, bf16[528,128]{1,0:T(8,128)(2,1)S(1)} %get-tuple-element.16.own.s0, bf16[528,128]{1,0:T(8,128)(2,1)S(1)} %copy-done.11, bf16[5,128,608]{2,1,0:T(8,128)(2,1)S(1)} %pad_maximum_fusion.k0, ...), custom_call_target="tpu_custom_call" | custom-call | tf_op jit(solution)/shard_map/first/pallas_call | solution.py:253
  75.8 1.9 %copy.16.k2 = bf16[5,128,608]{2,1,0:T(8,128)(2,1)S(1)} copy(bf16[5,128,608]{1,2,0:T(8,128)(2,1)} %collective-permute-done.5) | data formatting | bytes 1556480 | tf_op jit(solution)/shard_map/ppermute | solution.py:179
  77.7 4.1 %collective-permute-done.15 = bf16[5,32,608]{2,1,0:T(8,128)(2,1)} collective-permute-done((bf16[5,32,608]{2,1,0:T(8,128)(2,1)}, bf16[5,32,608]{2,1,0:T(8,128)(2,1)}, u32[]{:S(2)}, u32[]{:S(2)}) %collective-permute-start.15) | collective-permute-done | bytes 194592 | tf_op jit(solution)/shard_map/ppermute | solution.py:179
  81.8 2.0 %add_bitcast_fusion = f32[32,5,608]{2,0,1:T(8,128)} fusion(bf16[5,32,608]{2,1,0:T(8,128)(2,1)} %collective-permute-done.16, bf16[5,32,608]{2,1,0:T(8,128)(2,1)} %collective-permute-done.15, f32[5,32,608]{2,1,0:T(8,128)S(1)} %copy-done.7, bf16[5,32,608]{2,1,0:T(8,128)(2,1)} %collective-permute-done.14), kind=kLoop, calls=%fused_computation.1 | loop fusion | flops 583680 | bytes 1361920 | tf_op jit(solution)/shard_map/transpose | solution.py:245
  83.8 1.8 %copy.17.k3 = bf16[5,128,608]{2,1,0:T(8,128)(2,1)S(1)} copy(bf16[5,128,608]{1,2,0:T(8,128)(2,1)} %collective-permute-done.6) | data formatting | bytes 1556480 | tf_op jit(solution)/shard_map/ppermute | solution.py:179
  85.7 1.3 %copy-done.3 = f32[512,608]{1,0:T(8,128)S(1)} copy-done((f32[512,608]{1,0:T(8,128)S(1)}, f32[512,608]{1,0:T(8,128)}, u32[]{:S(2)}) %copy-start.3) | copy-done | bytes 1245208
  87.0 6.5 %second.1 = (bf16[608,512]{1,0:T(8,128)(2,1)}, bf16[1024,512]{1,0:T(8,128)(2,1)}) custom-call(s32[2]{0:T(128)S(1)} %pad_add_fusion.place, bf16[528,256]{1,0:T(8,128)(2,1)S(1)} %copy-done.9, bf16[5,128,608]{2,1,0:T(8,128)(2,1)S(1)} %copy.16.k2, bf16[5,128,608]{2,1,0:T(8,128)(2,1)S(1)} %copy.17.k3, bf16[512,608]{1,0:T(8,128)(2,1)S(1)} %copy.10.cot, ...), custom_call_target="tpu_custom_call" | custom-call | tf_op jit(solution)/shard_map/second/pallas_call | solution.py:266
  (60 shorter events, 9.5 us)
Async XLA Ops:
  0.6 11.4 %collective-permute-start.4 = (bf16[5,32,608]{2,1,0:T(8,128)(2,1)}, bf16[5,32,608]{2,1,0:T(8,128)(2,1)S(1)}, u32[]{:S(2)}, u32[]{:S(2)}) collective-permute-start(bf16[5,32,608]{2,1,0:T(8,128)(2,1)} %bitcast.10), channel_id=1, source_target_pairs={{0,12},{1,13},{2,14},{3,15},{4,8},{5,9},{6,10},{7,11},{8,4},{9,5},... | collective-permute-start | bytes 583688 | tf_op jit(solution)/shard_map/ppermute | solution.py:179
  5.7 17.6 %collective-permute-start.3 = (bf16[5,32,608]{2,1,0:T(8,128)(2,1)}, bf16[5,32,608]{2,1,0:T(8,128)(2,1)S(1)}, u32[]{:S(2)}, u32[]{:S(2)}) collective-permute-start(bf16[5,32,608]{2,1,0:T(8,128)(2,1)} %bitcast.11), channel_id=1, source_target_pairs={{0,8},{1,9},{2,10},{3,11},{4,12},{5,13},{6,14},{7,15},{8,0},{9,1},... | collective-permute-start | bytes 583688 | tf_op jit(solution)/shard_map/ppermute | solution.py:179
  5.7 17.6 %collective-permute-start.2 = (bf16[5,32,608]{2,1,0:T(8,128)(2,1)}, bf16[5,32,608]{2,1,0:T(8,128)(2,1)S(1)}, u32[]{:S(2)}, u32[]{:S(2)}) collective-permute-start(bf16[5,32,608]{2,1,0:T(8,128)(2,1)} %bitcast.12), channel_id=1, source_target_pairs={{0,4},{1,5},{2,6},{3,7},{4,0},{5,1},{6,2},{7,3},{8,12},{9,13},{10,... | collective-permute-start | bytes 583688 | tf_op jit(solution)/shard_map/ppermute | solution.py:179
  6.4 40.8 %collective-permute-start.12 = (bf16[608,512]{1,0:T(8,128)(2,1)}, bf16[608,512]{1,0:T(8,128)(2,1)}, u32[]{:S(2)}, u32[]{:S(2)}) collective-permute-start(bf16[608,512]{1,0:T(8,128)(2,1)} %bitcast.7), channel_id=1, source_target_pairs={{0,2},{1,3},{2,0},{3,1},{4,6},{5,7},{6,4},{7,5},{8,10},{9,11},{10,... | collective-permute-start | bytes 1867784 | tf_op jit(solution)/shard_map/ppermute | solution.py:179
  10.2 22.4 %copy-start = (bf16[1024,512]{1,0:T(8,128)(2,1)S(1)}, bf16[1024,512]{1,0:T(8,128)(2,1)}, u32[]{:S(2)}) copy-start(bf16[1024,512]{1,0:T(8,128)(2,1)} %act.3) | copy-start | bytes 3145732
  24.4 22.9 %copy-start.1 = (bf16[512,608]{0,1:T(8,128)(2,1)S(1)}, bf16[512,608]{0,1:T(8,128)(2,1)}, u32[]{:S(2)}) copy-start(bf16[512,608]{0,1:T(8,128)(2,1)} %param.5) | copy-start | bytes 1867780
  25.9 28.5 %collective-permute-start.5 = (bf16[5,128,608]{1,2,0:T(8,128)(2,1)}, bf16[5,128,608]{1,2,0:T(8,128)(2,1)}, u32[]{:S(2)}, u32[]{:S(2)}) collective-permute-start(bf16[5,128,608]{1,2,0:T(8,128)(2,1)} %copy.12), channel_id=1, source_target_pairs={{0,2},{1,3},{2,0},{3,1},{4,6},{5,7},{6,4},{7,5},{8,10},{9,11},{10,... | collective-permute-start | bytes 2334728 | tf_op jit(solution)/shard_map/ppermute | solution.py:179
  27.4 2.7 %collective-permute-start = (bf16[16,1120]{1,0:T(8,128)(2,1)S(1)}, bf16[16,1120]{1,0:T(8,128)(2,1)S(1)}, u32[]{:S(2)}, u32[]{:S(2)}) collective-permute-start(bf16[16,1120]{1,0:T(8,128)(2,1)S(1)} %pad_maximum_fusion.1), channel_id=1, source_target_pairs={{0,1},{1,2},{2,3},{3,4},{4,5},{5,6},{6,7},{7,8},{8,9},{9,10},{10,1... | collective-permute-start | bytes 107528 | tf_op jit(solution)/shard_map/ppermute | solution.py:199
  28.7 3.8 %collective-permute-start.1 = (bf16[16,1120]{1,0:T(8,128)(2,1)S(1)}, bf16[16,1120]{1,0:T(8,128)(2,1)S(1)}, u32[]{:S(2)}, u32[]{:S(2)}) collective-permute-start(bf16[16,1120]{1,0:T(8,128)(2,1)S(1)} %pad_maximum_fusion.2), channel_id=1, source_target_pairs={{1,0},{2,1},{3,2},{4,3},{5,4},{6,5},{7,6},{8,7},{9,8},{10,9},{11,1... | collective-permute-start | bytes 107528 | tf_op jit(solution)/shard_map/ppermute | solution.py:200
  32.6 23.3 %copy-start.12 = (bf16[16,1120]{1,0:T(8,128)(2,1)}, bf16[16,1120]{1,0:T(8,128)(2,1)S(1)}, u32[]{:S(2)}) copy-start(bf16[16,1120]{1,0:T(8,128)(2,1)S(1)} %collective-permute-done.1) | copy-start | bytes 107524
  34.4 22.7 %copy-start.8 = (bf16[528,256]{1,0:T(8,128)(2,1)}, bf16[528,256]{1,0:T(8,128)(2,1)S(1)}, u32[]{:S(2)}) copy-start(bf16[528,256]{1,0:T(8,128)(2,1)S(1)} %get-tuple-element.15.far) | copy-start | bytes 811012
  34.4 22.7 %copy-start.10 = (bf16[528,128]{1,0:T(8,128)(2,1)}, bf16[528,128]{1,0:T(8,128)(2,1)S(1)}, u32[]{:S(2)}) copy-start(bf16[528,128]{1,0:T(8,128)(2,1)S(1)} %get-tuple-element.17.near) | copy-start | bytes 405508
  34.4 19.8 %collective-permute-start.9 = (bf16[528,256]{1,0:T(8,128)(2,1)S(1)}, bf16[528,256]{1,0:T(8,128)(2,1)S(1)}, u32[]{:S(2)}, u32[]{:S(2)}) collective-permute-start(bf16[528,256]{1,0:T(8,128)(2,1)S(1)} %get-tuple-element.15.far), channel_id=1, source_target_pairs={{0,2},{1,3},{2,0},{3,1},{4,6},{5,7},{6,4},{7,5},{8,10},{9,11},{10,... | collective-permute-start | bytes 811016 | tf_op jit(solution)/shard_map/ppermute | solution.py:179
  47.2 9.9 %collective-permute-start.11 = (bf16[608,512]{1,0:T(8,128)(2,1)S(1)}, bf16[608,512]{1,0:T(8,128)(2,1)S(1)}, u32[]{:S(2)}, u32[]{:S(2)}) collective-permute-start(bf16[608,512]{1,0:T(8,128)(2,1)S(1)} %bitcast.8), channel_id=1, source_target_pairs={{0,1},{1,0},{2,3},{3,2},{4,5},{5,4},{6,7},{7,6},{8,9},{9,8},{10,11... | collective-permute-start | bytes 1867784 | tf_op jit(solution)/shard_map/ppermute | solution.py:179
  47.2 9.9 %collective-permute-start.13 = (bf16[608,512]{1,0:T(8,128)(2,1)}, bf16[608,512]{1,0:T(8,128)(2,1)S(1)}, u32[]{:S(2)}, u32[]{:S(2)}) collective-permute-start(bf16[608,512]{1,0:T(8,128)(2,1)} %collective-permute-done.12.c2), channel_id=1, source_target_pairs={{0,1},{1,0},{2,3},{3,2},{4,5},{5,4},{6,7},{7,6},{8,9},{9,8},{10,11... | collective-permute-start | bytes 1867784 | tf_op jit(solution)/shard_map/ppermute | solution.py:179
  47.7 18.7 %collective-permute-start.7 = (bf16[5,128,608]{1,2,0:T(8,128)(2,1)}, bf16[5,128,608]{1,2,0:T(8,128)(2,1)}, u32[]{:S(2)}, u32[]{:S(2)}) collective-permute-start(bf16[5,128,608]{1,2,0:T(8,128)(2,1)} %copy.12), channel_id=1, source_target_pairs={{0,1},{1,0},{2,3},{3,2},{4,5},{5,4},{6,7},{7,6},{8,9},{9,8},{10,11... | collective-permute-start | bytes 2334728 | tf_op jit(solution)/shard_map/ppermute | solution.py:179
  54.2 1.5 %collective-permute-start.10 = (bf16[528,256]{1,0:T(8,128)(2,1)S(1)}, bf16[528,256]{1,0:T(8,128)(2,1)S(1)}, u32[]{:S(2)}, u32[]{:S(2)}) collective-permute-start(bf16[528,256]{1,0:T(8,128)(2,1)S(1)} %collective-permute-done.9), channel_id=1, source_target_pairs={{0,1},{1,0},{2,3},{3,2},{4,5},{5,4},{6,7},{7,6},{8,9},{9,8},{10,11... | collective-permute-start | bytes 811016 | tf_op jit(solution)/shard_map/ppermute | solution.py:179
  54.4 29.4 %collective-permute-start.6 = (bf16[5,128,608]{1,2,0:T(8,128)(2,1)}, bf16[5,128,608]{1,2,0:T(8,128)(2,1)}, u32[]{:S(2)}, u32[]{:S(2)}) collective-permute-start(bf16[5,128,608]{1,2,0:T(8,128)(2,1)} %collective-permute-done.5), channel_id=1, source_target_pairs={{0,1},{1,0},{2,3},{3,2},{4,5},{5,4},{6,7},{7,6},{8,9},{9,8},{10,11... | collective-permute-start | bytes 2334728 | tf_op jit(solution)/shard_map/ppermute | solution.py:179
  55.8 1.4 %collective-permute-start.8 = (bf16[528,128]{1,0:T(8,128)(2,1)S(1)}, bf16[528,128]{1,0:T(8,128)(2,1)S(1)}, u32[]{:S(2)}, u32[]{:S(2)}) collective-permute-start(bf16[528,128]{1,0:T(8,128)(2,1)S(1)} %get-tuple-element.17.near), channel_id=1, source_target_pairs={{0,1},{1,0},{2,3},{3,2},{4,5},{5,4},{6,7},{7,6},{8,9},{9,8},{10,11... | collective-permute-start | bytes 405512 | tf_op jit(solution)/shard_map/ppermute | solution.py:179
  55.9 10.5 %copy-start.13 = (bf16[16,1120]{1,0:T(8,128)(2,1)S(1)}, bf16[16,1120]{1,0:T(8,128)(2,1)}, u32[]{:S(2)}) copy-start(bf16[16,1120]{1,0:T(8,128)(2,1)} %copy-done.12) | copy-start | bytes 107524
  62.0 15.6 %collective-permute-start.16 = (bf16[5,32,608]{2,1,0:T(8,128)(2,1)}, bf16[5,32,608]{2,1,0:T(8,128)(2,1)}, u32[]{:S(2)}, u32[]{:S(2)}) collective-permute-start(bf16[5,32,608]{2,1,0:T(8,128)(2,1)} %get-tuple-element.26), channel_id=1, source_target_pairs={{0,12},{1,13},{2,14},{3,15},{4,8},{5,9},{6,10},{7,11},{8,4},{9,5},... | collective-permute-start | bytes 583688 | tf_op jit(solution)/shard_map/ppermute | solution.py:179
  64.0 17.9 %collective-permute-start.15 = (bf16[5,32,608]{2,1,0:T(8,128)(2,1)}, bf16[5,32,608]{2,1,0:T(8,128)(2,1)}, u32[]{:S(2)}, u32[]{:S(2)}) collective-permute-start(bf16[5,32,608]{2,1,0:T(8,128)(2,1)} %get-tuple-element.25), channel_id=1, source_target_pairs={{0,8},{1,9},{2,10},{3,11},{4,12},{5,13},{6,14},{7,15},{8,0},{9,1},... | collective-permute-start | bytes 583688 | tf_op jit(solution)/shard_map/ppermute | solution.py:179
  64.0 17.9 %collective-permute-start.14 = (bf16[5,32,608]{2,1,0:T(8,128)(2,1)}, bf16[5,32,608]{2,1,0:T(8,128)(2,1)}, u32[]{:S(2)}, u32[]{:S(2)}) collective-permute-start(bf16[5,32,608]{2,1,0:T(8,128)(2,1)} %get-tuple-element.24), channel_id=1, source_target_pairs={{0,4},{1,5},{2,6},{3,7},{4,0},{5,1},{6,2},{7,3},{8,12},{9,13},{10,... | collective-permute-start | bytes 583688 | tf_op jit(solution)/shard_map/ppermute | solution.py:179
  77.7 8.0 %copy-start.5 = (f32[512,256]{1,0:T(8,128)S(1)}, f32[512,256]{1,0:T(8,128)}, u32[]{:S(2)}) copy-start(f32[512,256]{1,0:T(8,128)} %copy-done.4) | copy-start | bytes 1572868
  (7 other events, 18.8 us)

commit v2 on v1

--- a/solution.py
+++ b/solution.py
@@ -40,13 +40,19 @@
     quarter = channels // TEAM
     mate = lax.div(col, quarter)
     within = lax.rem(col, quarter)
-    level = lax.div(within, rows)
+    slot = lax.div(within, rows)
     row = lax.rem(within, rows)
+    level = jnp.zeros_like(slot)
+    bit = quarter // rows // 2
+    while bit:
+        level = level * 2 + lax.rem(slot, 2)
+        slot = lax.div(slot, 2)
+        bit //= 2
     want = rows * (TEAM * (level ^ place[0]) + (mate ^ place[1])) + row
     return jnp.where(chan == want, 1.0, 0.0).astype(BF16)
 
 
-def pool_kernel(rows, place, act, low, high, own, near, far):
+def pool_kernel(rows, place, act, low, high, *mates):
     channels = act.shape[1]
     quarter = channels // TEAM
     order = relative_order(place, rows, channels, False)
@@ -61,9 +67,8 @@
 
     def put(at, s):
         n = s.shape[0]
-        own[at : at + n, :] = s[:, :quarter]
-        near[at : at + n, :] = s[:, quarter : 2 * quarter]
-        far[at : at + n, :] = s[:, 2 * quarter :]
+        for r, mate in enumerate(mates):
+            mate[at : at + n, :] = s[:, r * quarter : (r + 1) * quarter]
 
     def gelu(v):
         return gelu_value(v.astype(F32)).astype(BF16)
@@ -98,8 +103,9 @@
     else:
         for k in range(TAPS):
             for m, out in enumerate(outs):
-                at = k * quarter + m * rows
-                out[k] = total[at : at + rows].astype(out.dtype)
+                size = out.shape[1]
+                at = k * quarter + m * size
+                out[k] = total[at : at + size].astype(out.dtype)
 
 
 def fill_ext(ext, cot, low, high):
@@ -128,12 +134,12 @@
     return acc, grad
 
 
-def first_kernel(rows, place, own, near, k0, k1, cot, low, high, act, acc, grad, slope, ext):
+def first_kernel(rows, place, s0, s1, k0, k1, cot, low, high, act, acc, grad, slope, ext):
     positions = cot.shape[0]
     fill_ext(ext, cot, low, high)
     acc[...], grad[...] = pair_products(
-        lambda at: jnp.concatenate([own[at : at + positions], near[at : at + positions]], axis=1),
-        lambda k: jnp.concatenate([k0[k], k1[k]], axis=0),
+        lambda at: jnp.concatenate([s0[at : at + positions], s1[at : at + positions]], axis=1),
+        lambda k: jnp.concatenate([k0[k], k1[k]], axis=0)[:, : cot.shape[1]],
         ext,
         positions,
     )
@@ -145,15 +151,15 @@
 
 
 def second_kernel(
-    rows, place, far, k2, k3, cot, low, high, acc1, grad1, slope, pooled, out, ext, doubled
+    rows, place, s2, s3, k2, k3, cot, low, high, acc1, grad1, slope, pooled, out, ext, doubled
 ):
     positions = cot.shape[0]
     channels = out.shape[1]
     half = channels // 2
     fill_ext(ext, cot, low, high)
     acc, grad = pair_products(
-        lambda at: far[at : at + positions, :],
-        lambda k: jnp.concatenate([k2[k], k3[k]], axis=0),
+        lambda at: jnp.concatenate([s2[at : at + positions], s3[at : at + positions]], axis=1),
+        lambda k: jnp.concatenate([k2[k], k3[k]], axis=0)[:, : cot.shape[1]],
         ext,
         positions,
     )
@@ -174,6 +180,10 @@
         out[at : at + block, :] = jnp.dot(mixed, back, preferred_element_type=F32).astype(BF16)
 
 
+def after(x, *first):
+    return lax.optimization_barrier((x, first))[0]
+
+
 def flip(x, bit):
     n = lax.axis_size("pos")
     return lax.ppermute(x, "pos", [(i, i ^ bit) for i in range(n)])
@@ -193,7 +203,8 @@
     shard = kernel.transpose(1, 0, 2)
 
     cot_y = flip(cot_t, 2)
-    shards = [shard] + [flip(shard, TEAM * m) for m in range(1, levels)]
+    head = levels // 2
+    first_block = flip(shard, TEAM * head) if head else None
     edge_low = jnp.concatenate([activations[-HALO:], cotangent[-HALO:]], axis=1)
     edge_high = jnp.concatenate([activations[:HALO], cotangent[:HALO]], axis=1)
     low = lax.ppermute(edge_low, "pos", [(i, i + 1) for i in range(n - 1)])
@@ -201,29 +212,33 @@
     cot_c = flip(cot_t, 1)
 
     ext_rows = positions + 2 * EXT
-    own, near, far = pl.pallas_call(
+    pieces = pl.pallas_call(
         functools.partial(pool_kernel, rows),
-        out_shape=[
-            jax.ShapeDtypeStruct((ext_rows, quarter), BF16),
-            jax.ShapeDtypeStruct((ext_rows, quarter), BF16),
-            jax.ShapeDtypeStruct((ext_rows, 2 * quarter), BF16),
-        ],
+        out_shape=[jax.ShapeDtypeStruct((ext_rows, quarter), BF16)] * TEAM,
         in_specs=[SMEM, VMEM, VMEM, VMEM],
-        out_specs=[VMEM] * 3,
+        out_specs=[VMEM] * TEAM,
+        cost_estimate=pl.CostEstimate(flops=1, bytes_accessed=1, transcendentals=0),
         compiler_params=params(32),
         name="pool",
     )(place, activations, low[:, :channels], high[:, :channels])
 
-    far_y = flip(far, 2)
-    near_c = flip(near, 1)
+    order = [0]
+    k0 = shard
+    while len(order) < levels:
+        bit = levels // 2 // len(order)
+        got = after(first_block, pieces) if bit == head else flip(k0, TEAM * bit)
+        k0 = jnp.concatenate([k0, got], axis=1)
+        order += [m ^ bit for m in order]
+    far = after(pieces[2:], cot_y)
+    mates = [pieces[0], flip(pieces[1], 1), flip(far[0], 2), flip(far[1], 3)]
+    cot_y = after(cot_y, mates[1])
     cot_yc = flip(cot_y, 1)
-    far_yc = flip(far_y, 1)
-
+
+    halves = max(levels // 2, 1)
     split = rows % 16 == 0
     if split:
         grad_shape = [
-            jax.ShapeDtypeStruct((TAPS, rows, width), F32 if m == 0 else BF16)
-            for m in range(levels)
+            jax.ShapeDtypeStruct((TAPS, halves * rows, width), dtype) for dtype in (F32, BF16)
         ]
     else:
         grad_shape = [jax.ShapeDtypeStruct((TAPS, quarter, width), F32)]
@@ -233,21 +248,31 @@
         in_specs=[VMEM] * 8,
         out_specs=[VMEM] * len(grad_shape),
         scratch_shapes=[pltpu.VMEM((TAPS * quarter, positions), BF16)],
+        cost_estimate=pl.CostEstimate(flops=1, bytes_accessed=1, transcendentals=0),
         compiler_params=params(48),
         name="wgrad",
-    )(own, near_c, far_y[:, :quarter], far_yc[:, quarter:], cot_t, cot_c, cot_y, cot_yc)
-    if not split:
-        parts = [grads[0][:, m * rows : (m + 1) * rows] for m in range(levels)]
-        grads = [parts[0]] + [p.astype(BF16) for p in parts[1:]]
-    total = grads[0]
-    for m in range(1, levels):
-        total = total + flip(grads[m], TEAM * m).astype(F32)
-    kernel_grad = total.transpose(1, 0, 2)
-
-    k0 = jnp.concatenate(shards, axis=1)
+    )(*mates, cot_t, cot_c, cot_y, cot_yc)
+    keep = grads[0] if split else grads[0][:, : halves * rows]
+    give = grads[1] if split else grads[0][:, halves * rows :].astype(BF16)
+    bits = []
+    bit = 1
+    while bit < levels:
+        bits.append(bit)
+        bit *= 2
+    last = None
+    for i, bit in enumerate(bits):
+        got = flip(give, TEAM * bit)
+        if i + 1 == len(bits):
+            last = (keep, got)
+            break
+        keep = keep + got.astype(F32)
+        half = keep.shape[1] // 2
+        keep, give = keep[:, :half], keep[:, half:].astype(BF16)
+
+    k0 = after(k0, mates)
+    k0 = jnp.pad(k0, ((0, 0), (0, 0), (0, -width % 128)))
     k2 = flip(k0, 2)
     k1 = flip(k0, 1)
-    k3 = flip(k2, 1)
 
     low_cot, high_cot = low[:, channels:], high[:, channels:]
     acc, grad, slope = pl.pallas_call(
@@ -260,25 +285,32 @@
         in_specs=[SMEM] + [VMEM] * 8,
         out_specs=[VMEM] * 3,
         scratch_shapes=[pltpu.VMEM((positions + 2 * HALO, width), BF16)],
+        cost_estimate=pl.CostEstimate(flops=1, bytes_accessed=1, transcendentals=0),
         compiler_params=params(48),
         name="first",
-    )(place, own, near, k0, k1, cotangent, low_cot, high_cot, activations)
+    )(place, pieces[0], pieces[1], k0, k1, cotangent, low_cot, high_cot, activations)
+    k2 = after(k2, acc, keep)
+    k3 = flip(k2, 1)
     pooled_t, input_grad = pl.pallas_call(
         functools.partial(second_kernel, rows),
         out_shape=[
             jax.ShapeDtypeStruct((width, positions), BF16),
             jax.ShapeDtypeStruct((window, channels), BF16),
         ],
-        in_specs=[SMEM] + [VMEM] * 9,
+        in_specs=[SMEM] + [VMEM] * 10,
         out_specs=[VMEM] * 2,
         scratch_shapes=[
             pltpu.VMEM((positions + 2 * HALO, width), BF16),
             pltpu.VMEM((channels // 128, window, 128), F32),
         ],
+        cost_estimate=pl.CostEstimate(flops=1, bytes_accessed=1, transcendentals=0),
         compiler_params=params(48),
         name="second",
-    )(place, far, k2, k3, cotangent, low_cot, high_cot, acc, grad, slope)
-    return pooled_t.T, input_grad, kernel_grad
+    )(place, pieces[2], pieces[3], k2, k3, cotangent, low_cot, high_cot, acc, grad, slope)
+    if last is not None:
+        keep, got = last[0], after(last[1], pooled_t)
+        keep = keep + got.astype(F32)
+    return pooled_t.T, input_grad, keep.transpose(1, 0, 2)
 
 
 def solution(mesh):

time: 94 us -> 67 us (0.71)
  local copies, waits for them, and re-layouts: 14.1 us -> 2.29 us
  starting transfers between devices: 30 us -> 22.1 us
  waiting for transfers between devices: 28.3 us -> 24.9 us
  other arithmetic: 3.06 us -> 1.1 us
  Pallas kernels: 17.2 us -> 15.4 us
    ppermute x15 -> x13, starting transfers between devices: 27.4 us -> 19.5 us  [flip(): return lax.ppermute(x, 'pos', [(i, i ^ bit) for i in range(n)])]
    ppermute x3 -> x0, local copies, waits for them, and re-layouts: 5.51 us -> none  [flip(): return lax.ppermute(x, 'pos', [(i, i ^ bit) for i in range(n)])]
    unnamed x29 -> x7, local copies, waits for them, and re-layouts: 6.25 us -> 1.43 us
    ppermute x15 -> x13, waiting for transfers between devices: 25.8 us -> 22.5 us  [flip(): return lax.ppermute(x, 'pos', [(i, i ^ bit) for i in range(n)])]
    pallas_call x1, Pallas kernels: 4.17 us -> 2.26 us  [on_device(): pl.pallas_call(functools.partial(wgrad_kernel, rows), out_shape=grad_shap...]
    concatenate x1 -> x0, local copies, waits for them, and re-layouts: 1.53 us -> none  [on_device(): k0 = jnp.concatenate(shards, axis=1)]
    transpose x1, other arithmetic: 1.96 us -> 0.79 us  [on_device(): return (pooled_t.T, input_grad, keep.transpose(1, 0, 2))]
  transfers between devices with their start and end apart: 17 -> 15, of which waited for: 7 -> 9; matrix products, arithmetic and copies ran while one was open for 11% -> 4% of each run, Pallas kernels for 11% -> 23%
where the time goes in v2:
time: 67 us; the launch traced here: 66.6 us
  waiting for transfers between devices  24.9 us (37%)
  starting transfers between devices  22.1 us (33%)
  Pallas kernels  15.4 us (23%)
  local copies, waits for them, and re-layouts  2.29 us (3%)
  other arithmetic  1.1 us (2%)
  between operations  0.77 us (1%)
    ppermute x13, waiting for transfers between devices, flip(): return lax.ppermute(x, 'pos', [(i, i ^ bit) for i in range(n)])  22.5 us
    ppermute x13, starting transfers between devices, flip(): return lax.ppermute(x, 'pos', [(i, i ^ bit) for i in range(n)])  19.5 us
    pallas_call x1, Pallas kernels, on_device(): pl.pallas_call(functools.partial(second_kernel, rows), out_shape=[jax.Sha...  6.55 us
    pallas_call x1, Pallas kernels, on_device(): pl.pallas_call(functools.partial(first_kernel, rows), out_shape=[jax.Shap...  4.75 us
    ppermute x1, waiting for transfers between devices, on_device(): high = lax.ppermute(edge_high, 'pos', [(i + 1, i) for i in range(n - 1)])  2.45 us
    pallas_call x1, Pallas kernels, on_device(): pl.pallas_call(functools.partial(wgrad_kernel, rows), out_shape=grad_shap...  2.26 us
    pallas_call x1, Pallas kernels, on_device(): pl.pallas_call(functools.partial(pool_kernel, rows), out_shape=[jax.Shape...  1.81 us
    unnamed x7, local copies, waits for them, and re-layouts  1.43 us
  transfers between devices with their start and end apart: 15, of which 9 were waited for; matrix products, arithmetic and copies ran while one was open for 4% of the time, Pallas kernels for 23%

profile of v2, /device:TPU:0, one launch (start us, length us, event | category | flops | bytes accessed | tf_op | source)
XLA Modules:
  0.0 66.6 jit_solution(15163228753612499344)
XLA Ops:
  0.7 4.1 %collective-permute-start.2 = (bf16[5,32,608]{2,1,0:T(8,128)(2,1)}, bf16[5,32,608]{2,1,0:T(8,128)(2,1)S(1)}, u32[]{:S(2)}, u32[]{:S(2)}) collective-permute-start(bf16[5,32,608]{2,1,0:T(8,128)(2,1)} %bitcast.10), channel_id=1, source_target_pairs={{0,8},{1,9},{2,10},{3,11},{4,12},{5,13},{6,14},{7,15},{8,0},{9,1},... | collective-permute-start | bytes 583688 | tf_op jit(solution)/shard_map/ppermute | solution.py:189
  4.8 1.5 %collective-permute-start.5 = (bf16[608,512]{1,0:T(8,128)(2,1)}, bf16[608,512]{1,0:T(8,128)(2,1)S(1)}, u32[]{:S(2)}, u32[]{:S(2)}) collective-permute-start(bf16[608,512]{1,0:T(8,128)(2,1)} %bitcast.7), channel_id=1, source_target_pairs={{0,2},{1,3},{2,0},{3,1},{4,6},{5,7},{6,4},{7,5},{8,10},{9,11},{10,... | collective-permute-start | bytes 1867784 | tf_op jit(solution)/shard_map/ppermute | solution.py:189
  6.3 1.4 %copy.6.cot = bf16[512,608]{1,0:T(8,128)(2,1)S(1)} copy(bf16[512,608]{0,1:T(8,128)(2,1)} %param.5) | data formatting | bytes 1245184 | tf_op args[2]
  8.4 1.3 %collective-permute-start = (bf16[16,1120]{1,0:T(8,128)(2,1)S(1)}, bf16[16,1120]{1,0:T(8,128)(2,1)S(1)}, u32[]{:S(2)}, u32[]{:S(2)}) collective-permute-start(bf16[16,1120]{1,0:T(8,128)(2,1)S(1)} %pad_maximum_fusion.2), channel_id=1, source_target_pairs={{0,1},{1,2},{2,3},{3,4},{4,5},{5,6},{6,7},{7,8},{8,9},{9,10},{10,1... | collective-permute-start | bytes 107528 | tf_op jit(solution)/shard_map/ppermute | solution.py:210
  9.7 1.3 %collective-permute-start.1 = (bf16[16,1120]{1,0:T(8,128)(2,1)S(1)}, bf16[16,1120]{1,0:T(8,128)(2,1)S(1)}, u32[]{:S(2)}, u32[]{:S(2)}) collective-permute-start(bf16[16,1120]{1,0:T(8,128)(2,1)S(1)} %pad_maximum_fusion.3), channel_id=1, source_target_pairs={{1,0},{2,1},{3,2},{4,3},{5,4},{6,5},{7,6},{8,7},{9,8},{10,9},{11,1... | collective-permute-start | bytes 107528 | tf_op jit(solution)/shard_map/ppermute | solution.py:211
  11.1 2.4 %collective-permute-done.1 = bf16[16,1120]{1,0:T(8,128)(2,1)S(1)} collective-permute-done((bf16[16,1120]{1,0:T(8,128)(2,1)S(1)}, bf16[16,1120]{1,0:T(8,128)(2,1)S(1)}, u32[]{:S(2)}, u32[]{:S(2)}) %collective-permute-start.1) | collective-permute-done | bytes 35872 | tf_op jit(solution)/shard_map/ppermute | solution.py:211
  13.6 1.8 %pool.1 = (bf16[528,128]{1,0:T(8,128)(2,1)S(1)}, bf16[528,128]{1,0:T(8,128)(2,1)S(1)}, bf16[528,128]{1,0:T(8,128)(2,1)S(1)}, bf16[528,128]{1,0:T(8,128)(2,1)S(1)}) custom-call(s32[2]{0:T(128)S(1)} %pad_add_fusion.place, bf16[1024,512]{1,0:T(8,128)(2,1)S(1)} %copy-done, bf16[16,512]{1,0:T(8,128)(2,1)S(1)} %slice.42.low, bf16[16,512]{1,0:T(8,128)(2,1)S(1)} %slice.44.high), custom_call_target="tpu_custom_call" | custom-call | flops 1 | bytes 1 | tf_op jit(solution)/shard_map/pool/pallas_call | solution.py:215
  15.5 4.6 %collective-permute-start.3 = (bf16[5,64,608]{2,1,0:T(8,128)(2,1)S(1)}, bf16[5,64,608]{2,1,0:T(8,128)(2,1)S(1)}, u32[]{:S(2)}, u32[]{:S(2)}) collective-permute-start(bf16[5,64,608]{2,1,0:T(8,128)(2,1)S(1)} %pad_maximum_fusion.1), channel_id=1, source_target_pairs={{0,4},{1,5},{2,6},{3,7},{4,0},{5,1},{6,2},{7,3},{8,12},{9,13},{10,... | collective-permute-start | bytes 1167368 | tf_op jit(solution)/shard_map/ppermute | solution.py:189
  20.1 4.2 %collective-permute-start.4 = (bf16[528,128]{1,0:T(8,128)(2,1)S(1)}, bf16[528,128]{1,0:T(8,128)(2,1)S(1)}, u32[]{:S(2)}, u32[]{:S(2)}) collective-permute-start(bf16[528,128]{1,0:T(8,128)(2,1)S(1)} %get-tuple-element.24.s1), channel_id=1, source_target_pairs={{0,1},{1,0},{2,3},{3,2},{4,5},{5,4},{6,7},{7,6},{8,9},{9,8},{10,11... | collective-permute-start | bytes 405512 | tf_op jit(solution)/shard_map/ppermute | solution.py:189
  24.3 0.9 %collective-permute-start.6 = (bf16[528,128]{1,0:T(8,128)(2,1)S(1)}, bf16[528,128]{1,0:T(8,128)(2,1)S(1)}, u32[]{:S(2)}, u32[]{:S(2)}) collective-permute-start(bf16[528,128]{1,0:T(8,128)(2,1)S(1)} %get-tuple-element.26.s2), channel_id=1, source_target_pairs={{0,2},{1,3},{2,0},{3,1},{4,6},{5,7},{6,4},{7,5},{8,10},{9,11},{10,... | collective-permute-start | bytes 405512 | tf_op jit(solution)/shard_map/ppermute | solution.py:189
  25.7 0.8 %collective-permute-done.3 = bf16[5,64,608]{2,1,0:T(8,128)(2,1)S(1)} collective-permute-done((bf16[5,64,608]{2,1,0:T(8,128)(2,1)S(1)}, bf16[5,64,608]{2,1,0:T(8,128)(2,1)S(1)}, u32[]{:S(2)}, u32[]{:S(2)}) %collective-permute-start.3) | collective-permute-done | bytes 389152 | tf_op jit(solution)/shard_map/ppermute | solution.py:189
  26.6 4.2 %collective-permute-done.6.s2 = bf16[528,128]{1,0:T(8,128)(2,1)S(1)} collective-permute-done((bf16[528,128]{1,0:T(8,128)(2,1)S(1)}, bf16[528,128]{1,0:T(8,128)(2,1)S(1)}, u32[]{:S(2)}, u32[]{:S(2)}) %collective-permute-start.6) | collective-permute-done | bytes 135200 | tf_op jit(solution)/shard_map/ppermute | solution.py:189
  30.8 1.0 %collective-permute-done.7.s3 = bf16[528,128]{1,0:T(8,128)(2,1)S(1)} collective-permute-done((bf16[528,128]{1,0:T(8,128)(2,1)S(1)}, bf16[528,128]{1,0:T(8,128)(2,1)S(1)}, u32[]{:S(2)}, u32[]{:S(2)}) %collective-permute-start.7) | collective-permute-done | bytes 135200 | tf_op jit(solution)/shard_map/ppermute | solution.py:189
  31.8 0.9 %collective-permute-start.9 = (bf16[5,128,640]{2,1,0:T(8,128)(2,1)S(1)}, bf16[5,128,640]{2,1,0:T(8,128)(2,1)S(1)}, u32[]{:S(2)}, u32[]{:S(2)}) collective-permute-start(bf16[5,128,640]{2,1,0:T(8,128)(2,1)S(1)} %pad.4.k0), channel_id=1, source_target_pairs={{0,1},{1,0},{2,3},{3,2},{4,5},{5,4},{6,7},{7,6},{8,9},{9,8},{10,11... | collective-permute-start | bytes 2457608 | tf_op jit(solution)/shard_map/ppermute | solution.py:189
  32.7 1.4 %collective-permute-start.8 = (bf16[5,128,640]{2,1,0:T(8,128)(2,1)S(1)}, bf16[5,128,640]{2,1,0:T(8,128)(2,1)S(1)}, u32[]{:S(2)}, u32[]{:S(2)}) collective-permute-start(bf16[5,128,640]{2,1,0:T(8,128)(2,1)S(1)} %pad.4.k0), channel_id=1, source_target_pairs={{0,2},{1,3},{2,0},{3,1},{4,6},{5,7},{6,4},{7,5},{8,10},{9,11},{10,... | collective-permute-start | bytes 2457608 | tf_op jit(solution)/shard_map/ppermute | solution.py:189
  34.6 1.5 %collective-permute-done.10.c1 = bf16[608,512]{1,0:T(8,128)(2,1)S(1)} collective-permute-done((bf16[608,512]{1,0:T(8,128)(2,1)S(1)}, bf16[608,512]{1,0:T(8,128)(2,1)S(1)}, u32[]{:S(2)}, u32[]{:S(2)}) %collective-permute-start.10) | collective-permute-done | bytes 622624 | tf_op jit(solution)/shard_map/ppermute | solution.py:189
  36.2 0.9 %collective-permute-done.11.c3 = bf16[608,512]{1,0:T(8,128)(2,1)S(1)} collective-permute-done((bf16[608,512]{1,0:T(8,128)(2,1)S(1)}, bf16[608,512]{1,0:T(8,128)(2,1)S(1)}, u32[]{:S(2)}, u32[]{:S(2)}) %collective-permute-start.11) | collective-permute-done | bytes 622624 | tf_op jit(solution)/shard_map/ppermute | solution.py:189
  37.1 2.3 %wgrad.1 = (f32[5,64,608]{2,1,0:T(8,128)S(1)}, bf16[5,64,608]{2,1,0:T(8,128)(2,1)S(1)}) custom-call(bf16[528,128]{1,0:T(8,128)(2,1)S(1)} %get-tuple-element.23.s0, bf16[528,128]{1,0:T(8,128)(2,1)S(1)} %collective-permute-done.4.s1, bf16[528,128]{1,0:T(8,128)(2,1)S(1)} %collective-permute-done.6.s2, bf16[528,128]{1,0:T(8,128)(2,1)S(1)} %collective-permute-done.7.s3, ...), custom_call_target="tpu_custom_call" | custom-call | flops 1 | bytes 1 | tf_op jit(solution)/shard_map/wgrad/pallas_call | solution.py:245
  39.9 4.8 %first.1 = (f32[512,608]{1,0:T(8,128)S(1)}, f32[512,256]{1,0:T(8,128)S(1)}, f32[1024,512]{1,0:T(8,128)}) custom-call(s32[2]{0:T(128)S(1)} %pad_add_fusion.place, bf16[528,128]{1,0:T(8,128)(2,1)S(1)} %get-tuple-element.23.s0, bf16[528,128]{1,0:T(8,128)(2,1)S(1)} %get-tuple-element.24.s1, bf16[5,128,640]{2,1,0:T(8,128)(2,1)S(1)} %pad.4.k0, ...), custom_call_target="tpu_custom_call" | custom-call | flops 1 | bytes 1 | tf_op jit(solution)/shard_map/first/pallas_call | solution.py:278
  44.6 8.3 %collective-permute-done.8.k2 = bf16[5,128,640]{2,1,0:T(8,128)(2,1)S(1)} collective-permute-done((bf16[5,128,640]{2,1,0:T(8,128)(2,1)S(1)}, bf16[5,128,640]{2,1,0:T(8,128)(2,1)S(1)}, u32[]{:S(2)}, u32[]{:S(2)}) %collective-permute-start.8) | collective-permute-done | bytes 819232 | tf_op jit(solution)/shard_map/ppermute | solution.py:189
  53.5 1.8 %collective-permute-done.13.k3 = bf16[5,128,640]{2,1,0:T(8,128)(2,1)S(1)} collective-permute-done((bf16[5,128,640]{2,1,0:T(8,128)(2,1)S(1)}, bf16[5,128,640]{2,1,0:T(8,128)(2,1)S(1)}, u32[]{:S(2)}, u32[]{:S(2)}) %collective-permute-start.13) | collective-permute-done | bytes 819232 | tf_op jit(solution)/shard_map/ppermute | solution.py:189
  55.3 6.6 %second.1 = (bf16[608,512]{1,0:T(8,128)(2,1)}, bf16[1024,512]{1,0:T(8,128)(2,1)}) custom-call(s32[2]{0:T(128)S(1)} %pad_add_fusion.place, bf16[528,128]{1,0:T(8,128)(2,1)S(1)} %get-tuple-element.26.s2, bf16[528,128]{1,0:T(8,128)(2,1)S(1)} %get-tuple-element.27.s3, bf16[5,128,640]{2,1,0:T(8,128)(2,1)S(1)} %collective-permute-done.8.k2, ...), custom_call_target="tpu_custom_call" | custom-call | flops 1 | bytes 1 | tf_op jit(solution)/shard_map/second/pallas_call | solution.py:294
  61.8 4.0 %collective-permute-done.14 = bf16[5,32,608]{2,1,0:T(8,128)(2,1)S(1)} collective-permute-done((bf16[5,32,608]{2,1,0:T(8,128)(2,1)S(1)}, bf16[5,32,608]{2,1,0:T(8,128)(2,1)S(1)}, u32[]{:S(2)}, u32[]{:S(2)}) %collective-permute-start.14) | collective-permute-done | bytes 194592 | tf_op jit(solution)/shard_map/ppermute | solution.py:189
  65.8 0.8 %add_bitcast_fusion = f32[32,5,608]{2,0,1:T(8,128)} fusion(bf16[5,32,608]{2,1,0:T(8,128)(2,1)S(1)} %collective-permute-done.14, f32[5,64,608]{2,1,0:T(8,128)S(1)} %convert_add_fusion), kind=kLoop, calls=%fused_computation.4 | loop fusion | flops 194560 | bytes 972800 | tf_op jit(solution)/shard_map/transpose | solution.py:313
  (32 shorter events, 3.1 us)
Async XLA Ops:
  0.6 14.8 %copy-start.2 = (bf16[32,5,608]{2,0,1:T(8,128)(2,1)S(1)}, bf16[32,5,608]{2,0,1:T(8,128)(2,1)}, u32[]{:S(2)}) copy-start(bf16[32,5,608]{2,0,1:T(8,128)(2,1)} %param.4) | copy-start | bytes 583684
  0.6 13.0 %copy-start = (bf16[1024,512]{1,0:T(8,128)(2,1)S(1)}, bf16[1024,512]{1,0:T(8,128)(2,1)}, u32[]{:S(2)}) copy-start(bf16[1024,512]{1,0:T(8,128)(2,1)} %act.3) | copy-start | bytes 3145732
  0.7 14.8 %collective-permute-start.2 = (bf16[5,32,608]{2,1,0:T(8,128)(2,1)}, bf16[5,32,608]{2,1,0:T(8,128)(2,1)S(1)}, u32[]{:S(2)}, u32[]{:S(2)}) collective-permute-start(bf16[5,32,608]{2,1,0:T(8,128)(2,1)} %bitcast.10), channel_id=1, source_target_pairs={{0,8},{1,9},{2,10},{3,11},{4,12},{5,13},{6,14},{7,15},{8,0},{9,1},... | collective-permute-start | bytes 583688 | tf_op jit(solution)/shard_map/ppermute | solution.py:189
  4.8 19.6 %collective-permute-start.5 = (bf16[608,512]{1,0:T(8,128)(2,1)}, bf16[608,512]{1,0:T(8,128)(2,1)S(1)}, u32[]{:S(2)}, u32[]{:S(2)}) collective-permute-start(bf16[608,512]{1,0:T(8,128)(2,1)} %bitcast.7), channel_id=1, source_target_pairs={{0,2},{1,3},{2,0},{3,1},{4,6},{5,7},{6,4},{7,5},{8,10},{9,11},{10,... | collective-permute-start | bytes 1867784 | tf_op jit(solution)/shard_map/ppermute | solution.py:189
  8.4 2.7 %collective-permute-start = (bf16[16,1120]{1,0:T(8,128)(2,1)S(1)}, bf16[16,1120]{1,0:T(8,128)(2,1)S(1)}, u32[]{:S(2)}, u32[]{:S(2)}) collective-permute-start(bf16[16,1120]{1,0:T(8,128)(2,1)S(1)} %pad_maximum_fusion.2), channel_id=1, source_target_pairs={{0,1},{1,2},{2,3},{3,4},{4,5},{5,6},{6,7},{7,8},{8,9},{9,10},{10,1... | collective-permute-start | bytes 107528 | tf_op jit(solution)/shard_map/ppermute | solution.py:210
  9.7 3.8 %collective-permute-start.1 = (bf16[16,1120]{1,0:T(8,128)(2,1)S(1)}, bf16[16,1120]{1,0:T(8,128)(2,1)S(1)}, u32[]{:S(2)}, u32[]{:S(2)}) collective-permute-start(bf16[16,1120]{1,0:T(8,128)(2,1)S(1)} %pad_maximum_fusion.3), channel_id=1, source_target_pairs={{1,0},{2,1},{3,2},{4,3},{5,4},{6,5},{7,6},{8,7},{9,8},{10,9},{11,1... | collective-permute-start | bytes 107528 | tf_op jit(solution)/shard_map/ppermute | solution.py:211
  15.5 18.6 %copy-start.1 = (bf16[512,608]{0,1:T(8,128)(2,1)S(1)}, bf16[512,608]{0,1:T(8,128)(2,1)}, u32[]{:S(2)}) copy-start(bf16[512,608]{0,1:T(8,128)(2,1)} %param.5) | copy-start | bytes 1867780
  15.5 11.0 %collective-permute-start.3 = (bf16[5,64,608]{2,1,0:T(8,128)(2,1)S(1)}, bf16[5,64,608]{2,1,0:T(8,128)(2,1)S(1)}, u32[]{:S(2)}, u32[]{:S(2)}) collective-permute-start(bf16[5,64,608]{2,1,0:T(8,128)(2,1)S(1)} %pad_maximum_fusion.1), channel_id=1, source_target_pairs={{0,4},{1,5},{2,6},{3,7},{4,0},{5,1},{6,2},{7,3},{8,12},{9,13},{10,... | collective-permute-start | bytes 1167368 | tf_op jit(solution)/shard_map/ppermute | solution.py:189
  20.1 6.5 %collective-permute-start.4 = (bf16[528,128]{1,0:T(8,128)(2,1)S(1)}, bf16[528,128]{1,0:T(8,128)(2,1)S(1)}, u32[]{:S(2)}, u32[]{:S(2)}) collective-permute-start(bf16[528,128]{1,0:T(8,128)(2,1)S(1)} %get-tuple-element.24.s1), channel_id=1, source_target_pairs={{0,1},{1,0},{2,3},{3,2},{4,5},{5,4},{6,7},{7,6},{8,9},{9,8},{10,11... | collective-permute-start | bytes 405512 | tf_op jit(solution)/shard_map/ppermute | solution.py:189
  24.3 6.5 %collective-permute-start.6 = (bf16[528,128]{1,0:T(8,128)(2,1)S(1)}, bf16[528,128]{1,0:T(8,128)(2,1)S(1)}, u32[]{:S(2)}, u32[]{:S(2)}) collective-permute-start(bf16[528,128]{1,0:T(8,128)(2,1)S(1)} %get-tuple-element.26.s2), channel_id=1, source_target_pairs={{0,2},{1,3},{2,0},{3,1},{4,6},{5,7},{6,4},{7,5},{8,10},{9,11},{10,... | collective-permute-start | bytes 405512 | tf_op jit(solution)/shard_map/ppermute | solution.py:189
  25.3 6.5 %collective-permute-start.7 = (bf16[528,128]{1,0:T(8,128)(2,1)S(1)}, bf16[528,128]{1,0:T(8,128)(2,1)S(1)}, u32[]{:S(2)}, u32[]{:S(2)}) collective-permute-start(bf16[528,128]{1,0:T(8,128)(2,1)S(1)} %get-tuple-element.27.s3), channel_id=1, source_target_pairs={{0,3},{1,2},{2,1},{3,0},{4,7},{5,6},{6,5},{7,4},{8,11},{9,10},{10,... | collective-permute-start | bytes 405512 | tf_op jit(solution)/shard_map/ppermute | solution.py:189
  31.8 8.0 %collective-permute-start.9 = (bf16[5,128,640]{2,1,0:T(8,128)(2,1)S(1)}, bf16[5,128,640]{2,1,0:T(8,128)(2,1)S(1)}, u32[]{:S(2)}, u32[]{:S(2)}) collective-permute-start(bf16[5,128,640]{2,1,0:T(8,128)(2,1)S(1)} %pad.4.k0), channel_id=1, source_target_pairs={{0,1},{1,0},{2,3},{3,2},{4,5},{5,4},{6,7},{7,6},{8,9},{9,8},{10,11... | collective-permute-start | bytes 2457608 | tf_op jit(solution)/shard_map/ppermute | solution.py:189
  32.7 20.2 %collective-permute-start.8 = (bf16[5,128,640]{2,1,0:T(8,128)(2,1)S(1)}, bf16[5,128,640]{2,1,0:T(8,128)(2,1)S(1)}, u32[]{:S(2)}, u32[]{:S(2)}) collective-permute-start(bf16[5,128,640]{2,1,0:T(8,128)(2,1)S(1)} %pad.4.k0), channel_id=1, source_target_pairs={{0,2},{1,3},{2,0},{3,1},{4,6},{5,7},{6,4},{7,5},{8,10},{9,11},{10,... | collective-permute-start | bytes 2457608 | tf_op jit(solution)/shard_map/ppermute | solution.py:189
  34.1 2.1 %collective-permute-start.10 = (bf16[608,512]{1,0:T(8,128)(2,1)S(1)}, bf16[608,512]{1,0:T(8,128)(2,1)S(1)}, u32[]{:S(2)}, u32[]{:S(2)}) collective-permute-start(bf16[608,512]{1,0:T(8,128)(2,1)S(1)} %bitcast.8), channel_id=1, source_target_pairs={{0,1},{1,0},{2,3},{3,2},{4,5},{5,4},{6,7},{7,6},{8,9},{9,8},{10,11... | collective-permute-start | bytes 1867784 | tf_op jit(solution)/shard_map/ppermute | solution.py:189
  34.2 2.9 %collective-permute-start.11 = (bf16[608,512]{1,0:T(8,128)(2,1)S(1)}, bf16[608,512]{1,0:T(8,128)(2,1)S(1)}, u32[]{:S(2)}, u32[]{:S(2)}) collective-permute-start(bf16[608,512]{1,0:T(8,128)(2,1)S(1)} %collective-permute-done.5.c2), channel_id=1, source_target_pairs={{0,1},{1,0},{2,3},{3,2},{4,5},{5,4},{6,7},{7,6},{8,9},{9,8},{10,11... | collective-permute-start | bytes 1867784 | tf_op jit(solution)/shard_map/ppermute | solution.py:189
  39.3 13.6 %collective-permute-start.12 = (bf16[5,64,608]{2,1,0:T(8,128)(2,1)S(1)}, bf16[5,64,608]{2,1,0:T(8,128)(2,1)S(1)}, u32[]{:S(2)}, u32[]{:S(2)}) collective-permute-start(bf16[5,64,608]{2,1,0:T(8,128)(2,1)S(1)} %get-tuple-element.32), channel_id=1, source_target_pairs={{0,4},{1,5},{2,6},{3,7},{4,0},{5,1},{6,2},{7,3},{8,12},{9,13},{10,... | collective-permute-start | bytes 1167368 | tf_op jit(solution)/shard_map/ppermute | solution.py:189
  52.9 2.3 %collective-permute-start.13 = (bf16[5,128,640]{2,1,0:T(8,128)(2,1)S(1)}, bf16[5,128,640]{2,1,0:T(8,128)(2,1)S(1)}, u32[]{:S(2)}, u32[]{:S(2)}) collective-permute-start(bf16[5,128,640]{2,1,0:T(8,128)(2,1)S(1)} %collective-permute-done.8.k2), channel_id=1, source_target_pairs={{0,1},{1,0},{2,3},{3,2},{4,5},{5,4},{6,7},{7,6},{8,9},{9,8},{10,11... | collective-permute-start | bytes 2457608 | tf_op jit(solution)/shard_map/ppermute | solution.py:189
  53.1 12.7 %collective-permute-start.14 = (bf16[5,32,608]{2,1,0:T(8,128)(2,1)S(1)}, bf16[5,32,608]{2,1,0:T(8,128)(2,1)S(1)}, u32[]{:S(2)}, u32[]{:S(2)}) collective-permute-start(bf16[5,32,608]{2,1,0:T(8,128)(2,1)S(1)} %slice.51), channel_id=1, source_target_pairs={{0,8},{1,9},{2,10},{3,11},{4,12},{5,13},{6,14},{7,15},{8,0},{9,1},... | collective-permute-start | bytes 583688 | tf_op jit(solution)/shard_map/ppermute | solution.py:189

commit v3 on v2

--- a/solution.py
+++ b/solution.py
@@ -203,8 +203,14 @@
     shard = kernel.transpose(1, 0, 2)
 
     cot_y = flip(cot_t, 2)
-    head = levels // 2
-    first_block = flip(shard, TEAM * head) if head else None
+    order = [0]
+    blocks = [shard]
+    while len(order) < levels:
+        bit = levels // 2 // len(order)
+        blocks = blocks + [flip(block, TEAM * bit) for block in blocks]
+        order += [m ^ bit for m in order]
+    k0 = jnp.concatenate(blocks, axis=1)
+    early = blocks[1:2] + blocks[levels // 2 : levels // 2 + 1]
     edge_low = jnp.concatenate([activations[-HALO:], cotangent[-HALO:]], axis=1)
     edge_high = jnp.concatenate([activations[:HALO], cotangent[:HALO]], axis=1)
     low = lax.ppermute(edge_low, "pos", [(i, i + 1) for i in range(n - 1)])
@@ -217,28 +223,19 @@
         out_shape=[jax.ShapeDtypeStruct((ext_rows, quarter), BF16)] * TEAM,
         in_specs=[SMEM, VMEM, VMEM, VMEM],
         out_specs=[VMEM] * TEAM,
-        cost_estimate=pl.CostEstimate(flops=1, bytes_accessed=1, transcendentals=0),
         compiler_params=params(32),
         name="pool",
-    )(place, activations, low[:, :channels], high[:, :channels])
-
-    order = [0]
-    k0 = shard
-    while len(order) < levels:
-        bit = levels // 2 // len(order)
-        got = after(first_block, pieces) if bit == head else flip(k0, TEAM * bit)
-        k0 = jnp.concatenate([k0, got], axis=1)
-        order += [m ^ bit for m in order]
+    )(place, after(activations, *early), low[:, :channels], high[:, :channels])
+
     far = after(pieces[2:], cot_y)
     mates = [pieces[0], flip(pieces[1], 1), flip(far[0], 2), flip(far[1], 3)]
     cot_y = after(cot_y, mates[1])
     cot_yc = flip(cot_y, 1)
 
-    halves = max(levels // 2, 1)
     split = rows % 16 == 0
     if split:
         grad_shape = [
-            jax.ShapeDtypeStruct((TAPS, halves * rows, width), dtype) for dtype in (F32, BF16)
+            jax.ShapeDtypeStruct((TAPS, rows, width), BF16 if m else F32) for m in range(levels)
         ]
     else:
         grad_shape = [jax.ShapeDtypeStruct((TAPS, quarter, width), F32)]
@@ -248,28 +245,15 @@
         in_specs=[VMEM] * 8,
         out_specs=[VMEM] * len(grad_shape),
         scratch_shapes=[pltpu.VMEM((TAPS * quarter, positions), BF16)],
-        cost_estimate=pl.CostEstimate(flops=1, bytes_accessed=1, transcendentals=0),
         compiler_params=params(48),
         name="wgrad",
     )(*mates, cot_t, cot_c, cot_y, cot_yc)
-    keep = grads[0] if split else grads[0][:, : halves * rows]
-    give = grads[1] if split else grads[0][:, halves * rows :].astype(BF16)
-    bits = []
-    bit = 1
-    while bit < levels:
-        bits.append(bit)
-        bit *= 2
-    last = None
-    for i, bit in enumerate(bits):
-        got = flip(give, TEAM * bit)
-        if i + 1 == len(bits):
-            last = (keep, got)
-            break
-        keep = keep + got.astype(F32)
-        half = keep.shape[1] // 2
-        keep, give = keep[:, :half], keep[:, half:].astype(BF16)
-
-    k0 = after(k0, mates)
+    if not split:
+        parts = [grads[0][:, m * rows : (m + 1) * rows] for m in range(levels)]
+        grads = parts[:1] + [p.astype(BF16) for p in parts[1:]]
+    terms = [flip(g, TEAM * m) for g, m in zip(grads[1:], order[1:])]
+
+    k0 = after(k0, mates, cot_c, cot_yc)
     k0 = jnp.pad(k0, ((0, 0), (0, 0), (0, -width % 128)))
     k2 = flip(k0, 2)
     k1 = flip(k0, 1)
@@ -285,11 +269,10 @@
         in_specs=[SMEM] + [VMEM] * 8,
         out_specs=[VMEM] * 3,
         scratch_shapes=[pltpu.VMEM((positions + 2 * HALO, width), BF16)],
-        cost_estimate=pl.CostEstimate(flops=1, bytes_accessed=1, transcendentals=0),
         compiler_params=params(48),
         name="first",
     )(place, pieces[0], pieces[1], k0, k1, cotangent, low_cot, high_cot, activations)
-    k2 = after(k2, acc, keep)
+    k2 = after(k2, acc, terms)
     k3 = flip(k2, 1)
     pooled_t, input_grad = pl.pallas_call(
         functools.partial(second_kernel, rows),
@@ -303,14 +286,13 @@
             pltpu.VMEM((positions + 2 * HALO, width), BF16),
             pltpu.VMEM((channels // 128, window, 128), F32),
         ],
-        cost_estimate=pl.CostEstimate(flops=1, bytes_accessed=1, transcendentals=0),
         compiler_params=params(48),
         name="second",
     )(place, pieces[2], pieces[3], k2, k3, cotangent, low_cot, high_cot, acc, grad, slope)
-    if last is not None:
-        keep, got = last[0], after(last[1], pooled_t)
-        keep = keep + got.astype(F32)
-    return pooled_t.T, input_grad, keep.transpose(1, 0, 2)
+    total = grads[0]
+    for term in terms:
+        total = total + term.astype(F32)
+    return pooled_t.T, input_grad, total.transpose(1, 0, 2)
 
 
 def solution(mesh):

time: 67 us -> 65.4 us (0.976)
  the two profiles are of different devices: /device:TPU:0 before, /device:TPU:9 now
where the time goes in v3:
time: 65.4 us; the launch traced here: 65 us
  waiting for transfers between devices  26.4 us (40%)
  starting transfers between devices  18.2 us (28%)
  Pallas kernels  15.4 us (24%)
  local copies, waits for them, and re-layouts  2.26 us (3%)
  other arithmetic  1.96 us (3%)
  between operations  0.79 us (1%)
    ppermute x15, waiting for transfers between devices, flip(): return lax.ppermute(x, 'pos', [(i, i ^ bit) for i in range(n)])  18.7 us
    ppermute x15, starting transfers between devices, flip(): return lax.ppermute(x, 'pos', [(i, i ^ bit) for i in range(n)])  12.7 us
    pallas_call x1, Pallas kernels, on_device(): pl.pallas_call(functools.partial(second_kernel, rows), out_shape=[jax.Sha...  6.56 us
    ppermute x1, waiting for transfers between devices, on_device(): low = lax.ppermute(edge_low, 'pos', [(i, i + 1) for i in range(n - 1)])  5.73 us
    pallas_call x1, Pallas kernels, on_device(): pl.pallas_call(functools.partial(first_kernel, rows), out_shape=[jax.Shap...  4.75 us
    ppermute x1, starting transfers between devices, on_device(): low = lax.ppermute(edge_low, 'pos', [(i, i + 1) for i in range(n - 1)])  3.53 us
    pallas_call x1, Pallas kernels, on_device(): pl.pallas_call(functools.partial(wgrad_kernel, rows), out_shape=grad_shap...  2.25 us
    ppermute x1, waiting for transfers between devices, on_device(): high = lax.ppermute(edge_high, 'pos', [(i + 1, i) for i in range(n - 1)])  2.03 us
  transfers between devices with their start and end apart: 17, of which 8 were waited for; matrix products, arithmetic and copies ran while one was open for 6% of the time, Pallas kernels for 14%

profile of v3, /device:TPU:9, one launch (start us, length us, event | category | flops | bytes accessed | tf_op | source)
XLA Modules:
  0.0 65.0 jit_solution(1138936941191460268)
XLA Ops:
  0.7 2.4 %collective-permute-start = (bf16[5,32,608]{2,1,0:T(8,128)(2,1)}, bf16[5,32,608]{2,1,0:T(8,128)(2,1)S(1)}, u32[]{:S(2)}, u32[]{:S(2)}) collective-permute-start(bf16[5,32,608]{2,1,0:T(8,128)(2,1)} %bitcast.10), channel_id=1, source_target_pairs={{0,8},{1,9},{2,10},{3,11},{4,12},{5,13},{6,14},{7,15},{8,0},{9,1},... | collective-permute-start | bytes 583688 | tf_op jit(solution)/shard_map/ppermute | solution.py:189
  3.2 1.2 %collective-permute-start.6 = (bf16[608,512]{1,0:T(8,128)(2,1)}, bf16[608,512]{1,0:T(8,128)(2,1)S(1)}, u32[]{:S(2)}, u32[]{:S(2)}) collective-permute-start(bf16[608,512]{1,0:T(8,128)(2,1)} %bitcast.7), channel_id=1, source_target_pairs={{0,2},{1,3},{2,0},{3,1},{4,6},{5,7},{6,4},{7,5},{8,10},{9,11},{10,... | collective-permute-start | bytes 1867784 | tf_op jit(solution)/shard_map/ppermute | solution.py:189
  4.4 1.4 %copy.6.cot = bf16[512,608]{1,0:T(8,128)(2,1)S(1)} copy(bf16[512,608]{0,1:T(8,128)(2,1)} %param.5) | data formatting | bytes 1245184 | tf_op args[2]
  6.6 3.5 %collective-permute-start.2 = (bf16[16,1120]{1,0:T(8,128)(2,1)S(1)}, bf16[16,1120]{1,0:T(8,128)(2,1)S(1)}, u32[]{:S(2)}, u32[]{:S(2)}) collective-permute-start(bf16[16,1120]{1,0:T(8,128)(2,1)S(1)} %pad_maximum_fusion.1), channel_id=1, source_target_pairs={{0,1},{1,2},{2,3},{3,4},{4,5},{5,6},{6,7},{7,8},{8,9},{9,10},{10,1... | collective-permute-start | bytes 107528 | tf_op jit(solution)/shard_map/ppermute | solution.py:216
  10.2 1.9 %collective-permute-start.3 = (bf16[16,1120]{1,0:T(8,128)(2,1)S(1)}, bf16[16,1120]{1,0:T(8,128)(2,1)S(1)}, u32[]{:S(2)}, u32[]{:S(2)}) collective-permute-start(bf16[16,1120]{1,0:T(8,128)(2,1)S(1)} %pad_maximum_fusion.2), channel_id=1, source_target_pairs={{1,0},{2,1},{3,2},{4,3},{5,4},{6,5},{7,6},{8,7},{9,8},{10,9},{11,1... | collective-permute-start | bytes 107528 | tf_op jit(solution)/shard_map/ppermute | solution.py:217
  12.2 5.7 %collective-permute-done.2 = bf16[16,1120]{1,0:T(8,128)(2,1)S(1)} collective-permute-done((bf16[16,1120]{1,0:T(8,128)(2,1)S(1)}, bf16[16,1120]{1,0:T(8,128)(2,1)S(1)}, u32[]{:S(2)}, u32[]{:S(2)}) %collective-permute-start.2) | collective-permute-done | bytes 35872 | tf_op jit(solution)/shard_map/ppermute | solution.py:216
  17.9 2.0 %collective-permute-done.3 = bf16[16,1120]{1,0:T(8,128)(2,1)S(1)} collective-permute-done((bf16[16,1120]{1,0:T(8,128)(2,1)S(1)}, bf16[16,1120]{1,0:T(8,128)(2,1)S(1)}, u32[]{:S(2)}, u32[]{:S(2)}) %collective-permute-start.3) | collective-permute-done | bytes 35872 | tf_op jit(solution)/shard_map/ppermute | solution.py:217
  20.0 1.8 %pool.1 = (bf16[528,128]{1,0:T(8,128)(2,1)S(1)}, bf16[528,128]{1,0:T(8,128)(2,1)S(1)}, bf16[528,128]{1,0:T(8,128)(2,1)S(1)}, bf16[528,128]{1,0:T(8,128)(2,1)S(1)}) custom-call(s32[2]{0:T(128)S(1)} %pad_add_fusion.place, bf16[1024,512]{1,0:T(8,128)(2,1)S(1)} %copy-done, bf16[16,512]{1,0:T(8,128)(2,1)S(1)} %slice.33.low, bf16[16,512]{1,0:T(8,128)(2,1)S(1)} %slice.35.high), custom_call_target="tpu_custom_call" | custom-call | tf_op jit(solution)/shard_map/pool/pallas_call | solution.py:221
  22.3 0.8 %collective-permute-done.5.s1 = bf16[528,128]{1,0:T(8,128)(2,1)S(1)} collective-permute-done((bf16[528,128]{1,0:T(8,128)(2,1)S(1)}, bf16[528,128]{1,0:T(8,128)(2,1)S(1)}, u32[]{:S(2)}, u32[]{:S(2)}) %collective-permute-start.5) | collective-permute-done | bytes 135200 | tf_op jit(solution)/shard_map/ppermute | solution.py:189
  23.3 0.9 %collective-permute-start.4 = (bf16[5,32,608]{2,1,0:T(8,128)(2,1)S(1)}, bf16[5,32,608]{2,1,0:T(8,128)(2,1)S(1)}, u32[]{:S(2)}, u32[]{:S(2)}) collective-permute-start(bf16[5,32,608]{2,1,0:T(8,128)(2,1)S(1)} %collective-permute-done), channel_id=1, source_target_pairs={{0,4},{1,5},{2,6},{3,7},{4,0},{5,1},{6,2},{7,3},{8,12},{9,13},{10,... | collective-permute-start | bytes 583688 | tf_op jit(solution)/shard_map/ppermute | solution.py:189
  25.1 1.4 %collective-permute-start.8 = (bf16[528,128]{1,0:T(8,128)(2,1)S(1)}, bf16[528,128]{1,0:T(8,128)(2,1)S(1)}, u32[]{:S(2)}, u32[]{:S(2)}) collective-permute-start(bf16[528,128]{1,0:T(8,128)(2,1)S(1)} %get-tuple-element.28.s3), channel_id=1, source_target_pairs={{0,3},{1,2},{2,1},{3,0},{4,7},{5,6},{6,5},{7,4},{8,11},{9,10},{10,... | collective-permute-start | bytes 405512 | tf_op jit(solution)/shard_map/ppermute | solution.py:189
  26.5 3.1 %collective-permute-done.4 = bf16[5,32,608]{2,1,0:T(8,128)(2,1)S(1)} collective-permute-done((bf16[5,32,608]{2,1,0:T(8,128)(2,1)S(1)}, bf16[5,32,608]{2,1,0:T(8,128)(2,1)S(1)}, u32[]{:S(2)}, u32[]{:S(2)}) %collective-permute-start.4) | collective-permute-done | bytes 194592 | tf_op jit(solution)/shard_map/ppermute | solution.py:189
  29.6 1.0 %pad_maximum_fusion = bf16[5,128,608]{2,1,0:T(8,128)(2,1)S(1)} fusion(bf16[5,32,608]{2,1,0:T(8,128)(2,1)S(1)} %collective-permute-done.4, bf16[5,32,608]{2,1,0:T(8,128)(2,1)} %collective-permute-done.1, bf16[5,32,608]{2,1,0:T(8,128)(2,1)S(1)} %collective-permute-done, bf16[5,32,608]{2,1,0:T(8,128)(2,1)S(1)} %bitcast.12), kind=kLoop, calls=%fused_computation | loop fusion | flops 3112960 | bytes 1556480 | tf_op jit(solution)/shard_map/concatenate | solution.py:212
  30.7 1.8 %collective-permute-done.8.s3 = bf16[528,128]{1,0:T(8,128)(2,1)S(1)} collective-permute-done((bf16[528,128]{1,0:T(8,128)(2,1)S(1)}, bf16[528,128]{1,0:T(8,128)(2,1)S(1)}, u32[]{:S(2)}, u32[]{:S(2)}) %collective-permute-start.8) | collective-permute-done | bytes 135200 | tf_op jit(solution)/shard_map/ppermute | solution.py:189
  32.6 0.9 %collective-permute-start.11 = (bf16[5,128,640]{2,1,0:T(8,128)(2,1)S(1)}, bf16[5,128,640]{2,1,0:T(8,128)(2,1)S(1)}, u32[]{:S(2)}, u32[]{:S(2)}) collective-permute-start(bf16[5,128,640]{2,1,0:T(8,128)(2,1)S(1)} %pad.4.k0), channel_id=1, source_target_pairs={{0,2},{1,3},{2,0},{3,1},{4,6},{5,7},{6,4},{7,5},{8,10},{9,11},{10,... | collective-permute-start | bytes 2457608 | tf_op jit(solution)/shard_map/ppermute | solution.py:189
  33.5 2.3 %wgrad.1 = (f32[5,32,608]{2,1,0:T(8,128)S(1)}, bf16[5,32,608]{2,1,0:T(8,128)(2,1)S(1)}, bf16[5,32,608]{2,1,0:T(8,128)(2,1)S(1)}, bf16[5,32,608]{2,1,0:T(8,128)(2,1)S(1)}) custom-call(bf16[528,128]{1,0:T(8,128)(2,1)S(1)} %get-tuple-element.25.s0, bf16[528,128]{1,0:T(8,128)(2,1)S(1)} %collective-permute-done.5.s1, ...), custom_call_target="tpu_custom_call" | custom-call | tf_op jit(solution)/shard_map/wgrad/pallas_call | solution.py:242
  36.2 2.3 %collective-permute-start.15 = (bf16[5,32,608]{2,1,0:T(8,128)(2,1)S(1)}, bf16[5,32,608]{2,1,0:T(8,128)(2,1)S(1)}, u32[]{:S(2)}, u32[]{:S(2)}) collective-permute-start(bf16[5,32,608]{2,1,0:T(8,128)(2,1)S(1)} %get-tuple-element.34), channel_id=1, source_target_pairs={{0,12},{1,13},{2,14},{3,15},{4,8},{5,9},{6,10},{7,11},{8,4},{9,5},... | collective-permute-start | bytes 583688 | tf_op jit(solution)/shard_map/ppermute | solution.py:189
  38.5 4.7 %first.1 = (f32[512,608]{1,0:T(8,128)S(1)}, f32[512,256]{1,0:T(8,128)S(1)}, f32[1024,512]{1,0:T(8,128)}) custom-call(s32[2]{0:T(128)S(1)} %pad_add_fusion.place, bf16[528,128]{1,0:T(8,128)(2,1)S(1)} %get-tuple-element.25.s0, bf16[528,128]{1,0:T(8,128)(2,1)S(1)} %get-tuple-element.26.s1, bf16[5,128,640]{2,1,0:T(8,128)(2,1)S(1)} %pad.4.k0, ...), custom_call_target="tpu_custom_call" | custom-call | tf_op jit(solution)/shard_map/first/pallas_call | solution.py:262
  43.2 2.2 %collective-permute-done.13 = bf16[5,32,608]{2,1,0:T(8,128)(2,1)S(1)} collective-permute-done((bf16[5,32,608]{2,1,0:T(8,128)(2,1)S(1)}, bf16[5,32,608]{2,1,0:T(8,128)(2,1)S(1)}, u32[]{:S(2)}, u32[]{:S(2)}) %collective-permute-start.13) | collective-permute-done | bytes 194592 | tf_op jit(solution)/shard_map/ppermute | solution.py:189
  45.4 9.6 %collective-permute-done.15 = bf16[5,32,608]{2,1,0:T(8,128)(2,1)S(1)} collective-permute-done((bf16[5,32,608]{2,1,0:T(8,128)(2,1)S(1)}, bf16[5,32,608]{2,1,0:T(8,128)(2,1)S(1)}, u32[]{:S(2)}, u32[]{:S(2)}) %collective-permute-start.15) | collective-permute-done | bytes 194592 | tf_op jit(solution)/shard_map/ppermute | solution.py:189
  55.0 1.4 %collective-permute-start.16 = (bf16[5,128,640]{2,1,0:T(8,128)(2,1)S(1)}, bf16[5,128,640]{2,1,0:T(8,128)(2,1)S(1)}, u32[]{:S(2)}, u32[]{:S(2)}) collective-permute-start(bf16[5,128,640]{2,1,0:T(8,128)(2,1)S(1)} %collective-permute-done.11.k2), channel_id=1, source_target_pairs={{0,1},{1,0},{2,3},{3,2},{4,5},{5,4},{6,7},{7,6},{8,9},{9,8},{10,11... | collective-permute-start | bytes 2457608 | tf_op jit(solution)/shard_map/ppermute | solution.py:189
  56.5 0.9 %add_bitcast_fusion = f32[32,5,608]{2,0,1:T(8,128)} fusion(bf16[5,32,608]{2,1,0:T(8,128)(2,1)S(1)} %collective-permute-done.15, bf16[5,32,608]{2,1,0:T(8,128)(2,1)S(1)} %collective-permute-done.14, f32[5,32,608]{2,1,0:T(8,128)S(1)} %get-tuple-element.40, bf16[5,32,608]{2,1,0:T(8,128)(2,1)S(1)} %collective-permute-done.13), kind=kLoop, calls=%fused_computation.1 | loop fusion | flops 583680 | bytes 1361920 | tf_op jit(solution)/shard_map/transpose | solution.py:295
  57.3 1.1 %collective-permute-done.16.k3 = bf16[5,128,640]{2,1,0:T(8,128)(2,1)S(1)} collective-permute-done((bf16[5,128,640]{2,1,0:T(8,128)(2,1)S(1)}, bf16[5,128,640]{2,1,0:T(8,128)(2,1)S(1)}, u32[]{:S(2)}, u32[]{:S(2)}) %collective-permute-start.16) | collective-permute-done | bytes 819232 | tf_op jit(solution)/shard_map/ppermute | solution.py:189
  58.4 6.6 %second.1 = (bf16[608,512]{1,0:T(8,128)(2,1)}, bf16[1024,512]{1,0:T(8,128)(2,1)}) custom-call(s32[2]{0:T(128)S(1)} %pad_add_fusion.place, bf16[528,128]{1,0:T(8,128)(2,1)S(1)} %get-tuple-element.27.s2, bf16[528,128]{1,0:T(8,128)(2,1)S(1)} %get-tuple-element.28.s3, bf16[5,128,640]{2,1,0:T(8,128)(2,1)S(1)} %collective-permute-done.11.k2, ...), custom_call_target="tpu_custom_call" | custom-call | tf_op jit(solution)/shard_map/second/pallas_call | solution.py:277
  (33 shorter events, 3.1 us)
Async XLA Ops:
  0.6 21.2 %copy-start.1 = (bf16[512,608]{0,1:T(8,128)(2,1)S(1)}, bf16[512,608]{0,1:T(8,128)(2,1)}, u32[]{:S(2)}) copy-start(bf16[512,608]{0,1:T(8,128)(2,1)} %param.5) | copy-start | bytes 1867780
  0.6 19.3 %copy-start = (bf16[1024,512]{1,0:T(8,128)(2,1)S(1)}, bf16[1024,512]{1,0:T(8,128)(2,1)}, u32[]{:S(2)}) copy-start(bf16[1024,512]{1,0:T(8,128)(2,1)} %act.2) | copy-start | bytes 3145732
  0.7 29.0 %copy-start.2 = (bf16[32,5,608]{2,0,1:T(8,128)(2,1)S(1)}, bf16[32,5,608]{2,0,1:T(8,128)(2,1)}, u32[]{:S(2)}) copy-start(bf16[32,5,608]{2,0,1:T(8,128)(2,1)} %param.4) | copy-start | bytes 583684
  0.7 19.3 %collective-permute-start = (bf16[5,32,608]{2,1,0:T(8,128)(2,1)}, bf16[5,32,608]{2,1,0:T(8,128)(2,1)S(1)}, u32[]{:S(2)}, u32[]{:S(2)}) collective-permute-start(bf16[5,32,608]{2,1,0:T(8,128)(2,1)} %bitcast.10), channel_id=1, source_target_pairs={{0,8},{1,9},{2,10},{3,11},{4,12},{5,13},{6,14},{7,15},{8,0},{9,1},... | collective-permute-start | bytes 583688 | tf_op jit(solution)/shard_map/ppermute | solution.py:189
  3.0 16.9 %collective-permute-start.1 = (bf16[5,32,608]{2,1,0:T(8,128)(2,1)}, bf16[5,32,608]{2,1,0:T(8,128)(2,1)}, u32[]{:S(2)}, u32[]{:S(2)}) collective-permute-start(bf16[5,32,608]{2,1,0:T(8,128)(2,1)} %bitcast.11), channel_id=1, source_target_pairs={{0,4},{1,5},{2,6},{3,7},{4,0},{5,1},{6,2},{7,3},{8,12},{9,13},{10,... | collective-permute-start | bytes 583688 | tf_op jit(solution)/shard_map/ppermute | solution.py:189
  3.2 20.0 %collective-permute-start.6 = (bf16[608,512]{1,0:T(8,128)(2,1)}, bf16[608,512]{1,0:T(8,128)(2,1)S(1)}, u32[]{:S(2)}, u32[]{:S(2)}) collective-permute-start(bf16[608,512]{1,0:T(8,128)(2,1)} %bitcast.7), channel_id=1, source_target_pairs={{0,2},{1,3},{2,0},{3,1},{4,6},{5,7},{6,4},{7,5},{8,10},{9,11},{10,... | collective-permute-start | bytes 1867784 | tf_op jit(solution)/shard_map/ppermute | solution.py:189
  6.6 11.3 %collective-permute-start.2 = (bf16[16,1120]{1,0:T(8,128)(2,1)S(1)}, bf16[16,1120]{1,0:T(8,128)(2,1)S(1)}, u32[]{:S(2)}, u32[]{:S(2)}) collective-permute-start(bf16[16,1120]{1,0:T(8,128)(2,1)S(1)} %pad_maximum_fusion.1), channel_id=1, source_target_pairs={{0,1},{1,2},{2,3},{3,4},{4,5},{5,6},{6,7},{7,8},{8,9},{9,10},{10,1... | collective-permute-start | bytes 107528 | tf_op jit(solution)/shard_map/ppermute | solution.py:216
  10.2 9.8 %collective-permute-start.3 = (bf16[16,1120]{1,0:T(8,128)(2,1)S(1)}, bf16[16,1120]{1,0:T(8,128)(2,1)S(1)}, u32[]{:S(2)}, u32[]{:S(2)}) collective-permute-start(bf16[16,1120]{1,0:T(8,128)(2,1)S(1)} %pad_maximum_fusion.2), channel_id=1, source_target_pairs={{1,0},{2,1},{3,2},{4,3},{5,4},{6,5},{7,6},{8,7},{9,8},{10,9},{11,1... | collective-permute-start | bytes 107528 | tf_op jit(solution)/shard_map/ppermute | solution.py:217
  21.8 1.4 %collective-permute-start.5 = (bf16[528,128]{1,0:T(8,128)(2,1)S(1)}, bf16[528,128]{1,0:T(8,128)(2,1)S(1)}, u32[]{:S(2)}, u32[]{:S(2)}) collective-permute-start(bf16[528,128]{1,0:T(8,128)(2,1)S(1)} %get-tuple-element.26.s1), channel_id=1, source_target_pairs={{0,1},{1,0},{2,3},{3,2},{4,5},{5,4},{6,7},{7,6},{8,9},{9,8},{10,11... | collective-permute-start | bytes 405512 | tf_op jit(solution)/shard_map/ppermute | solution.py:189
  21.8 8.8 %collective-permute-start.9 = (bf16[608,512]{1,0:T(8,128)(2,1)S(1)}, bf16[608,512]{1,0:T(8,128)(2,1)S(1)}, u32[]{:S(2)}, u32[]{:S(2)}) collective-permute-start(bf16[608,512]{1,0:T(8,128)(2,1)S(1)} %bitcast.8), channel_id=1, source_target_pairs={{0,1},{1,0},{2,3},{3,2},{4,5},{5,4},{6,7},{7,6},{8,9},{9,8},{10,11... | collective-permute-start | bytes 1867784 | tf_op jit(solution)/shard_map/ppermute | solution.py:189
  23.2 9.3 %collective-permute-start.10 = (bf16[608,512]{1,0:T(8,128)(2,1)S(1)}, bf16[608,512]{1,0:T(8,128)(2,1)S(1)}, u32[]{:S(2)}, u32[]{:S(2)}) collective-permute-start(bf16[608,512]{1,0:T(8,128)(2,1)S(1)} %collective-permute-done.6.c2), channel_id=1, source_target_pairs={{0,1},{1,0},{2,3},{3,2},{4,5},{5,4},{6,7},{7,6},{8,9},{9,8},{10,11... | collective-permute-start | bytes 1867784 | tf_op jit(solution)/shard_map/ppermute | solution.py:189
  23.3 6.3 %collective-permute-start.4 = (bf16[5,32,608]{2,1,0:T(8,128)(2,1)S(1)}, bf16[5,32,608]{2,1,0:T(8,128)(2,1)S(1)}, u32[]{:S(2)}, u32[]{:S(2)}) collective-permute-start(bf16[5,32,608]{2,1,0:T(8,128)(2,1)S(1)} %collective-permute-done), channel_id=1, source_target_pairs={{0,4},{1,5},{2,6},{3,7},{4,0},{5,1},{6,2},{7,3},{8,12},{9,13},{10,... | collective-permute-start | bytes 583688 | tf_op jit(solution)/shard_map/ppermute | solution.py:189
  24.2 6.4 %collective-permute-start.7 = (bf16[528,128]{1,0:T(8,128)(2,1)S(1)}, bf16[528,128]{1,0:T(8,128)(2,1)S(1)}, u32[]{:S(2)}, u32[]{:S(2)}) collective-permute-start(bf16[528,128]{1,0:T(8,128)(2,1)S(1)} %get-tuple-element.27.s2), channel_id=1, source_target_pairs={{0,2},{1,3},{2,0},{3,1},{4,6},{5,7},{6,4},{7,5},{8,10},{9,11},{10,... | collective-permute-start | bytes 405512 | tf_op jit(solution)/shard_map/ppermute | solution.py:189
  25.1 7.4 %collective-permute-start.8 = (bf16[528,128]{1,0:T(8,128)(2,1)S(1)}, bf16[528,128]{1,0:T(8,128)(2,1)S(1)}, u32[]{:S(2)}, u32[]{:S(2)}) collective-permute-start(bf16[528,128]{1,0:T(8,128)(2,1)S(1)} %get-tuple-element.28.s3), channel_id=1, source_target_pairs={{0,3},{1,2},{2,1},{3,0},{4,7},{5,6},{6,5},{7,4},{8,11},{9,10},{10,... | collective-permute-start | bytes 405512 | tf_op jit(solution)/shard_map/ppermute | solution.py:189
  32.5 6.0 %collective-permute-start.12 = (bf16[5,128,640]{2,1,0:T(8,128)(2,1)S(1)}, bf16[5,128,640]{2,1,0:T(8,128)(2,1)S(1)}, u32[]{:S(2)}, u32[]{:S(2)}) collective-permute-start(bf16[5,128,640]{2,1,0:T(8,128)(2,1)S(1)} %pad.4.k0), channel_id=1, source_target_pairs={{0,1},{1,0},{2,3},{3,2},{4,5},{5,4},{6,7},{7,6},{8,9},{9,8},{10,11... | collective-permute-start | bytes 2457608 | tf_op jit(solution)/shard_map/ppermute | solution.py:189
  32.6 22.4 %collective-permute-start.11 = (bf16[5,128,640]{2,1,0:T(8,128)(2,1)S(1)}, bf16[5,128,640]{2,1,0:T(8,128)(2,1)S(1)}, u32[]{:S(2)}, u32[]{:S(2)}) collective-permute-start(bf16[5,128,640]{2,1,0:T(8,128)(2,1)S(1)} %pad.4.k0), channel_id=1, source_target_pairs={{0,2},{1,3},{2,0},{3,1},{4,6},{5,7},{6,4},{7,5},{8,10},{9,11},{10,... | collective-permute-start | bytes 2457608 | tf_op jit(solution)/shard_map/ppermute | solution.py:189
  35.8 9.7 %collective-permute-start.13 = (bf16[5,32,608]{2,1,0:T(8,128)(2,1)S(1)}, bf16[5,32,608]{2,1,0:T(8,128)(2,1)S(1)}, u32[]{:S(2)}, u32[]{:S(2)}) collective-permute-start(bf16[5,32,608]{2,1,0:T(8,128)(2,1)S(1)} %get-tuple-element.32), channel_id=1, source_target_pairs={{0,8},{1,9},{2,10},{3,11},{4,12},{5,13},{6,14},{7,15},{8,0},{9,1},... | collective-permute-start | bytes 583688 | tf_op jit(solution)/shard_map/ppermute | solution.py:189
  35.9 9.5 %collective-permute-start.14 = (bf16[5,32,608]{2,1,0:T(8,128)(2,1)S(1)}, bf16[5,32,608]{2,1,0:T(8,128)(2,1)S(1)}, u32[]{:S(2)}, u32[]{:S(2)}) collective-permute-start(bf16[5,32,608]{2,1,0:T(8,128)(2,1)S(1)} %get-tuple-element.33), channel_id=1, source_target_pairs={{0,4},{1,5},{2,6},{3,7},{4,0},{5,1},{6,2},{7,3},{8,12},{9,13},{10,... | collective-permute-start | bytes 583688 | tf_op jit(solution)/shard_map/ppermute | solution.py:189
  36.2 18.8 %collective-permute-start.15 = (bf16[5,32,608]{2,1,0:T(8,128)(2,1)S(1)}, bf16[5,32,608]{2,1,0:T(8,128)(2,1)S(1)}, u32[]{:S(2)}, u32[]{:S(2)}) collective-permute-start(bf16[5,32,608]{2,1,0:T(8,128)(2,1)S(1)} %get-tuple-element.34), channel_id=1, source_target_pairs={{0,12},{1,13},{2,14},{3,15},{4,8},{5,9},{6,10},{7,11},{8,4},{9,5},... | collective-permute-start | bytes 583688 | tf_op jit(solution)/shard_map/ppermute | solution.py:189
  55.0 3.4 %collective-permute-start.16 = (bf16[5,128,640]{2,1,0:T(8,128)(2,1)S(1)}, bf16[5,128,640]{2,1,0:T(8,128)(2,1)S(1)}, u32[]{:S(2)}, u32[]{:S(2)}) collective-permute-start(bf16[5,128,640]{2,1,0:T(8,128)(2,1)S(1)} %collective-permute-done.11.k2), channel_id=1, source_target_pairs={{0,1},{1,0},{2,3},{3,2},{4,5},{5,4},{6,7},{7,6},{8,9},{9,8},{10,11... | collective-permute-start | bytes 2457608 | tf_op jit(solution)/shard_map/ppermute | solution.py:189

commit v4 on v3

--- a/solution.py
+++ b/solution.py
@@ -115,69 +115,83 @@
     ext[HALO + positions :, :] = high[...]
 
 
-def pair_products(s_pair, k_pair, ext, positions):
-    acc = None
+def taps_of(k_a, k_b, width):
+    return [jnp.concatenate([k_a[k], k_b[k]], axis=0)[:, :width] for k in range(TAPS)]
+
+
+def products(columns, shifted, weights):
+    acc = jnp.dot(columns, jnp.concatenate(weights, axis=0), preferred_element_type=F32)
     grad = None
-    for k in range(TAPS):
-        at = EXT + 2 * (k - 2)
-        weights = k_pair(k)
-        term = jnp.dot(s_pair(at), weights, preferred_element_type=F32)
-        acc = term if acc is None else acc + term
-        back = HALO - 2 * (k - 2)
+    for k, weight in enumerate(weights):
         term = lax.dot_general(
-            ext[back : back + positions, :],
-            weights,
-            (((1,), (1,)), ((), ())),
-            preferred_element_type=F32,
+            shifted[k], weight, (((1,), (1,)), ((), ())), preferred_element_type=F32
         )
         grad = term if grad is None else grad + term
     return acc, grad
 
 
-def first_kernel(rows, place, s0, s1, k0, k1, cot, low, high, act, acc, grad, slope, ext):
-    positions = cot.shape[0]
-    fill_ext(ext, cot, low, high)
-    acc[...], grad[...] = pair_products(
-        lambda at: jnp.concatenate([s0[at : at + positions], s1[at : at + positions]], axis=1),
-        lambda k: jnp.concatenate([k0[k], k1[k]], axis=0)[:, : cot.shape[1]],
-        ext,
-        positions,
-    )
-    order = relative_order(place, rows, act.shape[1], False)
+def fill_columns(columns, s_a, s_b, positions):
+    quarter = s_a.shape[1]
+    for k in range(TAPS):
+        at = EXT + 2 * (k - 2)
+        for i, s in enumerate((s_a, s_b)):
+            lane = (2 * k + i) * quarter
+            columns[:, lane : lane + quarter] = s[at : at + positions, :]
+
+
+def spread(grad, slope, doubled, back, base, out):
+    positions = grad.shape[0]
+    blocks, _, lanes = doubled.shape
+    for j in range(blocks):
+        g = grad[:, j * lanes : (j + 1) * lanes]
+        doubled[j, pl.ds(0, positions, 2), :] = g
+        doubled[j, pl.ds(1, positions, 2), :] = g
     block = 256
-    for at in range(0, act.shape[0], block):
-        v = jnp.dot(act[at : at + block, :], order, preferred_element_type=F32)
-        slope[at : at + block, :] = 0.5 * gelu_slope(v)
-
-
-def second_kernel(
-    rows, place, s2, s3, k2, k3, cot, low, high, acc1, grad1, slope, pooled, out, ext, doubled
-):
-    positions = cot.shape[0]
-    channels = out.shape[1]
+    for at in range(0, 2 * positions, block):
+        rows = slice(at, at + block)
+        mixed = jnp.concatenate(
+            [
+                (doubled[j, rows, :] * slope(rows, j * lanes, (j + 1) * lanes)).astype(BF16)
+                for j in range(blocks)
+            ],
+            axis=1,
+        )
+        put = jnp.dot(mixed, back, preferred_element_type=F32)
+        if base is not None:
+            put = put + base[rows, :].astype(F32)
+        out[rows, :] = put.astype(BF16)
+
+
+def first_kernel(rows, place, s0, s1, s2, s3, k0, k1, cot, low, high, act, *refs):
+    acc, part, slope, back, later, shifted, ext, columns, doubled = refs
+    positions, width = cot.shape
+    window, channels = act.shape
     half = channels // 2
     fill_ext(ext, cot, low, high)
-    acc, grad = pair_products(
-        lambda at: jnp.concatenate([s2[at : at + positions], s3[at : at + positions]], axis=1),
-        lambda k: jnp.concatenate([k2[k], k3[k]], axis=0)[:, : cot.shape[1]],
-        ext,
-        positions,
-    )
-    pooled[...] = (acc + acc1[...]).T.astype(BF16)
-    lanes = doubled.shape[2]
-    for j in range(channels // lanes):
-        g = grad1[:, j * lanes : (j + 1) * lanes] if j * lanes < half else grad[:, j * lanes - half : (j + 1) * lanes - half]
-        doubled[j, pl.ds(0, positions, 2), :] = g
-        doubled[j, pl.ds(1, positions, 2), :] = g
-    back = relative_order(place, rows, channels, True)
-    block = 256
-    for at in range(0, 2 * positions, block):
-        pieces = [
-            (doubled[j, at : at + block, :] * slope[at : at + block, j * lanes : (j + 1) * lanes]).astype(BF16)
-            for j in range(channels // lanes)
-        ]
-        mixed = jnp.concatenate(pieces, axis=1)
-        out[at : at + block, :] = jnp.dot(mixed, back, preferred_element_type=F32).astype(BF16)
+    for k in range(TAPS):
+        at = HALO - 2 * (k - 2)
+        shifted[k] = ext[at : at + positions, :]
+    fill_columns(columns, s0, s1, positions)
+    fill_columns(later, s2, s3, positions)
+    order = relative_order(place, rows, channels, True)
+    back[...] = order[half:, :]
+    acc[...], grad = products(columns[...], shifted, taps_of(k0, k1, width))
+
+    def slope_of(rows, start, stop):
+        v = lax.dot_general(
+            act[rows, :], order[start:stop, :], (((1,), (1,)), ((), ())), preferred_element_type=F32
+        )
+        return 0.5 * gelu_slope(v)
+
+    spread(grad, slope_of, doubled, order[:half, :], None, part)
+    for at in range(0, window, 256):
+        slope[at : at + 256, :] = slope_of(slice(at, at + 256), half, channels)
+
+
+def second_kernel(k2, k3, columns, shifted, acc1, part, slope, back, pooled, out, doubled):
+    acc, grad = products(columns[...], shifted, taps_of(k2, k3, shifted.shape[2]))
+    pooled[...] = (acc + acc1[...]).astype(BF16).T
+    spread(grad, lambda rows, i, j: slope[rows, i:j], doubled, back[...], part, out)
 
 
 def after(x, *first):
@@ -259,36 +273,43 @@
     k1 = flip(k0, 1)
 
     low_cot, high_cot = low[:, channels:], high[:, channels:]
-    acc, grad, slope = pl.pallas_call(
+    half = channels // 2
+    doubled = pltpu.VMEM((half // 128, window, 128), F32)
+    acc, part, *handed = pl.pallas_call(
         functools.partial(first_kernel, rows),
         out_shape=[
             jax.ShapeDtypeStruct((positions, width), F32),
-            jax.ShapeDtypeStruct((positions, channels // 2), F32),
-            jax.ShapeDtypeStruct((window, channels), F32),
+            jax.ShapeDtypeStruct((window, channels), BF16),
+            jax.ShapeDtypeStruct((window, half), F32),
+            jax.ShapeDtypeStruct((half, channels), BF16),
+            jax.ShapeDtypeStruct((positions, TAPS * half), BF16),
+            jax.ShapeDtypeStruct((TAPS, positions, width), BF16),
         ],
-        in_specs=[SMEM] + [VMEM] * 8,
-        out_specs=[VMEM] * 3,
-        scratch_shapes=[pltpu.VMEM((positions + 2 * HALO, width), BF16)],
-        compiler_params=params(48),
+        in_specs=[SMEM] + [VMEM] * 10,
+        out_specs=[VMEM] * 6,
+        scratch_shapes=[
+            pltpu.VMEM((positions + 2 * HALO, width), BF16),
+            pltpu.VMEM((positions, TAPS * half), BF16),
+            doubled,
+        ],
+        compiler_params=params(40),
         name="first",
-    )(place, pieces[0], pieces[1], k0, k1, cotangent, low_cot, high_cot, activations)
+    )(place, *pieces, k0, k1, cotangent, low_cot, high_cot, activations)
+    slope, back, columns, shifted = handed
     k2 = after(k2, acc, terms)
     k3 = flip(k2, 1)
     pooled_t, input_grad = pl.pallas_call(
-        functools.partial(second_kernel, rows),
+        second_kernel,
         out_shape=[
             jax.ShapeDtypeStruct((width, positions), BF16),
             jax.ShapeDtypeStruct((window, channels), BF16),
         ],
-        in_specs=[SMEM] + [VMEM] * 10,
+        in_specs=[VMEM] * 8,
         out_specs=[VMEM] * 2,
-        scratch_shapes=[
-            pltpu.VMEM((positions + 2 * HALO, width), BF16),
-            pltpu.VMEM((channels // 128, window, 128), F32),
-        ],
-        compiler_params=params(48),
+        scratch_shapes=[doubled],
+        compiler_params=params(40),
         name="second",
-    )(place, pieces[2], pieces[3], k2, k3, cotangent, low_cot, high_cot, acc, grad, slope)
+    )(k2, k3, columns, shifted, acc, part, slope, back)
     total = grads[0]
     for term in terms:
         total = total + term.astype(F32)

time: 65.4 us -> 62.4 us (0.954)
  Pallas kernels: 15.4 us -> 13.6 us
  waiting for transfers between devices: 26.4 us -> 25.3 us
    pallas_call x1, Pallas kernels: 6.56 us -> 3.67 us  [on_device(): pl.pallas_call(second_kernel, out_shape=[jax.ShapeDtypeStruct((width, pos...]
    pallas_call x1, Pallas kernels: 4.75 us -> 5.86 us  [on_device(): pl.pallas_call(functools.partial(first_kernel, rows), out_shape=[jax.Shap...]
    ppermute x15, waiting for transfers between devices: 18.7 us -> 17.6 us  [flip(): return lax.ppermute(x, 'pos', [(i, i ^ bit) for i in range(n)])]
  transfers between devices with their start and end apart: 17 -> 17, of which waited for: 8 -> 8; matrix products, arithmetic and copies ran while one was open for 6% -> 7% of each run, Pallas kernels for 14% -> 16%
where the time goes in v4:
time: 62.4 us; the launch traced here: 62.1 us
  waiting for transfers between devices  25.3 us (41%)
  starting transfers between devices  18.2 us (29%)
  Pallas kernels  13.6 us (22%)
  local copies, waits for them, and re-layouts  2.26 us (4%)
  other arithmetic  1.95 us (3%)
  between operations  0.8 us (1%)
    ppermute x15, waiting for transfers between devices, flip(): return lax.ppermute(x, 'pos', [(i, i ^ bit) for i in range(n)])  17.6 us
    ppermute x15, starting transfers between devices, flip(): return lax.ppermute(x, 'pos', [(i, i ^ bit) for i in range(n)])  12.7 us
    pallas_call x1, Pallas kernels, on_device(): pl.pallas_call(functools.partial(first_kernel, rows), out_shape=[jax.Shap...  5.86 us
    ppermute x1, waiting for transfers between devices, on_device(): low = lax.ppermute(edge_low, 'pos', [(i, i + 1) for i in range(n - 1)])  5.73 us
    pallas_call x1, Pallas kernels, on_device(): pl.pallas_call(second_kernel, out_shape=[jax.ShapeDtypeStruct((width, pos...  3.67 us
    ppermute x1, starting transfers between devices, on_device(): low = lax.ppermute(edge_low, 'pos', [(i, i + 1) for i in range(n - 1)])  3.53 us
    pallas_call x1, Pallas kernels, on_device(): pl.pallas_call(functools.partial(wgrad_kernel, rows), out_shape=grad_shap...  2.25 us
    ppermute x1, waiting for transfers between devices, on_device(): high = lax.ppermute(edge_high, 'pos', [(i + 1, i) for i in range(n - 1)])  2.03 us
  transfers between devices with their start and end apart: 17, of which 8 were waited for; matrix products, arithmetic and copies ran while one was open for 7% of the time, Pallas kernels for 16%

profile of v4, /device:TPU:9, one launch (start us, length us, event | category | flops | bytes accessed | tf_op | source)
XLA Modules:
  0.0 62.1 jit_solution(10220817097194869098)
XLA Ops:
  0.7 2.4 %collective-permute-start = (bf16[5,32,608]{2,1,0:T(8,128)(2,1)}, bf16[5,32,608]{2,1,0:T(8,128)(2,1)S(1)}, u32[]{:S(2)}, u32[]{:S(2)}) collective-permute-start(bf16[5,32,608]{2,1,0:T(8,128)(2,1)} %bitcast.10), channel_id=1, source_target_pairs={{0,8},{1,9},{2,10},{3,11},{4,12},{5,13},{6,14},{7,15},{8,0},{9,1},... | collective-permute-start | bytes 583688 | tf_op jit(solution)/shard_map/ppermute | solution.py:203
  3.2 1.2 %collective-permute-start.6 = (bf16[608,512]{1,0:T(8,128)(2,1)}, bf16[608,512]{1,0:T(8,128)(2,1)S(1)}, u32[]{:S(2)}, u32[]{:S(2)}) collective-permute-start(bf16[608,512]{1,0:T(8,128)(2,1)} %bitcast.7), channel_id=1, source_target_pairs={{0,2},{1,3},{2,0},{3,1},{4,6},{5,7},{6,4},{7,5},{8,10},{9,11},{10,... | collective-permute-start | bytes 1867784 | tf_op jit(solution)/shard_map/ppermute | solution.py:203
  4.4 1.4 %copy.6.cot = bf16[512,608]{1,0:T(8,128)(2,1)S(1)} copy(bf16[512,608]{0,1:T(8,128)(2,1)} %param.5) | data formatting | bytes 1245184 | tf_op args[2]
  6.6 3.5 %collective-permute-start.3 = (bf16[16,1120]{1,0:T(8,128)(2,1)S(1)}, bf16[16,1120]{1,0:T(8,128)(2,1)S(1)}, u32[]{:S(2)}, u32[]{:S(2)}) collective-permute-start(bf16[16,1120]{1,0:T(8,128)(2,1)S(1)} %pad_maximum_fusion.1), channel_id=1, source_target_pairs={{0,1},{1,2},{2,3},{3,4},{4,5},{5,6},{6,7},{7,8},{8,9},{9,10},{10,1... | collective-permute-start | bytes 107528 | tf_op jit(solution)/shard_map/ppermute | solution.py:230
  10.2 1.9 %collective-permute-start.4 = (bf16[16,1120]{1,0:T(8,128)(2,1)S(1)}, bf16[16,1120]{1,0:T(8,128)(2,1)S(1)}, u32[]{:S(2)}, u32[]{:S(2)}) collective-permute-start(bf16[16,1120]{1,0:T(8,128)(2,1)S(1)} %pad_maximum_fusion.2), channel_id=1, source_target_pairs={{1,0},{2,1},{3,2},{4,3},{5,4},{6,5},{7,6},{8,7},{9,8},{10,9},{11,1... | collective-permute-start | bytes 107528 | tf_op jit(solution)/shard_map/ppermute | solution.py:231
  12.2 5.7 %collective-permute-done.3 = bf16[16,1120]{1,0:T(8,128)(2,1)S(1)} collective-permute-done((bf16[16,1120]{1,0:T(8,128)(2,1)S(1)}, bf16[16,1120]{1,0:T(8,128)(2,1)S(1)}, u32[]{:S(2)}, u32[]{:S(2)}) %collective-permute-start.3) | collective-permute-done | bytes 35872 | tf_op jit(solution)/shard_map/ppermute | solution.py:230
  17.9 2.0 %collective-permute-done.4 = bf16[16,1120]{1,0:T(8,128)(2,1)S(1)} collective-permute-done((bf16[16,1120]{1,0:T(8,128)(2,1)S(1)}, bf16[16,1120]{1,0:T(8,128)(2,1)S(1)}, u32[]{:S(2)}, u32[]{:S(2)}) %collective-permute-start.4) | collective-permute-done | bytes 35872 | tf_op jit(solution)/shard_map/ppermute | solution.py:231
  20.0 1.8 %pool.1 = (bf16[528,128]{1,0:T(8,128)(2,1)S(1)}, bf16[528,128]{1,0:T(8,128)(2,1)S(1)}, bf16[528,128]{1,0:T(8,128)(2,1)S(1)}, bf16[528,128]{1,0:T(8,128)(2,1)S(1)}) custom-call(s32[2]{0:T(128)S(1)} %pad_add_fusion.place, bf16[1024,512]{1,0:T(8,128)(2,1)S(1)} %copy-done, bf16[16,512]{1,0:T(8,128)(2,1)S(1)} %slice.33.low, bf16[16,512]{1,0:T(8,128)(2,1)S(1)} %slice.35.high), custom_call_target="tpu_custom_call" | custom-call | tf_op jit(solution)/shard_map/pool/pallas_call | solution.py:235
  22.3 0.8 %collective-permute-done.5.s1 = bf16[528,128]{1,0:T(8,128)(2,1)S(1)} collective-permute-done((bf16[528,128]{1,0:T(8,128)(2,1)S(1)}, bf16[528,128]{1,0:T(8,128)(2,1)S(1)}, u32[]{:S(2)}, u32[]{:S(2)}) %collective-permute-start.5) | collective-permute-done | bytes 135200 | tf_op jit(solution)/shard_map/ppermute | solution.py:203
  23.3 0.9 %collective-permute-start.2 = (bf16[5,32,608]{2,1,0:T(8,128)(2,1)S(1)}, bf16[5,32,608]{2,1,0:T(8,128)(2,1)S(1)}, u32[]{:S(2)}, u32[]{:S(2)}) collective-permute-start(bf16[5,32,608]{2,1,0:T(8,128)(2,1)S(1)} %collective-permute-done), channel_id=1, source_target_pairs={{0,4},{1,5},{2,6},{3,7},{4,0},{5,1},{6,2},{7,3},{8,12},{9,13},{10,... | collective-permute-start | bytes 583688 | tf_op jit(solution)/shard_map/ppermute | solution.py:203
  25.1 1.4 %collective-permute-start.8 = (bf16[528,128]{1,0:T(8,128)(2,1)S(1)}, bf16[528,128]{1,0:T(8,128)(2,1)S(1)}, u32[]{:S(2)}, u32[]{:S(2)}) collective-permute-start(bf16[528,128]{1,0:T(8,128)(2,1)S(1)} %get-tuple-element.31.s3), channel_id=1, source_target_pairs={{0,3},{1,2},{2,1},{3,0},{4,7},{5,6},{6,5},{7,4},{8,11},{9,10},{10,... | collective-permute-start | bytes 405512 | tf_op jit(solution)/shard_map/ppermute | solution.py:203
  26.5 3.1 %collective-permute-done.2 = bf16[5,32,608]{2,1,0:T(8,128)(2,1)S(1)} collective-permute-done((bf16[5,32,608]{2,1,0:T(8,128)(2,1)S(1)}, bf16[5,32,608]{2,1,0:T(8,128)(2,1)S(1)}, u32[]{:S(2)}, u32[]{:S(2)}) %collective-permute-start.2) | collective-permute-done | bytes 194592 | tf_op jit(solution)/shard_map/ppermute | solution.py:203
  29.6 1.0 %pad_maximum_fusion = bf16[5,128,608]{2,1,0:T(8,128)(2,1)S(1)} fusion(bf16[5,32,608]{2,1,0:T(8,128)(2,1)S(1)} %collective-permute-done.2, bf16[5,32,608]{2,1,0:T(8,128)(2,1)} %collective-permute-done.1, bf16[5,32,608]{2,1,0:T(8,128)(2,1)S(1)} %collective-permute-done, bf16[5,32,608]{2,1,0:T(8,128)(2,1)S(1)} %bitcast.12), kind=kLoop, calls=%fused_computation | loop fusion | flops 3112960 | bytes 1556480 | tf_op jit(solution)/shard_map/concatenate | solution.py:226
  30.7 1.8 %collective-permute-done.8.s3 = bf16[528,128]{1,0:T(8,128)(2,1)S(1)} collective-permute-done((bf16[528,128]{1,0:T(8,128)(2,1)S(1)}, bf16[528,128]{1,0:T(8,128)(2,1)S(1)}, u32[]{:S(2)}, u32[]{:S(2)}) %collective-permute-start.8) | collective-permute-done | bytes 135200 | tf_op jit(solution)/shard_map/ppermute | solution.py:203
  32.6 0.9 %collective-permute-start.11 = (bf16[5,128,640]{2,1,0:T(8,128)(2,1)S(1)}, bf16[5,128,640]{2,1,0:T(8,128)(2,1)S(1)}, u32[]{:S(2)}, u32[]{:S(2)}) collective-permute-start(bf16[5,128,640]{2,1,0:T(8,128)(2,1)S(1)} %pad.4.k0), channel_id=1, source_target_pairs={{0,2},{1,3},{2,0},{3,1},{4,6},{5,7},{6,4},{7,5},{8,10},{9,11},{10,... | collective-permute-start | bytes 2457608 | tf_op jit(solution)/shard_map/ppermute | solution.py:203
  33.5 2.3 %wgrad.1 = (f32[5,32,608]{2,1,0:T(8,128)S(1)}, bf16[5,32,608]{2,1,0:T(8,128)(2,1)S(1)}, bf16[5,32,608]{2,1,0:T(8,128)(2,1)S(1)}, bf16[5,32,608]{2,1,0:T(8,128)(2,1)S(1)}) custom-call(bf16[528,128]{1,0:T(8,128)(2,1)S(1)} %get-tuple-element.26.s0, bf16[528,128]{1,0:T(8,128)(2,1)S(1)} %collective-permute-done.5.s1, ...), custom_call_target="tpu_custom_call" | custom-call | tf_op jit(solution)/shard_map/wgrad/pallas_call | solution.py:256
  36.2 2.3 %collective-permute-start.15 = (bf16[5,32,608]{2,1,0:T(8,128)(2,1)S(1)}, bf16[5,32,608]{2,1,0:T(8,128)(2,1)S(1)}, u32[]{:S(2)}, u32[]{:S(2)}) collective-permute-start(bf16[5,32,608]{2,1,0:T(8,128)(2,1)S(1)} %get-tuple-element.37), channel_id=1, source_target_pairs={{0,12},{1,13},{2,14},{3,15},{4,8},{5,9},{6,10},{7,11},{8,4},{9,5},... | collective-permute-start | bytes 583688 | tf_op jit(solution)/shard_map/ppermute | solution.py:203
  38.5 5.9 %first.1 = (f32[512,608]{1,0:T(8,128)S(1)}, bf16[1024,512]{1,0:T(8,128)(2,1)S(1)}, f32[1024,256]{1,0:T(8,128)S(1)}, bf16[256,512]{1,0:T(8,128)(2,1)S(1)}, bf16[5...) custom-call(s32[2]{0:T(128)S(1)} %pad_add_fusion.place, bf16[528,128]{1,0:T(8,128)(2,1)S(1)} %get-tuple-element.26.s0, ...), custom_call_target="tpu_custom_call" | custom-call | tf_op jit(solution)/shard_map/first/pallas_call | solution.py:278
  44.3 1.1 %collective-permute-done.13 = bf16[5,32,608]{2,1,0:T(8,128)(2,1)S(1)} collective-permute-done((bf16[5,32,608]{2,1,0:T(8,128)(2,1)S(1)}, bf16[5,32,608]{2,1,0:T(8,128)(2,1)S(1)}, u32[]{:S(2)}, u32[]{:S(2)}) %collective-permute-start.13) | collective-permute-done | bytes 194592 | tf_op jit(solution)/shard_map/ppermute | solution.py:203
  45.4 9.6 %collective-permute-done.15 = bf16[5,32,608]{2,1,0:T(8,128)(2,1)S(1)} collective-permute-done((bf16[5,32,608]{2,1,0:T(8,128)(2,1)S(1)}, bf16[5,32,608]{2,1,0:T(8,128)(2,1)S(1)}, u32[]{:S(2)}, u32[]{:S(2)}) %collective-permute-start.15) | collective-permute-done | bytes 194592 | tf_op jit(solution)/shard_map/ppermute | solution.py:203
  55.0 1.4 %collective-permute-start.16 = (bf16[5,128,640]{2,1,0:T(8,128)(2,1)S(1)}, bf16[5,128,640]{2,1,0:T(8,128)(2,1)S(1)}, u32[]{:S(2)}, u32[]{:S(2)}) collective-permute-start(bf16[5,128,640]{2,1,0:T(8,128)(2,1)S(1)} %collective-permute-done.11.k2), channel_id=1, source_target_pairs={{0,1},{1,0},{2,3},{3,2},{4,5},{5,4},{6,7},{7,6},{8,9},{9,8},{10,11... | collective-permute-start | bytes 2457608 | tf_op jit(solution)/shard_map/ppermute | solution.py:203
  56.5 0.8 %add_bitcast_fusion = f32[32,5,608]{2,0,1:T(8,128)} fusion(bf16[5,32,608]{2,1,0:T(8,128)(2,1)S(1)} %collective-permute-done.15, bf16[5,32,608]{2,1,0:T(8,128)(2,1)S(1)} %collective-permute-done.14, f32[5,32,608]{2,1,0:T(8,128)S(1)} %get-tuple-element.46, bf16[5,32,608]{2,1,0:T(8,128)(2,1)S(1)} %collective-permute-done.13), kind=kLoop, calls=%fused_computation.1 | loop fusion | flops 583680 | bytes 1361920 | tf_op jit(solution)/shard_map/transpose | solution.py:316
  57.3 1.1 %collective-permute-done.16.k3 = bf16[5,128,640]{2,1,0:T(8,128)(2,1)S(1)} collective-permute-done((bf16[5,128,640]{2,1,0:T(8,128)(2,1)S(1)}, bf16[5,128,640]{2,1,0:T(8,128)(2,1)S(1)}, u32[]{:S(2)}, u32[]{:S(2)}) %collective-permute-start.16) | collective-permute-done | bytes 819232 | tf_op jit(solution)/shard_map/ppermute | solution.py:203
  58.4 3.7 %second.1 = (bf16[608,512]{1,0:T(8,128)(2,1)}, bf16[1024,512]{1,0:T(8,128)(2,1)}) custom-call(bf16[5,128,640]{2,1,0:T(8,128)(2,1)S(1)} %collective-permute-done.11.k2, bf16[5,128,640]{2,1,0:T(8,128)(2,1)S(1)} %collective-permute-done.16.k3, bf16[512,1280]{1,0:T(8,128)(2,1)S(1)} %get-tuple-element.39.columns, ...), custom_call_target="tpu_custom_call" | custom-call | tf_op jit(solution)/shard_map/second/pallas_call | solution.py:301
  (33 shorter events, 3.1 us)
Async XLA Ops:
  0.6 21.2 %copy-start.1 = (bf16[512,608]{0,1:T(8,128)(2,1)S(1)}, bf16[512,608]{0,1:T(8,128)(2,1)}, u32[]{:S(2)}) copy-start(bf16[512,608]{0,1:T(8,128)(2,1)} %param.5) | copy-start | bytes 1867780
  0.6 19.3 %copy-start = (bf16[1024,512]{1,0:T(8,128)(2,1)S(1)}, bf16[1024,512]{1,0:T(8,128)(2,1)}, u32[]{:S(2)}) copy-start(bf16[1024,512]{1,0:T(8,128)(2,1)} %act.2) | copy-start | bytes 3145732
  0.7 29.0 %copy-start.2 = (bf16[32,5,608]{2,0,1:T(8,128)(2,1)S(1)}, bf16[32,5,608]{2,0,1:T(8,128)(2,1)}, u32[]{:S(2)}) copy-start(bf16[32,5,608]{2,0,1:T(8,128)(2,1)} %param.4) | copy-start | bytes 583684
  0.7 19.3 %collective-permute-start = (bf16[5,32,608]{2,1,0:T(8,128)(2,1)}, bf16[5,32,608]{2,1,0:T(8,128)(2,1)S(1)}, u32[]{:S(2)}, u32[]{:S(2)}) collective-permute-start(bf16[5,32,608]{2,1,0:T(8,128)(2,1)} %bitcast.10), channel_id=1, source_target_pairs={{0,8},{1,9},{2,10},{3,11},{4,12},{5,13},{6,14},{7,15},{8,0},{9,1},... | collective-permute-start | bytes 583688 | tf_op jit(solution)/shard_map/ppermute | solution.py:203
  3.0 16.9 %collective-permute-start.1 = (bf16[5,32,608]{2,1,0:T(8,128)(2,1)}, bf16[5,32,608]{2,1,0:T(8,128)(2,1)}, u32[]{:S(2)}, u32[]{:S(2)}) collective-permute-start(bf16[5,32,608]{2,1,0:T(8,128)(2,1)} %bitcast.11), channel_id=1, source_target_pairs={{0,4},{1,5},{2,6},{3,7},{4,0},{5,1},{6,2},{7,3},{8,12},{9,13},{10,... | collective-permute-start | bytes 583688 | tf_op jit(solution)/shard_map/ppermute | solution.py:203
  3.2 20.0 %collective-permute-start.6 = (bf16[608,512]{1,0:T(8,128)(2,1)}, bf16[608,512]{1,0:T(8,128)(2,1)S(1)}, u32[]{:S(2)}, u32[]{:S(2)}) collective-permute-start(bf16[608,512]{1,0:T(8,128)(2,1)} %bitcast.7), channel_id=1, source_target_pairs={{0,2},{1,3},{2,0},{3,1},{4,6},{5,7},{6,4},{7,5},{8,10},{9,11},{10,... | collective-permute-start | bytes 1867784 | tf_op jit(solution)/shard_map/ppermute | solution.py:203
  6.6 11.3 %collective-permute-start.3 = (bf16[16,1120]{1,0:T(8,128)(2,1)S(1)}, bf16[16,1120]{1,0:T(8,128)(2,1)S(1)}, u32[]{:S(2)}, u32[]{:S(2)}) collective-permute-start(bf16[16,1120]{1,0:T(8,128)(2,1)S(1)} %pad_maximum_fusion.1), channel_id=1, source_target_pairs={{0,1},{1,2},{2,3},{3,4},{4,5},{5,6},{6,7},{7,8},{8,9},{9,10},{10,1... | collective-permute-start | bytes 107528 | tf_op jit(solution)/shard_map/ppermute | solution.py:230
  10.2 9.8 %collective-permute-start.4 = (bf16[16,1120]{1,0:T(8,128)(2,1)S(1)}, bf16[16,1120]{1,0:T(8,128)(2,1)S(1)}, u32[]{:S(2)}, u32[]{:S(2)}) collective-permute-start(bf16[16,1120]{1,0:T(8,128)(2,1)S(1)} %pad_maximum_fusion.2), channel_id=1, source_target_pairs={{1,0},{2,1},{3,2},{4,3},{5,4},{6,5},{7,6},{8,7},{9,8},{10,9},{11,1... | collective-permute-start | bytes 107528 | tf_op jit(solution)/shard_map/ppermute | solution.py:231
  21.8 1.4 %collective-permute-start.5 = (bf16[528,128]{1,0:T(8,128)(2,1)S(1)}, bf16[528,128]{1,0:T(8,128)(2,1)S(1)}, u32[]{:S(2)}, u32[]{:S(2)}) collective-permute-start(bf16[528,128]{1,0:T(8,128)(2,1)S(1)} %get-tuple-element.27.s1), channel_id=1, source_target_pairs={{0,1},{1,0},{2,3},{3,2},{4,5},{5,4},{6,7},{7,6},{8,9},{9,8},{10,11... | collective-permute-start | bytes 405512 | tf_op jit(solution)/shard_map/ppermute | solution.py:203
  21.8 8.8 %collective-permute-start.9 = (bf16[608,512]{1,0:T(8,128)(2,1)S(1)}, bf16[608,512]{1,0:T(8,128)(2,1)S(1)}, u32[]{:S(2)}, u32[]{:S(2)}) collective-permute-start(bf16[608,512]{1,0:T(8,128)(2,1)S(1)} %bitcast.8), channel_id=1, source_target_pairs={{0,1},{1,0},{2,3},{3,2},{4,5},{5,4},{6,7},{7,6},{8,9},{9,8},{10,11... | collective-permute-start | bytes 1867784 | tf_op jit(solution)/shard_map/ppermute | solution.py:203
  23.2 9.3 %collective-permute-start.10 = (bf16[608,512]{1,0:T(8,128)(2,1)S(1)}, bf16[608,512]{1,0:T(8,128)(2,1)S(1)}, u32[]{:S(2)}, u32[]{:S(2)}) collective-permute-start(bf16[608,512]{1,0:T(8,128)(2,1)S(1)} %collective-permute-done.6.c2), channel_id=1, source_target_pairs={{0,1},{1,0},{2,3},{3,2},{4,5},{5,4},{6,7},{7,6},{8,9},{9,8},{10,11... | collective-permute-start | bytes 1867784 | tf_op jit(solution)/shard_map/ppermute | solution.py:203
  23.3 6.3 %collective-permute-start.2 = (bf16[5,32,608]{2,1,0:T(8,128)(2,1)S(1)}, bf16[5,32,608]{2,1,0:T(8,128)(2,1)S(1)}, u32[]{:S(2)}, u32[]{:S(2)}) collective-permute-start(bf16[5,32,608]{2,1,0:T(8,128)(2,1)S(1)} %collective-permute-done), channel_id=1, source_target_pairs={{0,4},{1,5},{2,6},{3,7},{4,0},{5,1},{6,2},{7,3},{8,12},{9,13},{10,... | collective-permute-start | bytes 583688 | tf_op jit(solution)/shard_map/ppermute | solution.py:203
  24.2 6.4 %collective-permute-start.7 = (bf16[528,128]{1,0:T(8,128)(2,1)S(1)}, bf16[528,128]{1,0:T(8,128)(2,1)S(1)}, u32[]{:S(2)}, u32[]{:S(2)}) collective-permute-start(bf16[528,128]{1,0:T(8,128)(2,1)S(1)} %get-tuple-element.30.s2), channel_id=1, source_target_pairs={{0,2},{1,3},{2,0},{3,1},{4,6},{5,7},{6,4},{7,5},{8,10},{9,11},{10,... | collective-permute-start | bytes 405512 | tf_op jit(solution)/shard_map/ppermute | solution.py:203
  25.1 7.4 %collective-permute-start.8 = (bf16[528,128]{1,0:T(8,128)(2,1)S(1)}, bf16[528,128]{1,0:T(8,128)(2,1)S(1)}, u32[]{:S(2)}, u32[]{:S(2)}) collective-permute-start(bf16[528,128]{1,0:T(8,128)(2,1)S(1)} %get-tuple-element.31.s3), channel_id=1, source_target_pairs={{0,3},{1,2},{2,1},{3,0},{4,7},{5,6},{6,5},{7,4},{8,11},{9,10},{10,... | collective-permute-start | bytes 405512 | tf_op jit(solution)/shard_map/ppermute | solution.py:203
  32.5 6.0 %collective-permute-start.12 = (bf16[5,128,640]{2,1,0:T(8,128)(2,1)S(1)}, bf16[5,128,640]{2,1,0:T(8,128)(2,1)S(1)}, u32[]{:S(2)}, u32[]{:S(2)}) collective-permute-start(bf16[5,128,640]{2,1,0:T(8,128)(2,1)S(1)} %pad.4.k0), channel_id=1, source_target_pairs={{0,1},{1,0},{2,3},{3,2},{4,5},{5,4},{6,7},{7,6},{8,9},{9,8},{10,11... | collective-permute-start | bytes 2457608 | tf_op jit(solution)/shard_map/ppermute | solution.py:203
  32.6 22.4 %collective-permute-start.11 = (bf16[5,128,640]{2,1,0:T(8,128)(2,1)S(1)}, bf16[5,128,640]{2,1,0:T(8,128)(2,1)S(1)}, u32[]{:S(2)}, u32[]{:S(2)}) collective-permute-start(bf16[5,128,640]{2,1,0:T(8,128)(2,1)S(1)} %pad.4.k0), channel_id=1, source_target_pairs={{0,2},{1,3},{2,0},{3,1},{4,6},{5,7},{6,4},{7,5},{8,10},{9,11},{10,... | collective-permute-start | bytes 2457608 | tf_op jit(solution)/shard_map/ppermute | solution.py:203
  35.8 9.7 %collective-permute-start.13 = (bf16[5,32,608]{2,1,0:T(8,128)(2,1)S(1)}, bf16[5,32,608]{2,1,0:T(8,128)(2,1)S(1)}, u32[]{:S(2)}, u32[]{:S(2)}) collective-permute-start(bf16[5,32,608]{2,1,0:T(8,128)(2,1)S(1)} %get-tuple-element.35), channel_id=1, source_target_pairs={{0,8},{1,9},{2,10},{3,11},{4,12},{5,13},{6,14},{7,15},{8,0},{9,1},... | collective-permute-start | bytes 583688 | tf_op jit(solution)/shard_map/ppermute | solution.py:203
  35.9 9.5 %collective-permute-start.14 = (bf16[5,32,608]{2,1,0:T(8,128)(2,1)S(1)}, bf16[5,32,608]{2,1,0:T(8,128)(2,1)S(1)}, u32[]{:S(2)}, u32[]{:S(2)}) collective-permute-start(bf16[5,32,608]{2,1,0:T(8,128)(2,1)S(1)} %get-tuple-element.36), channel_id=1, source_target_pairs={{0,4},{1,5},{2,6},{3,7},{4,0},{5,1},{6,2},{7,3},{8,12},{9,13},{10,... | collective-permute-start | bytes 583688 | tf_op jit(solution)/shard_map/ppermute | solution.py:203
  36.2 18.8 %collective-permute-start.15 = (bf16[5,32,608]{2,1,0:T(8,128)(2,1)S(1)}, bf16[5,32,608]{2,1,0:T(8,128)(2,1)S(1)}, u32[]{:S(2)}, u32[]{:S(2)}) collective-permute-start(bf16[5,32,608]{2,1,0:T(8,128)(2,1)S(1)} %get-tuple-element.37), channel_id=1, source_target_pairs={{0,12},{1,13},{2,14},{3,15},{4,8},{5,9},{6,10},{7,11},{8,4},{9,5},... | collective-permute-start | bytes 583688 | tf_op jit(solution)/shard_map/ppermute | solution.py:203
  55.0 3.4 %collective-permute-start.16 = (bf16[5,128,640]{2,1,0:T(8,128)(2,1)S(1)}, bf16[5,128,640]{2,1,0:T(8,128)(2,1)S(1)}, u32[]{:S(2)}, u32[]{:S(2)}) collective-permute-start(bf16[5,128,640]{2,1,0:T(8,128)(2,1)S(1)} %collective-permute-done.11.k2), channel_id=1, source_target_pairs={{0,1},{1,0},{2,3},{3,2},{4,5},{5,4},{6,7},{7,6},{8,9},{9,8},{10,11... | collective-permute-start | bytes 2457608 | tf_op jit(solution)/shard_map/ppermute | solution.py:203

commit v5 on v4

--- a/solution.py
+++ b/solution.py
@@ -84,12 +84,11 @@
     put(window // 2, pooled(jnp.concatenate([g_prev, gelu(high[...])], axis=0)))
 
 
-def wgrad_kernel(rows, s0, s1, s2, s3, c0, c1, c2, c3, *refs):
-    *outs, left = refs
-    positions = c0.shape[1]
-    quarter = s0.shape[1]
-    total = None
-    for s, c in ((s0, c0), (s1, c1), (s2, c2), (s3, c3)):
+def team_sums(left, pairs, start):
+    total = start
+    for s, c in pairs:
+        positions = c.shape[1]
+        quarter = s.shape[1]
         for k in range(TAPS):
             at = EXT + 2 * (k - 2)
             left[k * quarter : (k + 1) * quarter, :] = s[at : at + positions, :].T
@@ -97,6 +96,17 @@
             left[...], c[...], (((1,), (1,)), ((), ())), preferred_element_type=F32
         )
         total = term if total is None else total + term
+    return total
+
+
+def near_kernel(s0, s1, c0, c1, out, left):
+    out[...] = team_sums(left, ((s0, c0), (s1, c1)), None)
+
+
+def wgrad_kernel(rows, start, s2, s3, c2, c3, *refs):
+    *outs, left = refs
+    quarter = s2.shape[1]
+    total = team_sums(left, ((s2, c2), (s3, c3)), start[...])
     if len(outs) == 1:
         for k in range(TAPS):
             outs[0][k] = total[k * quarter : (k + 1) * quarter]
@@ -243,7 +253,7 @@
 
     far = after(pieces[2:], cot_y)
     mates = [pieces[0], flip(pieces[1], 1), flip(far[0], 2), flip(far[1], 3)]
-    cot_y = after(cot_y, mates[1])
+    cot_y = after(cot_y, pieces, blocks[-1])
     cot_yc = flip(cot_y, 1)
 
     split = rows % 16 == 0
@@ -253,21 +263,31 @@
         ]
     else:
         grad_shape = [jax.ShapeDtypeStruct((TAPS, quarter, width), F32)]
+    left = pltpu.VMEM((TAPS * quarter, positions), BF16)
+    start = pl.pallas_call(
+        near_kernel,
+        out_shape=jax.ShapeDtypeStruct((TAPS * quarter, width), F32),
+        in_specs=[VMEM] * 4,
+        out_specs=VMEM,
+        scratch_shapes=[left],
+        compiler_params=params(24),
+        name="near",
+    )(mates[0], mates[1], cot_t, cot_c)
     grads = pl.pallas_call(
         functools.partial(wgrad_kernel, rows),
         out_shape=grad_shape,
-        in_specs=[VMEM] * 8,
+        in_specs=[VMEM] * 5,
         out_specs=[VMEM] * len(grad_shape),
-        scratch_shapes=[pltpu.VMEM((TAPS * quarter, positions), BF16)],
+        scratch_shapes=[left],
         compiler_params=params(48),
         name="wgrad",
-    )(*mates, cot_t, cot_c, cot_y, cot_yc)
+    )(start, mates[2], mates[3], cot_y, cot_yc)
     if not split:
         parts = [grads[0][:, m * rows : (m + 1) * rows] for m in range(levels)]
         grads = parts[:1] + [p.astype(BF16) for p in parts[1:]]
     terms = [flip(g, TEAM * m) for g, m in zip(grads[1:], order[1:])]
 
-    k0 = after(k0, mates, cot_c, cot_yc)
+    k0 = after(k0, mates, cot_yc, start)
     k0 = jnp.pad(k0, ((0, 0), (0, 0), (0, -width % 128)))
     k2 = flip(k0, 2)
     k1 = flip(k0, 1)

time: 62.4 us -> 60.7 us (0.973)
  waiting for transfers between devices: 25.3 us -> 22.5 us
  starting transfers between devices: 18.2 us -> 18.9 us
    ppermute x1, waiting for transfers between devices: 5.73 us -> 1.3 us  [on_device(): low = lax.ppermute(edge_low, 'pos', [(i, i + 1) for i in range(n - 1)])]
    ppermute x1, starting transfers between devices: 1.92 us -> 3.47 us  [on_device(): high = lax.ppermute(edge_high, 'pos', [(i + 1, i) for i in range(n - 1)])]
    ppermute x15, waiting for transfers between devices: 17.6 us -> 18.8 us  [flip(): return lax.ppermute(x, 'pos', [(i, i ^ bit) for i in range(n)])]
    pallas_call x0 -> x1, Pallas kernels: none -> 1.22 us  [on_device(): pl.pallas_call(near_kernel, out_shape=jax.ShapeDtypeStruct((TAPS * quarte...]
    pallas_call x1, Pallas kernels: 2.25 us -> 1.22 us  [on_device(): pl.pallas_call(functools.partial(wgrad_kernel, rows), out_shape=grad_shap...]
    ppermute x15, starting transfers between devices: 12.7 us -> 11.9 us  [flip(): return lax.ppermute(x, 'pos', [(i, i ^ bit) for i in range(n)])]
  transfers between devices with their start and end apart: 17 -> 17, of which waited for: 8 -> 8; matrix products, arithmetic and copies ran while one was open for 7% -> 7% of each run, Pallas kernels for 16% -> 17%
where the time goes in v5:
time: 60.7 us; the launch traced here: 60.4 us
  waiting for transfers between devices  22.5 us (37%)
  starting transfers between devices  18.9 us (31%)
  Pallas kernels  13.8 us (23%)
  local copies, waits for them, and re-layouts  2.31 us (4%)
  other arithmetic  2.06 us (3%)
  between operations  0.81 us (1%)
    ppermute x15, waiting for transfers between devices, flip(): return lax.ppermute(x, 'pos', [(i, i ^ bit) for i in range(n)])  18.8 us
    ppermute x15, starting transfers between devices, flip(): return lax.ppermute(x, 'pos', [(i, i ^ bit) for i in range(n)])  11.9 us
    pallas_call x1, Pallas kernels, on_device(): pl.pallas_call(functools.partial(first_kernel, rows), out_shape=[jax.Shap...  5.85 us
    pallas_call x1, Pallas kernels, on_device(): pl.pallas_call(second_kernel, out_shape=[jax.ShapeDtypeStruct((width, pos...  3.67 us
    ppermute x1, starting transfers between devices, on_device(): low = lax.ppermute(edge_low, 'pos', [(i, i + 1) for i in range(n - 1)])  3.53 us
    ppermute x1, starting transfers between devices, on_device(): high = lax.ppermute(edge_high, 'pos', [(i + 1, i) for i in range(n - 1)])  3.47 us
    ppermute x1, waiting for transfers between devices, on_device(): high = lax.ppermute(edge_high, 'pos', [(i + 1, i) for i in range(n - 1)])  2.43 us
    pallas_call x1, Pallas kernels, on_device(): pl.pallas_call(functools.partial(pool_kernel, rows), out_shape=[jax.Shape...  1.82 us
  transfers between devices with their start and end apart: 17, of which 8 were waited for; matrix products, arithmetic and copies ran while one was open for 7% of the time, Pallas kernels for 17%

profile of v5, /device:TPU:9, one launch (start us, length us, event | category | flops | bytes accessed | tf_op | source)
XLA Modules:
  0.0 60.4 jit_solution(5782428810998654576)
XLA Ops:
  0.7 2.4 %collective-permute-start = (bf16[5,32,608]{2,1,0:T(8,128)(2,1)}, bf16[5,32,608]{2,1,0:T(8,128)(2,1)S(1)}, u32[]{:S(2)}, u32[]{:S(2)}) collective-permute-start(bf16[5,32,608]{2,1,0:T(8,128)(2,1)} %bitcast.10), channel_id=1, source_target_pairs={{0,8},{1,9},{2,10},{3,11},{4,12},{5,13},{6,14},{7,15},{8,0},{9,1},... | collective-permute-start | bytes 583688 | tf_op jit(solution)/shard_map/ppermute | solution.py:213
  3.2 1.2 %collective-permute-start.6 = (bf16[608,512]{1,0:T(8,128)(2,1)}, bf16[608,512]{1,0:T(8,128)(2,1)S(1)}, u32[]{:S(2)}, u32[]{:S(2)}) collective-permute-start(bf16[608,512]{1,0:T(8,128)(2,1)} %bitcast.7), channel_id=1, source_target_pairs={{0,2},{1,3},{2,0},{3,1},{4,6},{5,7},{6,4},{7,5},{8,10},{9,11},{10,... | collective-permute-start | bytes 1867784 | tf_op jit(solution)/shard_map/ppermute | solution.py:213
  4.4 1.4 %copy.6.cot = bf16[512,608]{1,0:T(8,128)(2,1)S(1)} copy(bf16[512,608]{0,1:T(8,128)(2,1)} %param.5) | data formatting | bytes 1245184 | tf_op args[2]
  6.7 3.5 %collective-permute-start.3 = (bf16[16,1120]{1,0:T(8,128)(2,1)S(1)}, bf16[16,1120]{1,0:T(8,128)(2,1)S(1)}, u32[]{:S(2)}, u32[]{:S(2)}) collective-permute-start(bf16[16,1120]{1,0:T(8,128)(2,1)S(1)} %pad_maximum_fusion.1), channel_id=1, source_target_pairs={{0,1},{1,2},{2,3},{3,4},{4,5},{5,6},{6,7},{7,8},{8,9},{9,10},{10,1... | collective-permute-start | bytes 107528 | tf_op jit(solution)/shard_map/ppermute | solution.py:240
  10.2 2.2 %collective-permute-done = bf16[5,32,608]{2,1,0:T(8,128)(2,1)S(1)} collective-permute-done((bf16[5,32,608]{2,1,0:T(8,128)(2,1)}, bf16[5,32,608]{2,1,0:T(8,128)(2,1)S(1)}, u32[]{:S(2)}, u32[]{:S(2)}) %collective-permute-start) | collective-permute-done | bytes 194592 | tf_op jit(solution)/shard_map/ppermute | solution.py:213
  12.7 3.5 %collective-permute-start.4 = (bf16[16,1120]{1,0:T(8,128)(2,1)S(1)}, bf16[16,1120]{1,0:T(8,128)(2,1)S(1)}, u32[]{:S(2)}, u32[]{:S(2)}) collective-permute-start(bf16[16,1120]{1,0:T(8,128)(2,1)S(1)} %pad_maximum_fusion.2), channel_id=1, source_target_pairs={{1,0},{2,1},{3,2},{4,3},{5,4},{6,5},{7,6},{8,7},{9,8},{10,9},{11,1... | collective-permute-start | bytes 107528 | tf_op jit(solution)/shard_map/ppermute | solution.py:241
  16.2 1.3 %collective-permute-done.3 = bf16[16,1120]{1,0:T(8,128)(2,1)S(1)} collective-permute-done((bf16[16,1120]{1,0:T(8,128)(2,1)S(1)}, bf16[16,1120]{1,0:T(8,128)(2,1)S(1)}, u32[]{:S(2)}, u32[]{:S(2)}) %collective-permute-start.3) | collective-permute-done | bytes 35872 | tf_op jit(solution)/shard_map/ppermute | solution.py:240
  17.5 2.4 %collective-permute-done.4 = bf16[16,1120]{1,0:T(8,128)(2,1)S(1)} collective-permute-done((bf16[16,1120]{1,0:T(8,128)(2,1)S(1)}, bf16[16,1120]{1,0:T(8,128)(2,1)S(1)}, u32[]{:S(2)}, u32[]{:S(2)}) %collective-permute-start.4) | collective-permute-done | bytes 35872 | tf_op jit(solution)/shard_map/ppermute | solution.py:241
  20.0 1.8 %pool.1 = (bf16[528,128]{1,0:T(8,128)(2,1)S(1)}, bf16[528,128]{1,0:T(8,128)(2,1)S(1)}, bf16[528,128]{1,0:T(8,128)(2,1)S(1)}, bf16[528,128]{1,0:T(8,128)(2,1)S(1)}) custom-call(s32[2]{0:T(128)S(1)} %pad_add_fusion.place, bf16[1024,512]{1,0:T(8,128)(2,1)S(1)} %copy-done, bf16[16,512]{1,0:T(8,128)(2,1)S(1)} %slice.33.low, bf16[16,512]{1,0:T(8,128)(2,1)S(1)} %slice.35.high), custom_call_target="tpu_custom_call" | custom-call | tf_op jit(solution)/shard_map/pool/pallas_call | solution.py:245
  22.4 1.2 %collective-permute-start.7 = (bf16[528,128]{1,0:T(8,128)(2,1)S(1)}, bf16[528,128]{1,0:T(8,128)(2,1)S(1)}, u32[]{:S(2)}, u32[]{:S(2)}) collective-permute-start(bf16[528,128]{1,0:T(8,128)(2,1)S(1)} %get-tuple-element.30.s2), channel_id=1, source_target_pairs={{0,2},{1,3},{2,0},{3,1},{4,6},{5,7},{6,4},{7,5},{8,10},{9,11},{10,... | collective-permute-start | bytes 405512 | tf_op jit(solution)/shard_map/ppermute | solution.py:213
  24.1 1.1 %pad_maximum_fusion = bf16[5,128,608]{2,1,0:T(8,128)(2,1)S(1)} fusion(bf16[5,32,608]{2,1,0:T(8,128)(2,1)} %collective-permute-done.2, bf16[5,32,608]{2,1,0:T(8,128)(2,1)} %collective-permute-done.1, bf16[5,32,608]{2,1,0:T(8,128)(2,1)S(1)} %collective-permute-done, bf16[5,32,608]{2,1,0:T(8,128)(2,1)S(1)} %bitcast.12), kind=kLoop, calls=%fused_computation | loop fusion | flops 3112960 | bytes 1556480 | tf_op jit(solution)/shard_map/concatenate | solution.py:236
  25.2 1.2 %near.1.start = f32[640,608]{1,0:T(8,128)S(1)} custom-call(bf16[528,128]{1,0:T(8,128)(2,1)S(1)} %get-tuple-element.26.s0, bf16[528,128]{1,0:T(8,128)(2,1)S(1)} %collective-permute-done.5.s1, bf16[608,512]{1,0:T(8,128)(2,1)S(1)} %bitcast.9, bf16[608,512]{1,0:T(8,128)(2,1)S(1)} %collective-permute-done.10.c1), custom_call_target="tpu_custom_call" | custom-call | tf_op jit(solution)/shard_map/near/pallas_call | solution.py:267
  26.5 1.1 %collective-permute-done.7.s2 = bf16[528,128]{1,0:T(8,128)(2,1)S(1)} collective-permute-done((bf16[528,128]{1,0:T(8,128)(2,1)S(1)}, bf16[528,128]{1,0:T(8,128)(2,1)S(1)}, u32[]{:S(2)}, u32[]{:S(2)}) %collective-permute-start.7) | collective-permute-done | bytes 135200 | tf_op jit(solution)/shard_map/ppermute | solution.py:213
  27.5 3.1 %collective-permute-done.8.s3 = bf16[528,128]{1,0:T(8,128)(2,1)S(1)} collective-permute-done((bf16[528,128]{1,0:T(8,128)(2,1)S(1)}, bf16[528,128]{1,0:T(8,128)(2,1)S(1)}, u32[]{:S(2)}, u32[]{:S(2)}) %collective-permute-start.8) | collective-permute-done | bytes 135200 | tf_op jit(solution)/shard_map/ppermute | solution.py:213
  31.0 1.2 %collective-permute-start.11 = (bf16[5,128,640]{2,1,0:T(8,128)(2,1)S(1)}, bf16[5,128,640]{2,1,0:T(8,128)(2,1)S(1)}, u32[]{:S(2)}, u32[]{:S(2)}) collective-permute-start(bf16[5,128,640]{2,1,0:T(8,128)(2,1)S(1)} %pad.4.k0), channel_id=1, source_target_pairs={{0,2},{1,3},{2,0},{3,1},{4,6},{5,7},{6,4},{7,5},{8,10},{9,11},{10,... | collective-permute-start | bytes 2457608 | tf_op jit(solution)/shard_map/ppermute | solution.py:213
  32.2 1.2 %wgrad.1 = (f32[5,32,608]{2,1,0:T(8,128)S(1)}, bf16[5,32,608]{2,1,0:T(8,128)(2,1)S(1)}, bf16[5,32,608]{2,1,0:T(8,128)(2,1)S(1)}, bf16[5,32,608]{2,1,0:T(8,128)(2,1)S(1)}) custom-call(f32[640,608]{1,0:T(8,128)S(1)} %near.1.start, bf16[528,128]{1,0:T(8,128)(2,1)S(1)} %collective-permute-done.7.s2, bf16[528,128]{1,0:T(8,128)(2,1)S(1)} %collective-permute-done.8.s3, ...), custom_call_target="tpu_custom_call" | custom-call | tf_op jit(solution)/shard_map/wgrad/pallas_call | solution.py:276
  34.0 2.7 %collective-permute-start.14 = (bf16[5,32,608]{2,1,0:T(8,128)(2,1)S(1)}, bf16[5,32,608]{2,1,0:T(8,128)(2,1)S(1)}, u32[]{:S(2)}, u32[]{:S(2)}) collective-permute-start(bf16[5,32,608]{2,1,0:T(8,128)(2,1)S(1)} %get-tuple-element.36), channel_id=1, source_target_pairs={{0,4},{1,5},{2,6},{3,7},{4,0},{5,1},{6,2},{7,3},{8,12},{9,13},{10,... | collective-permute-start | bytes 583688 | tf_op jit(solution)/shard_map/ppermute | solution.py:213
  36.7 5.9 %first.1 = (f32[512,608]{1,0:T(8,128)S(1)}, bf16[1024,512]{1,0:T(8,128)(2,1)S(1)}, f32[1024,256]{1,0:T(8,128)S(1)}, bf16[256,512]{1,0:T(8,128)(2,1)S(1)}, bf16[5...) custom-call(s32[2]{0:T(128)S(1)} %pad_add_fusion.place, bf16[528,128]{1,0:T(8,128)(2,1)S(1)} %get-tuple-element.26.s0, ...), custom_call_target="tpu_custom_call" | custom-call | tf_op jit(solution)/shard_map/first/pallas_call | solution.py:298
  42.6 3.2 %collective-permute-done.14 = bf16[5,32,608]{2,1,0:T(8,128)(2,1)S(1)} collective-permute-done((bf16[5,32,608]{2,1,0:T(8,128)(2,1)S(1)}, bf16[5,32,608]{2,1,0:T(8,128)(2,1)S(1)}, u32[]{:S(2)}, u32[]{:S(2)}) %collective-permute-start.14) | collective-permute-done | bytes 194592 | tf_op jit(solution)/shard_map/ppermute | solution.py:213
  45.8 8.1 %collective-permute-done.15 = bf16[5,32,608]{2,1,0:T(8,128)(2,1)S(1)} collective-permute-done((bf16[5,32,608]{2,1,0:T(8,128)(2,1)S(1)}, bf16[5,32,608]{2,1,0:T(8,128)(2,1)S(1)}, u32[]{:S(2)}, u32[]{:S(2)}) %collective-permute-start.15) | collective-permute-done | bytes 194592 | tf_op jit(solution)/shard_map/ppermute | solution.py:213
  53.9 0.8 %collective-permute-start.16 = (bf16[5,128,640]{2,1,0:T(8,128)(2,1)S(1)}, bf16[5,128,640]{2,1,0:T(8,128)(2,1)S(1)}, u32[]{:S(2)}, u32[]{:S(2)}) collective-permute-start(bf16[5,128,640]{2,1,0:T(8,128)(2,1)S(1)} %collective-permute-done.11.k2), channel_id=1, source_target_pairs={{0,1},{1,0},{2,3},{3,2},{4,5},{5,4},{6,7},{7,6},{8,9},{9,8},{10,11... | collective-permute-start | bytes 2457608 | tf_op jit(solution)/shard_map/ppermute | solution.py:213
  54.7 0.9 %add_bitcast_fusion = f32[32,5,608]{2,0,1:T(8,128)} fusion(bf16[5,32,608]{2,1,0:T(8,128)(2,1)S(1)} %collective-permute-done.15, bf16[5,32,608]{2,1,0:T(8,128)(2,1)S(1)} %collective-permute-done.14, f32[5,32,608]{2,1,0:T(8,128)S(1)} %get-tuple-element.46, bf16[5,32,608]{2,1,0:T(8,128)(2,1)S(1)} %collective-permute-done.13), kind=kLoop, calls=%fused_computation.1 | loop fusion | flops 583680 | bytes 1361920 | tf_op jit(solution)/shard_map/transpose | solution.py:336
  55.6 1.1 %collective-permute-done.16.k3 = bf16[5,128,640]{2,1,0:T(8,128)(2,1)S(1)} collective-permute-done((bf16[5,128,640]{2,1,0:T(8,128)(2,1)S(1)}, bf16[5,128,640]{2,1,0:T(8,128)(2,1)S(1)}, u32[]{:S(2)}, u32[]{:S(2)}) %collective-permute-start.16) | collective-permute-done | bytes 819232 | tf_op jit(solution)/shard_map/ppermute | solution.py:213
  56.7 3.7 %second.1 = (bf16[608,512]{1,0:T(8,128)(2,1)}, bf16[1024,512]{1,0:T(8,128)(2,1)}) custom-call(bf16[5,128,640]{2,1,0:T(8,128)(2,1)S(1)} %collective-permute-done.11.k2, bf16[5,128,640]{2,1,0:T(8,128)(2,1)S(1)} %collective-permute-done.16.k3, bf16[512,1280]{1,0:T(8,128)(2,1)S(1)} %get-tuple-element.39.columns, ...), custom_call_target="tpu_custom_call" | custom-call | tf_op jit(solution)/shard_map/second/pallas_call | solution.py:321
  (34 shorter events, 3.4 us)
Async XLA Ops:
  0.6 23.5 %copy-start.2 = (bf16[32,5,608]{2,0,1:T(8,128)(2,1)S(1)}, bf16[32,5,608]{2,0,1:T(8,128)(2,1)}, u32[]{:S(2)}) copy-start(bf16[32,5,608]{2,0,1:T(8,128)(2,1)} %param.4) | copy-start | bytes 583684
  0.6 19.3 %copy-start = (bf16[1024,512]{1,0:T(8,128)(2,1)S(1)}, bf16[1024,512]{1,0:T(8,128)(2,1)}, u32[]{:S(2)}) copy-start(bf16[1024,512]{1,0:T(8,128)(2,1)} %act.2) | copy-start | bytes 3145732
  0.7 11.8 %collective-permute-start = (bf16[5,32,608]{2,1,0:T(8,128)(2,1)}, bf16[5,32,608]{2,1,0:T(8,128)(2,1)S(1)}, u32[]{:S(2)}, u32[]{:S(2)}) collective-permute-start(bf16[5,32,608]{2,1,0:T(8,128)(2,1)} %bitcast.10), channel_id=1, source_target_pairs={{0,8},{1,9},{2,10},{3,11},{4,12},{5,13},{6,14},{7,15},{8,0},{9,1},... | collective-permute-start | bytes 583688 | tf_op jit(solution)/shard_map/ppermute | solution.py:213
  3.0 16.9 %collective-permute-start.1 = (bf16[5,32,608]{2,1,0:T(8,128)(2,1)}, bf16[5,32,608]{2,1,0:T(8,128)(2,1)}, u32[]{:S(2)}, u32[]{:S(2)}) collective-permute-start(bf16[5,32,608]{2,1,0:T(8,128)(2,1)} %bitcast.11), channel_id=1, source_target_pairs={{0,4},{1,5},{2,6},{3,7},{4,0},{5,1},{6,2},{7,3},{8,12},{9,13},{10,... | collective-permute-start | bytes 583688 | tf_op jit(solution)/shard_map/ppermute | solution.py:213
  3.2 18.6 %collective-permute-start.6 = (bf16[608,512]{1,0:T(8,128)(2,1)}, bf16[608,512]{1,0:T(8,128)(2,1)S(1)}, u32[]{:S(2)}, u32[]{:S(2)}) collective-permute-start(bf16[608,512]{1,0:T(8,128)(2,1)} %bitcast.7), channel_id=1, source_target_pairs={{0,2},{1,3},{2,0},{3,1},{4,6},{5,7},{6,4},{7,5},{8,10},{9,11},{10,... | collective-permute-start | bytes 1867784 | tf_op jit(solution)/shard_map/ppermute | solution.py:213
  5.8 19.4 %copy-start.1 = (bf16[512,608]{0,1:T(8,128)(2,1)S(1)}, bf16[512,608]{0,1:T(8,128)(2,1)}, u32[]{:S(2)}) copy-start(bf16[512,608]{0,1:T(8,128)(2,1)} %param.5) | copy-start | bytes 1867780
  6.7 10.8 %collective-permute-start.3 = (bf16[16,1120]{1,0:T(8,128)(2,1)S(1)}, bf16[16,1120]{1,0:T(8,128)(2,1)S(1)}, u32[]{:S(2)}, u32[]{:S(2)}) collective-permute-start(bf16[16,1120]{1,0:T(8,128)(2,1)S(1)} %pad_maximum_fusion.1), channel_id=1, source_target_pairs={{0,1},{1,2},{2,3},{3,4},{4,5},{5,6},{6,7},{7,8},{8,9},{9,10},{10,1... | collective-permute-start | bytes 107528 | tf_op jit(solution)/shard_map/ppermute | solution.py:240
  12.4 9.4 %collective-permute-start.2 = (bf16[5,32,608]{2,1,0:T(8,128)(2,1)S(1)}, bf16[5,32,608]{2,1,0:T(8,128)(2,1)}, u32[]{:S(2)}, u32[]{:S(2)}) collective-permute-start(bf16[5,32,608]{2,1,0:T(8,128)(2,1)S(1)} %collective-permute-done), channel_id=1, source_target_pairs={{0,4},{1,5},{2,6},{3,7},{4,0},{5,1},{6,2},{7,3},{8,12},{9,13},{10,... | collective-permute-start | bytes 583688 | tf_op jit(solution)/shard_map/ppermute | solution.py:213
  12.7 7.3 %collective-permute-start.4 = (bf16[16,1120]{1,0:T(8,128)(2,1)S(1)}, bf16[16,1120]{1,0:T(8,128)(2,1)S(1)}, u32[]{:S(2)}, u32[]{:S(2)}) collective-permute-start(bf16[16,1120]{1,0:T(8,128)(2,1)S(1)} %pad_maximum_fusion.2), channel_id=1, source_target_pairs={{1,0},{2,1},{3,2},{4,3},{5,4},{6,5},{7,6},{8,7},{9,8},{10,9},{11,1... | collective-permute-start | bytes 107528 | tf_op jit(solution)/shard_map/ppermute | solution.py:241
  17.5 7.7 %collective-permute-start.10 = (bf16[608,512]{1,0:T(8,128)(2,1)}, bf16[608,512]{1,0:T(8,128)(2,1)S(1)}, u32[]{:S(2)}, u32[]{:S(2)}) collective-permute-start(bf16[608,512]{1,0:T(8,128)(2,1)} %bitcast.8), channel_id=1, source_target_pairs={{0,1},{1,0},{2,3},{3,2},{4,5},{5,4},{6,7},{7,6},{8,9},{9,8},{10,11... | collective-permute-start | bytes 1867784 | tf_op jit(solution)/shard_map/ppermute | solution.py:213
  21.8 8.8 %collective-permute-start.9 = (bf16[608,512]{1,0:T(8,128)(2,1)S(1)}, bf16[608,512]{1,0:T(8,128)(2,1)S(1)}, u32[]{:S(2)}, u32[]{:S(2)}) collective-permute-start(bf16[608,512]{1,0:T(8,128)(2,1)S(1)} %collective-permute-done.6.c2), channel_id=1, source_target_pairs={{0,1},{1,0},{2,3},{3,2},{4,5},{5,4},{6,7},{7,6},{8,9},{9,8},{10,11... | collective-permute-start | bytes 1867784 | tf_op jit(solution)/shard_map/ppermute | solution.py:213
  21.9 3.3 %collective-permute-start.5 = (bf16[528,128]{1,0:T(8,128)(2,1)S(1)}, bf16[528,128]{1,0:T(8,128)(2,1)S(1)}, u32[]{:S(2)}, u32[]{:S(2)}) collective-permute-start(bf16[528,128]{1,0:T(8,128)(2,1)S(1)} %get-tuple-element.27.s1), channel_id=1, source_target_pairs={{0,1},{1,0},{2,3},{3,2},{4,5},{5,4},{6,7},{7,6},{8,9},{9,8},{10,11... | collective-permute-start | bytes 405512 | tf_op jit(solution)/shard_map/ppermute | solution.py:213
  22.4 5.2 %collective-permute-start.7 = (bf16[528,128]{1,0:T(8,128)(2,1)S(1)}, bf16[528,128]{1,0:T(8,128)(2,1)S(1)}, u32[]{:S(2)}, u32[]{:S(2)}) collective-permute-start(bf16[528,128]{1,0:T(8,128)(2,1)S(1)} %get-tuple-element.30.s2), channel_id=1, source_target_pairs={{0,2},{1,3},{2,0},{3,1},{4,6},{5,7},{6,4},{7,5},{8,10},{9,11},{10,... | collective-permute-start | bytes 405512 | tf_op jit(solution)/shard_map/ppermute | solution.py:213
  23.6 7.0 %collective-permute-start.8 = (bf16[528,128]{1,0:T(8,128)(2,1)S(1)}, bf16[528,128]{1,0:T(8,128)(2,1)S(1)}, u32[]{:S(2)}, u32[]{:S(2)}) collective-permute-start(bf16[528,128]{1,0:T(8,128)(2,1)S(1)} %get-tuple-element.31.s3), channel_id=1, source_target_pairs={{0,3},{1,2},{2,1},{3,0},{4,7},{5,6},{6,5},{7,4},{8,11},{9,10},{10,... | collective-permute-start | bytes 405512 | tf_op jit(solution)/shard_map/ppermute | solution.py:213
  30.7 6.0 %collective-permute-start.12 = (bf16[5,128,640]{2,1,0:T(8,128)(2,1)S(1)}, bf16[5,128,640]{2,1,0:T(8,128)(2,1)S(1)}, u32[]{:S(2)}, u32[]{:S(2)}) collective-permute-start(bf16[5,128,640]{2,1,0:T(8,128)(2,1)S(1)} %pad.4.k0), channel_id=1, source_target_pairs={{0,1},{1,0},{2,3},{3,2},{4,5},{5,4},{6,7},{7,6},{8,9},{9,8},{10,11... | collective-permute-start | bytes 2457608 | tf_op jit(solution)/shard_map/ppermute | solution.py:213
  31.0 22.9 %collective-permute-start.11 = (bf16[5,128,640]{2,1,0:T(8,128)(2,1)S(1)}, bf16[5,128,640]{2,1,0:T(8,128)(2,1)S(1)}, u32[]{:S(2)}, u32[]{:S(2)}) collective-permute-start(bf16[5,128,640]{2,1,0:T(8,128)(2,1)S(1)} %pad.4.k0), channel_id=1, source_target_pairs={{0,2},{1,3},{2,0},{3,1},{4,6},{5,7},{6,4},{7,5},{8,10},{9,11},{10,... | collective-permute-start | bytes 2457608 | tf_op jit(solution)/shard_map/ppermute | solution.py:213
  33.4 9.1 %collective-permute-start.13 = (bf16[5,32,608]{2,1,0:T(8,128)(2,1)S(1)}, bf16[5,32,608]{2,1,0:T(8,128)(2,1)S(1)}, u32[]{:S(2)}, u32[]{:S(2)}) collective-permute-start(bf16[5,32,608]{2,1,0:T(8,128)(2,1)S(1)} %get-tuple-element.35), channel_id=1, source_target_pairs={{0,8},{1,9},{2,10},{3,11},{4,12},{5,13},{6,14},{7,15},{8,0},{9,1},... | collective-permute-start | bytes 583688 | tf_op jit(solution)/shard_map/ppermute | solution.py:213
  34.0 11.8 %collective-permute-start.14 = (bf16[5,32,608]{2,1,0:T(8,128)(2,1)S(1)}, bf16[5,32,608]{2,1,0:T(8,128)(2,1)S(1)}, u32[]{:S(2)}, u32[]{:S(2)}) collective-permute-start(bf16[5,32,608]{2,1,0:T(8,128)(2,1)S(1)} %get-tuple-element.36), channel_id=1, source_target_pairs={{0,4},{1,5},{2,6},{3,7},{4,0},{5,1},{6,2},{7,3},{8,12},{9,13},{10,... | collective-permute-start | bytes 583688 | tf_op jit(solution)/shard_map/ppermute | solution.py:213
  36.7 17.2 %collective-permute-start.15 = (bf16[5,32,608]{2,1,0:T(8,128)(2,1)S(1)}, bf16[5,32,608]{2,1,0:T(8,128)(2,1)S(1)}, u32[]{:S(2)}, u32[]{:S(2)}) collective-permute-start(bf16[5,32,608]{2,1,0:T(8,128)(2,1)S(1)} %get-tuple-element.37), channel_id=1, source_target_pairs={{0,12},{1,13},{2,14},{3,15},{4,8},{5,9},{6,10},{7,11},{8,4},{9,5},... | collective-permute-start | bytes 583688 | tf_op jit(solution)/shard_map/ppermute | solution.py:213
  53.9 2.8 %collective-permute-start.16 = (bf16[5,128,640]{2,1,0:T(8,128)(2,1)S(1)}, bf16[5,128,640]{2,1,0:T(8,128)(2,1)S(1)}, u32[]{:S(2)}, u32[]{:S(2)}) collective-permute-start(bf16[5,128,640]{2,1,0:T(8,128)(2,1)S(1)} %collective-permute-done.11.k2), channel_id=1, source_target_pairs={{0,1},{1,0},{2,3},{3,2},{4,5},{5,4},{6,7},{7,6},{8,9},{9,8},{10,11... | collective-permute-start | bytes 2457608 | tf_op jit(solution)/shard_map/ppermute | solution.py:213

commit v6 on v5

--- a/solution.py
+++ b/solution.py
@@ -52,36 +52,36 @@
     return jnp.where(chan == want, 1.0, 0.0).astype(BF16)
 
 
-def pool_kernel(rows, place, act, low, high, *mates):
-    channels = act.shape[1]
-    quarter = channels // TEAM
-    order = relative_order(place, rows, channels, False)
-
-    def pooled(g):
-        t = g.shape[0]
-        u = lax.broadcasted_iota(jnp.int32, (t // 2, t), 0)
-        v = lax.broadcasted_iota(jnp.int32, (t // 2, t), 1)
-        halves = jnp.where(lax.div(v, 2) == u, 0.5, 0.0).astype(BF16)
-        s = jnp.dot(halves, g, preferred_element_type=F32).astype(BF16)
-        return jnp.dot(s, order, preferred_element_type=F32).astype(BF16)
-
-    def put(at, s):
-        n = s.shape[0]
-        for r, mate in enumerate(mates):
-            mate[at : at + n, :] = s[:, r * quarter : (r + 1) * quarter]
-
-    def gelu(v):
-        return gelu_value(v.astype(F32)).astype(BF16)
-
-    window = act.shape[0]
+def pooled_gelu(v, order):
+    g = gelu_value(v.astype(F32)).astype(BF16)
+    t = g.shape[0]
+    u = lax.broadcasted_iota(jnp.int32, (t // 2, t), 0)
+    w = lax.broadcasted_iota(jnp.int32, (t // 2, t), 1)
+    halves = jnp.where(lax.div(w, 2) == u, 0.5, 0.0).astype(BF16)
+    s = jnp.dot(halves, g, preferred_element_type=F32).astype(BF16)
+    return jnp.dot(s, order, preferred_element_type=F32).astype(BF16)
+
+
+def put_quarters(outs, at, s):
+    quarter = s.shape[1] // TEAM
+    for r, out in enumerate(outs):
+        out[at : at + s.shape[0], :] = s[:, r * quarter : (r + 1) * quarter]
+
+
+def body_kernel(rows, place, act, order, *bodies):
+    order[...] = relative_order(place, rows, act.shape[1], False)
     block = 256
-    g_prev = gelu(low[...])
-    for at in range(0, window, block):
-        g = gelu(act[at : at + block, :])
-        joined = jnp.concatenate([g_prev, g[: block - HALO]], axis=0)
-        put(at // 2, pooled(joined))
-        g_prev = g[block - HALO :]
-    put(window // 2, pooled(jnp.concatenate([g_prev, gelu(high[...])], axis=0)))
+    for at in range(0, act.shape[0], block):
+        put_quarters(bodies, at // 2, pooled_gelu(act[at : at + block, :], order[...]))
+
+
+def pool_kernel(order, low, high, *refs):
+    bodies, outs = refs[:TEAM], refs[TEAM:]
+    n = bodies[0].shape[0]
+    put_quarters(outs, 0, pooled_gelu(low[...], order[...]))
+    for body, out in zip(bodies, outs):
+        out[EXT : EXT + n, :] = body[...]
+    put_quarters(outs, EXT + n, pooled_gelu(high[...], order[...]))
 
 
 def team_sums(left, pairs, start):
@@ -227,11 +227,21 @@
     shard = kernel.transpose(1, 0, 2)
 
     cot_y = flip(cot_t, 2)
+    gelu_order, *bodies = pl.pallas_call(
+        functools.partial(body_kernel, rows),
+        out_shape=[jax.ShapeDtypeStruct((channels, channels), BF16)]
+        + [jax.ShapeDtypeStruct((positions, quarter), BF16)] * TEAM,
+        in_specs=[SMEM, VMEM],
+        out_specs=[VMEM] * (TEAM + 1),
+        compiler_params=params(24),
+        name="body",
+    )(place, activations)
     order = [0]
     blocks = [shard]
     while len(order) < levels:
         bit = levels // 2 // len(order)
-        blocks = blocks + [flip(block, TEAM * bit) for block in blocks]
+        received = after(blocks[1:], bodies)
+        blocks = blocks + [flip(block, TEAM * bit) for block in blocks[:1] + received]
         order += [m ^ bit for m in order]
     k0 = jnp.concatenate(blocks, axis=1)
     early = blocks[1:2] + blocks[levels // 2 : levels // 2 + 1]
@@ -243,13 +253,13 @@
 
     ext_rows = positions + 2 * EXT
     pieces = pl.pallas_call(
-        functools.partial(pool_kernel, rows),
+        pool_kernel,
         out_shape=[jax.ShapeDtypeStruct((ext_rows, quarter), BF16)] * TEAM,
-        in_specs=[SMEM, VMEM, VMEM, VMEM],
+        in_specs=[VMEM] * (TEAM + 3),
         out_specs=[VMEM] * TEAM,
-        compiler_params=params(32),
+        compiler_params=params(24),
         name="pool",
-    )(place, after(activations, *early), low[:, :channels], high[:, :channels])
+    )(after(gelu_order, *early), low[:, :channels], high[:, :channels], *bodies)
 
     far = after(pieces[2:], cot_y)
     mates = [pieces[0], flip(pieces[1], 1), flip(far[0], 2), flip(far[1], 3)]

time: 60.7 us -> 59.3 us (0.977)
  waiting for transfers between devices: 22.5 us -> 21.3 us
    ppermute x15, waiting for transfers between devices: 18.8 us -> 17.5 us  [flip(): return lax.ppermute(x, 'pos', [(i, i ^ bit) for i in range(n)])]
    ppermute x1, starting transfers between devices: 3.47 us -> 2.85 us  [on_device(): high = lax.ppermute(edge_high, 'pos', [(i + 1, i) for i in range(n - 1)])]
    pallas_call x1 -> x2, Pallas kernels: 1.82 us -> 2.05 us  [the longest x1 1.63 us: on_device(): pl.pallas_call(functools.partial(body_kernel, rows), out_shape=[jax.Shape...]
  transfers between devices with their start and end apart: 17 -> 17, of which waited for: 8 -> 9; matrix products, arithmetic and copies ran while one was open for 7% -> 7% of each run, Pallas kernels for 17% -> 18%
where the time goes in v6:
time: 59.3 us; the launch traced here: 59 us
  waiting for transfers between devices  21.3 us (36%)
  starting transfers between devices  18.7 us (32%)
  Pallas kernels  14 us (24%)
  local copies, waits for them, and re-layouts  2.25 us (4%)
  other arithmetic  1.96 us (3%)
  between operations  0.79 us (1%)
    ppermute x15, waiting for transfers between devices, flip(): return lax.ppermute(x, 'pos', [(i, i ^ bit) for i in range(n)])  17.5 us
    ppermute x15, starting transfers between devices, flip(): return lax.ppermute(x, 'pos', [(i, i ^ bit) for i in range(n)])  12.3 us
    pallas_call x1, Pallas kernels, on_device(): pl.pallas_call(functools.partial(first_kernel, rows), out_shape=[jax.Shap...  5.85 us
    pallas_call x1, Pallas kernels, on_device(): pl.pallas_call(second_kernel, out_shape=[jax.ShapeDtypeStruct((width, pos...  3.68 us
    ppermute x1, starting transfers between devices, on_device(): low = lax.ppermute(edge_low, 'pos', [(i, i + 1) for i in range(n - 1)])  3.53 us
    ppermute x1, starting transfers between devices, on_device(): high = lax.ppermute(edge_high, 'pos', [(i + 1, i) for i in range(n - 1)])  2.85 us
    ppermute x1, waiting for transfers between devices, on_device(): high = lax.ppermute(edge_high, 'pos', [(i + 1, i) for i in range(n - 1)])  2.42 us
    pallas_call x1, Pallas kernels, on_device(): pl.pallas_call(functools.partial(body_kernel, rows), out_shape=[jax.Shape...  1.63 us
  transfers between devices with their start and end apart: 17, of which 9 were waited for; matrix products, arithmetic and copies ran while one was open for 7% of the time, Pallas kernels for 18%

profile of v6, /device:TPU:9, one launch (start us, length us, event | category | flops | bytes accessed | tf_op | source)
XLA Modules:
  0.0 59.0 jit_solution(15467990165037617479)
XLA Ops:
  0.7 2.4 %collective-permute-start = (bf16[5,32,608]{2,1,0:T(8,128)(2,1)}, bf16[5,32,608]{2,1,0:T(8,128)(2,1)S(1)}, u32[]{:S(2)}, u32[]{:S(2)}) collective-permute-start(bf16[5,32,608]{2,1,0:T(8,128)(2,1)} %bitcast.10), channel_id=1, source_target_pairs={{0,8},{1,9},{2,10},{3,11},{4,12},{5,13},{6,14},{7,15},{8,0},{9,1},... | collective-permute-start | bytes 583688 | tf_op jit(solution)/shard_map/ppermute | solution.py:213
  3.2 1.2 %collective-permute-start.6 = (bf16[608,512]{1,0:T(8,128)(2,1)}, bf16[608,512]{1,0:T(8,128)(2,1)S(1)}, u32[]{:S(2)}, u32[]{:S(2)}) collective-permute-start(bf16[608,512]{1,0:T(8,128)(2,1)} %bitcast.7), channel_id=1, source_target_pairs={{0,2},{1,3},{2,0},{3,1},{4,6},{5,7},{6,4},{7,5},{8,10},{9,11},{10,... | collective-permute-start | bytes 1867784 | tf_op jit(solution)/shard_map/ppermute | solution.py:213
  4.4 1.4 %copy.6.cot = bf16[512,608]{1,0:T(8,128)(2,1)S(1)} copy(bf16[512,608]{0,1:T(8,128)(2,1)} %param.5) | data formatting | bytes 1245184 | tf_op args[2]
  6.6 3.5 %collective-permute-start.3 = (bf16[16,1120]{1,0:T(8,128)(2,1)S(1)}, bf16[16,1120]{1,0:T(8,128)(2,1)S(1)}, u32[]{:S(2)}, u32[]{:S(2)}) collective-permute-start(bf16[16,1120]{1,0:T(8,128)(2,1)S(1)} %pad_maximum_fusion.1), channel_id=1, source_target_pairs={{0,1},{1,2},{2,3},{3,4},{4,5},{5,6},{6,7},{7,8},{8,9},{9,10},{10,1... | collective-permute-start | bytes 107528 | tf_op jit(solution)/shard_map/ppermute | solution.py:250
  10.2 1.6 %body.1 = (bf16[512,512]{1,0:T(8,128)(2,1)S(1)}, bf16[512,128]{1,0:T(8,128)(2,1)S(1)}, bf16[512,128]{1,0:T(8,128)(2,1)S(1)}, bf16[512,128]{1,0:T(8,128)(2,1)S(1)}, bf16[512,128]{1,0:T(8,128)(2,1)S(1)}) custom-call(s32[2]{0:T(128)S(1)} %pad_add_fusion.place, bf16[1024,512]{1,0:T(8,128)(2,1)S(1)} %copy-done), custom_call_target="tpu_custom_call" | custom-call | tf_op jit(solution)/shard_map/body/pallas_call | solution.py:230
  13.3 2.8 %collective-permute-start.4 = (bf16[16,1120]{1,0:T(8,128)(2,1)S(1)}, bf16[16,1120]{1,0:T(8,128)(2,1)S(1)}, u32[]{:S(2)}, u32[]{:S(2)}) collective-permute-start(bf16[16,1120]{1,0:T(8,128)(2,1)S(1)} %pad_maximum_fusion.2), channel_id=1, source_target_pairs={{1,0},{2,1},{3,2},{4,3},{5,4},{6,5},{7,6},{8,7},{9,8},{10,9},{11,1... | collective-permute-start | bytes 107528 | tf_op jit(solution)/shard_map/ppermute | solution.py:251
  16.1 1.4 %collective-permute-done.3 = bf16[16,1120]{1,0:T(8,128)(2,1)S(1)} collective-permute-done((bf16[16,1120]{1,0:T(8,128)(2,1)S(1)}, bf16[16,1120]{1,0:T(8,128)(2,1)S(1)}, u32[]{:S(2)}, u32[]{:S(2)}) %collective-permute-start.3) | collective-permute-done | bytes 35872 | tf_op jit(solution)/shard_map/ppermute | solution.py:250
  17.5 2.4 %collective-permute-done.4 = bf16[16,1120]{1,0:T(8,128)(2,1)S(1)} collective-permute-done((bf16[16,1120]{1,0:T(8,128)(2,1)S(1)}, bf16[16,1120]{1,0:T(8,128)(2,1)S(1)}, u32[]{:S(2)}, u32[]{:S(2)}) %collective-permute-start.4) | collective-permute-done | bytes 35872 | tf_op jit(solution)/shard_map/ppermute | solution.py:251
  20.9 1.2 %collective-permute-start.7 = (bf16[528,128]{1,0:T(8,128)(2,1)S(1)}, bf16[528,128]{1,0:T(8,128)(2,1)S(1)}, u32[]{:S(2)}, u32[]{:S(2)}) collective-permute-start(bf16[528,128]{1,0:T(8,128)(2,1)S(1)} %get-tuple-element.42.s2), channel_id=1, source_target_pairs={{0,2},{1,3},{2,0},{3,1},{4,6},{5,7},{6,4},{7,5},{8,10},{9,11},{10,... | collective-permute-start | bytes 405512 | tf_op jit(solution)/shard_map/ppermute | solution.py:213
  22.7 1.0 %pad_maximum_fusion = bf16[5,128,608]{2,1,0:T(8,128)(2,1)S(1)} fusion(bf16[5,32,608]{2,1,0:T(8,128)(2,1)S(1)} %collective-permute-done.2, bf16[5,32,608]{2,1,0:T(8,128)(2,1)} %collective-permute-done.1, bf16[5,32,608]{2,1,0:T(8,128)(2,1)S(1)} %collective-permute-done, bf16[5,32,608]{2,1,0:T(8,128)(2,1)S(1)} %bitcast.12), kind=kLoop, calls=%fused_computation | loop fusion | flops 3112960 | bytes 1556480 | tf_op jit(solution)/shard_map/concatenate | solution.py:246
  23.7 1.2 %near.1.start = f32[640,608]{1,0:T(8,128)S(1)} custom-call(bf16[528,128]{1,0:T(8,128)(2,1)S(1)} %get-tuple-element.38.s0, bf16[528,128]{1,0:T(8,128)(2,1)S(1)} %collective-permute-done.5.s1, bf16[608,512]{1,0:T(8,128)(2,1)S(1)} %bitcast.9, bf16[608,512]{1,0:T(8,128)(2,1)S(1)} %collective-permute-done.10.c1), custom_call_target="tpu_custom_call" | custom-call | tf_op jit(solution)/shard_map/near/pallas_call | solution.py:277
  24.9 1.2 %collective-permute-done.7.s2 = bf16[528,128]{1,0:T(8,128)(2,1)S(1)} collective-permute-done((bf16[528,128]{1,0:T(8,128)(2,1)S(1)}, bf16[528,128]{1,0:T(8,128)(2,1)S(1)}, u32[]{:S(2)}, u32[]{:S(2)}) %collective-permute-start.7) | collective-permute-done | bytes 135200 | tf_op jit(solution)/shard_map/ppermute | solution.py:213
  26.1 3.1 %collective-permute-done.8.s3 = bf16[528,128]{1,0:T(8,128)(2,1)S(1)} collective-permute-done((bf16[528,128]{1,0:T(8,128)(2,1)S(1)}, bf16[528,128]{1,0:T(8,128)(2,1)S(1)}, u32[]{:S(2)}, u32[]{:S(2)}) %collective-permute-start.8) | collective-permute-done | bytes 135200 | tf_op jit(solution)/shard_map/ppermute | solution.py:213
  29.6 1.1 %collective-permute-start.11 = (bf16[5,128,640]{2,1,0:T(8,128)(2,1)S(1)}, bf16[5,128,640]{2,1,0:T(8,128)(2,1)S(1)}, u32[]{:S(2)}, u32[]{:S(2)}) collective-permute-start(bf16[5,128,640]{2,1,0:T(8,128)(2,1)S(1)} %pad.4.k0), channel_id=1, source_target_pairs={{0,2},{1,3},{2,0},{3,1},{4,6},{5,7},{6,4},{7,5},{8,10},{9,11},{10,... | collective-permute-start | bytes 2457608 | tf_op jit(solution)/shard_map/ppermute | solution.py:213
  30.6 1.2 %wgrad.1 = (f32[5,32,608]{2,1,0:T(8,128)S(1)}, bf16[5,32,608]{2,1,0:T(8,128)(2,1)S(1)}, bf16[5,32,608]{2,1,0:T(8,128)(2,1)S(1)}, bf16[5,32,608]{2,1,0:T(8,128)(2,1)S(1)}) custom-call(f32[640,608]{1,0:T(8,128)S(1)} %near.1.start, bf16[528,128]{1,0:T(8,128)(2,1)S(1)} %collective-permute-done.7.s2, bf16[528,128]{1,0:T(8,128)(2,1)S(1)} %collective-permute-done.8.s3, ...), custom_call_target="tpu_custom_call" | custom-call | tf_op jit(solution)/shard_map/wgrad/pallas_call | solution.py:286
  31.8 2.1 %collective-permute-start.13 = (bf16[5,32,608]{2,1,0:T(8,128)(2,1)S(1)}, bf16[5,32,608]{2,1,0:T(8,128)(2,1)S(1)}, u32[]{:S(2)}, u32[]{:S(2)}) collective-permute-start(bf16[5,32,608]{2,1,0:T(8,128)(2,1)S(1)} %get-tuple-element.47), channel_id=1, source_target_pairs={{0,8},{1,9},{2,10},{3,11},{4,12},{5,13},{6,14},{7,15},{8,0},{9,1},... | collective-permute-start | bytes 583688 | tf_op jit(solution)/shard_map/ppermute | solution.py:213
  33.9 1.3 %collective-permute-start.14 = (bf16[5,32,608]{2,1,0:T(8,128)(2,1)S(1)}, bf16[5,32,608]{2,1,0:T(8,128)(2,1)S(1)}, u32[]{:S(2)}, u32[]{:S(2)}) collective-permute-start(bf16[5,32,608]{2,1,0:T(8,128)(2,1)S(1)} %get-tuple-element.48), channel_id=1, source_target_pairs={{0,4},{1,5},{2,6},{3,7},{4,0},{5,1},{6,2},{7,3},{8,12},{9,13},{10,... | collective-permute-start | bytes 583688 | tf_op jit(solution)/shard_map/ppermute | solution.py:213
  35.3 5.8 %first.1 = (f32[512,608]{1,0:T(8,128)S(1)}, bf16[1024,512]{1,0:T(8,128)(2,1)S(1)}, f32[1024,256]{1,0:T(8,128)S(1)}, bf16[256,512]{1,0:T(8,128)(2,1)S(1)}, bf16[5...) custom-call(s32[2]{0:T(128)S(1)} %pad_add_fusion.place, bf16[528,128]{1,0:T(8,128)(2,1)S(1)} %get-tuple-element.38.s0, ...), custom_call_target="tpu_custom_call" | custom-call | tf_op jit(solution)/shard_map/first/pallas_call | solution.py:308
  41.1 1.1 %collective-permute-done.13 = bf16[5,32,608]{2,1,0:T(8,128)(2,1)S(1)} collective-permute-done((bf16[5,32,608]{2,1,0:T(8,128)(2,1)S(1)}, bf16[5,32,608]{2,1,0:T(8,128)(2,1)S(1)}, u32[]{:S(2)}, u32[]{:S(2)}) %collective-permute-start.13) | collective-permute-done | bytes 194592 | tf_op jit(solution)/shard_map/ppermute | solution.py:213
  42.2 2.2 %collective-permute-done.14 = bf16[5,32,608]{2,1,0:T(8,128)(2,1)S(1)} collective-permute-done((bf16[5,32,608]{2,1,0:T(8,128)(2,1)S(1)}, bf16[5,32,608]{2,1,0:T(8,128)(2,1)S(1)}, u32[]{:S(2)}, u32[]{:S(2)}) %collective-permute-start.14) | collective-permute-done | bytes 194592 | tf_op jit(solution)/shard_map/ppermute | solution.py:213
  44.3 8.4 %collective-permute-done.15 = bf16[5,32,608]{2,1,0:T(8,128)(2,1)S(1)} collective-permute-done((bf16[5,32,608]{2,1,0:T(8,128)(2,1)S(1)}, bf16[5,32,608]{2,1,0:T(8,128)(2,1)S(1)}, u32[]{:S(2)}, u32[]{:S(2)}) %collective-permute-start.15) | collective-permute-done | bytes 194592 | tf_op jit(solution)/shard_map/ppermute | solution.py:213
  53.3 0.9 %add_bitcast_fusion = f32[32,5,608]{2,0,1:T(8,128)} fusion(bf16[5,32,608]{2,1,0:T(8,128)(2,1)S(1)} %collective-permute-done.15, bf16[5,32,608]{2,1,0:T(8,128)(2,1)S(1)} %collective-permute-done.14, f32[5,32,608]{2,1,0:T(8,128)S(1)} %get-tuple-element.58, bf16[5,32,608]{2,1,0:T(8,128)(2,1)S(1)} %collective-permute-done.13), kind=kLoop, calls=%fused_computation.1 | loop fusion | flops 583680 | bytes 1361920 | tf_op jit(solution)/shard_map/transpose | solution.py:346
  54.2 1.1 %collective-permute-done.16.k3 = bf16[5,128,640]{2,1,0:T(8,128)(2,1)S(1)} collective-permute-done((bf16[5,128,640]{2,1,0:T(8,128)(2,1)S(1)}, bf16[5,128,640]{2,1,0:T(8,128)(2,1)S(1)}, u32[]{:S(2)}, u32[]{:S(2)}) %collective-permute-start.16) | collective-permute-done | bytes 819232 | tf_op jit(solution)/shard_map/ppermute | solution.py:213
  55.3 3.7 %second.1 = (bf16[608,512]{1,0:T(8,128)(2,1)}, bf16[1024,512]{1,0:T(8,128)(2,1)}) custom-call(bf16[5,128,640]{2,1,0:T(8,128)(2,1)S(1)} %collective-permute-done.11.k2, bf16[5,128,640]{2,1,0:T(8,128)(2,1)S(1)} %collective-permute-done.16.k3, bf16[512,1280]{1,0:T(8,128)(2,1)S(1)} %get-tuple-element.51.columns, ...), custom_call_target="tpu_custom_call" | custom-call | tf_op jit(solution)/shard_map/second/pallas_call | solution.py:331
  (35 shorter events, 4.9 us)
Async XLA Ops:
  0.6 9.6 %copy-start = (bf16[1024,512]{1,0:T(8,128)(2,1)S(1)}, bf16[1024,512]{1,0:T(8,128)(2,1)}, u32[]{:S(2)}) copy-start(bf16[1024,512]{1,0:T(8,128)(2,1)} %act.3) | copy-start | bytes 3145732
  0.6 16.9 %copy-start.1 = (bf16[512,608]{0,1:T(8,128)(2,1)S(1)}, bf16[512,608]{0,1:T(8,128)(2,1)}, u32[]{:S(2)}) copy-start(bf16[512,608]{0,1:T(8,128)(2,1)} %param.5) | copy-start | bytes 1867780
  0.7 11.8 %collective-permute-start = (bf16[5,32,608]{2,1,0:T(8,128)(2,1)}, bf16[5,32,608]{2,1,0:T(8,128)(2,1)S(1)}, u32[]{:S(2)}, u32[]{:S(2)}) collective-permute-start(bf16[5,32,608]{2,1,0:T(8,128)(2,1)} %bitcast.10), channel_id=1, source_target_pairs={{0,8},{1,9},{2,10},{3,11},{4,12},{5,13},{6,14},{7,15},{8,0},{9,1},... | collective-permute-start | bytes 583688 | tf_op jit(solution)/shard_map/ppermute | solution.py:213
  3.0 16.9 %collective-permute-start.1 = (bf16[5,32,608]{2,1,0:T(8,128)(2,1)}, bf16[5,32,608]{2,1,0:T(8,128)(2,1)}, u32[]{:S(2)}, u32[]{:S(2)}) collective-permute-start(bf16[5,32,608]{2,1,0:T(8,128)(2,1)} %bitcast.11), channel_id=1, source_target_pairs={{0,4},{1,5},{2,6},{3,7},{4,0},{5,1},{6,2},{7,3},{8,12},{9,13},{10,... | collective-permute-start | bytes 583688 | tf_op jit(solution)/shard_map/ppermute | solution.py:213
  3.2 19.5 %copy-start.2 = (bf16[32,5,608]{2,0,1:T(8,128)(2,1)S(1)}, bf16[32,5,608]{2,0,1:T(8,128)(2,1)}, u32[]{:S(2)}) copy-start(bf16[32,5,608]{2,0,1:T(8,128)(2,1)} %param.4) | copy-start | bytes 583684
  3.2 17.2 %collective-permute-start.6 = (bf16[608,512]{1,0:T(8,128)(2,1)}, bf16[608,512]{1,0:T(8,128)(2,1)S(1)}, u32[]{:S(2)}, u32[]{:S(2)}) collective-permute-start(bf16[608,512]{1,0:T(8,128)(2,1)} %bitcast.7), channel_id=1, source_target_pairs={{0,2},{1,3},{2,0},{3,1},{4,6},{5,7},{6,4},{7,5},{8,10},{9,11},{10,... | collective-permute-start | bytes 1867784 | tf_op jit(solution)/shard_map/ppermute | solution.py:213
  6.6 10.9 %collective-permute-start.3 = (bf16[16,1120]{1,0:T(8,128)(2,1)S(1)}, bf16[16,1120]{1,0:T(8,128)(2,1)S(1)}, u32[]{:S(2)}, u32[]{:S(2)}) collective-permute-start(bf16[16,1120]{1,0:T(8,128)(2,1)S(1)} %pad_maximum_fusion.1), channel_id=1, source_target_pairs={{0,1},{1,2},{2,3},{3,4},{4,5},{5,6},{6,7},{7,8},{8,9},{9,10},{10,1... | collective-permute-start | bytes 107528 | tf_op jit(solution)/shard_map/ppermute | solution.py:250
  12.4 8.0 %collective-permute-start.2 = (bf16[5,32,608]{2,1,0:T(8,128)(2,1)S(1)}, bf16[5,32,608]{2,1,0:T(8,128)(2,1)S(1)}, u32[]{:S(2)}, u32[]{:S(2)}) collective-permute-start(bf16[5,32,608]{2,1,0:T(8,128)(2,1)S(1)} %collective-permute-done), channel_id=1, source_target_pairs={{0,4},{1,5},{2,6},{3,7},{4,0},{5,1},{6,2},{7,3},{8,12},{9,13},{10,... | collective-permute-start | bytes 583688 | tf_op jit(solution)/shard_map/ppermute | solution.py:213
  13.3 6.7 %collective-permute-start.4 = (bf16[16,1120]{1,0:T(8,128)(2,1)S(1)}, bf16[16,1120]{1,0:T(8,128)(2,1)S(1)}, u32[]{:S(2)}, u32[]{:S(2)}) collective-permute-start(bf16[16,1120]{1,0:T(8,128)(2,1)S(1)} %pad_maximum_fusion.2), channel_id=1, source_target_pairs={{1,0},{2,1},{3,2},{4,3},{5,4},{6,5},{7,6},{8,7},{9,8},{10,9},{11,1... | collective-permute-start | bytes 107528 | tf_op jit(solution)/shard_map/ppermute | solution.py:251
  17.5 6.2 %collective-permute-start.10 = (bf16[608,512]{1,0:T(8,128)(2,1)S(1)}, bf16[608,512]{1,0:T(8,128)(2,1)S(1)}, u32[]{:S(2)}, u32[]{:S(2)}) collective-permute-start(bf16[608,512]{1,0:T(8,128)(2,1)S(1)} %bitcast.8), channel_id=1, source_target_pairs={{0,1},{1,0},{2,3},{3,2},{4,5},{5,4},{6,7},{7,6},{8,9},{9,8},{10,11... | collective-permute-start | bytes 1867784 | tf_op jit(solution)/shard_map/ppermute | solution.py:213
  20.4 8.8 %collective-permute-start.9 = (bf16[608,512]{1,0:T(8,128)(2,1)S(1)}, bf16[608,512]{1,0:T(8,128)(2,1)S(1)}, u32[]{:S(2)}, u32[]{:S(2)}) collective-permute-start(bf16[608,512]{1,0:T(8,128)(2,1)S(1)} %collective-permute-done.6.c2), channel_id=1, source_target_pairs={{0,1},{1,0},{2,3},{3,2},{4,5},{5,4},{6,7},{7,6},{8,9},{9,8},{10,11... | collective-permute-start | bytes 1867784 | tf_op jit(solution)/shard_map/ppermute | solution.py:213
  20.5 3.2 %collective-permute-start.5 = (bf16[528,128]{1,0:T(8,128)(2,1)S(1)}, bf16[528,128]{1,0:T(8,128)(2,1)S(1)}, u32[]{:S(2)}, u32[]{:S(2)}) collective-permute-start(bf16[528,128]{1,0:T(8,128)(2,1)S(1)} %get-tuple-element.39.s1), channel_id=1, source_target_pairs={{0,1},{1,0},{2,3},{3,2},{4,5},{5,4},{6,7},{7,6},{8,9},{9,8},{10,11... | collective-permute-start | bytes 405512 | tf_op jit(solution)/shard_map/ppermute | solution.py:213
  20.9 5.2 %collective-permute-start.7 = (bf16[528,128]{1,0:T(8,128)(2,1)S(1)}, bf16[528,128]{1,0:T(8,128)(2,1)S(1)}, u32[]{:S(2)}, u32[]{:S(2)}) collective-permute-start(bf16[528,128]{1,0:T(8,128)(2,1)S(1)} %get-tuple-element.42.s2), channel_id=1, source_target_pairs={{0,2},{1,3},{2,0},{3,1},{4,6},{5,7},{6,4},{7,5},{8,10},{9,11},{10,... | collective-permute-start | bytes 405512 | tf_op jit(solution)/shard_map/ppermute | solution.py:213
  22.2 7.0 %collective-permute-start.8 = (bf16[528,128]{1,0:T(8,128)(2,1)S(1)}, bf16[528,128]{1,0:T(8,128)(2,1)S(1)}, u32[]{:S(2)}, u32[]{:S(2)}) collective-permute-start(bf16[528,128]{1,0:T(8,128)(2,1)S(1)} %get-tuple-element.43.s3), channel_id=1, source_target_pairs={{0,3},{1,2},{2,1},{3,0},{4,7},{5,6},{6,5},{7,4},{8,11},{9,10},{10,... | collective-permute-start | bytes 405512 | tf_op jit(solution)/shard_map/ppermute | solution.py:213
  29.3 6.0 %collective-permute-start.12 = (bf16[5,128,640]{2,1,0:T(8,128)(2,1)S(1)}, bf16[5,128,640]{2,1,0:T(8,128)(2,1)S(1)}, u32[]{:S(2)}, u32[]{:S(2)}) collective-permute-start(bf16[5,128,640]{2,1,0:T(8,128)(2,1)S(1)} %pad.4.k0), channel_id=1, source_target_pairs={{0,1},{1,0},{2,3},{3,2},{4,5},{5,4},{6,7},{7,6},{8,9},{9,8},{10,11... | collective-permute-start | bytes 2457608 | tf_op jit(solution)/shard_map/ppermute | solution.py:213
  29.6 23.1 %collective-permute-start.11 = (bf16[5,128,640]{2,1,0:T(8,128)(2,1)S(1)}, bf16[5,128,640]{2,1,0:T(8,128)(2,1)S(1)}, u32[]{:S(2)}, u32[]{:S(2)}) collective-permute-start(bf16[5,128,640]{2,1,0:T(8,128)(2,1)S(1)} %pad.4.k0), channel_id=1, source_target_pairs={{0,2},{1,3},{2,0},{3,1},{4,6},{5,7},{6,4},{7,5},{8,10},{9,11},{10,... | collective-permute-start | bytes 2457608 | tf_op jit(solution)/shard_map/ppermute | solution.py:213
  31.8 10.3 %collective-permute-start.13 = (bf16[5,32,608]{2,1,0:T(8,128)(2,1)S(1)}, bf16[5,32,608]{2,1,0:T(8,128)(2,1)S(1)}, u32[]{:S(2)}, u32[]{:S(2)}) collective-permute-start(bf16[5,32,608]{2,1,0:T(8,128)(2,1)S(1)} %get-tuple-element.47), channel_id=1, source_target_pairs={{0,8},{1,9},{2,10},{3,11},{4,12},{5,13},{6,14},{7,15},{8,0},{9,1},... | collective-permute-start | bytes 583688 | tf_op jit(solution)/shard_map/ppermute | solution.py:213
  33.9 10.4 %collective-permute-start.14 = (bf16[5,32,608]{2,1,0:T(8,128)(2,1)S(1)}, bf16[5,32,608]{2,1,0:T(8,128)(2,1)S(1)}, u32[]{:S(2)}, u32[]{:S(2)}) collective-permute-start(bf16[5,32,608]{2,1,0:T(8,128)(2,1)S(1)} %get-tuple-element.48), channel_id=1, source_target_pairs={{0,4},{1,5},{2,6},{3,7},{4,0},{5,1},{6,2},{7,3},{8,12},{9,13},{10,... | collective-permute-start | bytes 583688 | tf_op jit(solution)/shard_map/ppermute | solution.py:213
  35.2 17.4 %collective-permute-start.15 = (bf16[5,32,608]{2,1,0:T(8,128)(2,1)S(1)}, bf16[5,32,608]{2,1,0:T(8,128)(2,1)S(1)}, u32[]{:S(2)}, u32[]{:S(2)}) collective-permute-start(bf16[5,32,608]{2,1,0:T(8,128)(2,1)S(1)} %get-tuple-element.49), channel_id=1, source_target_pairs={{0,12},{1,13},{2,14},{3,15},{4,8},{5,9},{6,10},{7,11},{8,4},{9,5},... | collective-permute-start | bytes 583688 | tf_op jit(solution)/shard_map/ppermute | solution.py:213
  52.7 2.6 %collective-permute-start.16 = (bf16[5,128,640]{2,1,0:T(8,128)(2,1)S(1)}, bf16[5,128,640]{2,1,0:T(8,128)(2,1)S(1)}, u32[]{:S(2)}, u32[]{:S(2)}) collective-permute-start(bf16[5,128,640]{2,1,0:T(8,128)(2,1)S(1)} %collective-permute-done.11.k2), channel_id=1, source_target_pairs={{0,1},{1,0},{2,3},{3,2},{4,5},{5,4},{6,7},{7,6},{8,9},{9,8},{10,11... | collective-permute-start | bytes 2457608 | tf_op jit(solution)/shard_map/ppermute | solution.py:213

commit v7 on v6

--- a/solution.py
+++ b/solution.py
@@ -297,10 +297,10 @@
         grads = parts[:1] + [p.astype(BF16) for p in parts[1:]]
     terms = [flip(g, TEAM * m) for g, m in zip(grads[1:], order[1:])]
 
-    k0 = after(k0, mates, cot_yc, start)
     k0 = jnp.pad(k0, ((0, 0), (0, 0), (0, -width % 128)))
-    k2 = flip(k0, 2)
+    k0 = after(k0, start)
     k1 = flip(k0, 1)
+    k2 = flip(after(k0, mates, cot_yc), 2)
 
     low_cot, high_cot = low[:, channels:], high[:, channels:]
     half = channels // 2

time: 59.3 us -> 59.2 us (level)
  waiting for transfers between devices: 21.3 us -> 20 us
  starting transfers between devices: 18.7 us -> 19.9 us
    ppermute x1, starting transfers between devices: 2.85 us -> 4.26 us  [on_device(): high = lax.ppermute(edge_high, 'pos', [(i + 1, i) for i in range(n - 1)])]
    ppermute x1, waiting for transfers between devices: 1.4 us -> 0.01 us  [on_device(): low = lax.ppermute(edge_low, 'pos', [(i, i + 1) for i in range(n - 1)])]
  transfers between devices with their start and end apart: 17 -> 17, of which waited for: 9 -> 7; matrix products, arithmetic and copies ran while one was open for 7% -> 7% of each run, Pallas kernels for 18% -> 18%
where the time goes in v7:
time: 59.2 us; the launch traced here: 58.8 us
  waiting for transfers between devices  20 us (34%)
  starting transfers between devices  19.9 us (34%)
  Pallas kernels  14 us (24%)
  local copies, waits for them, and re-layouts  2.17 us (4%)
  other arithmetic  1.99 us (3%)
  between operations  0.8 us (1%)
    ppermute x15, waiting for transfers between devices, flip(): return lax.ppermute(x, 'pos', [(i, i ^ bit) for i in range(n)])  17.3 us
    ppermute x15, starting transfers between devices, flip(): return lax.ppermute(x, 'pos', [(i, i ^ bit) for i in range(n)])  12.1 us
    pallas_call x1, Pallas kernels, on_device(): pl.pallas_call(functools.partial(first_kernel, rows), out_shape=[jax.Shap...  5.85 us
    ppermute x1, starting transfers between devices, on_device(): high = lax.ppermute(edge_high, 'pos', [(i + 1, i) for i in range(n - 1)])  4.26 us
    pallas_call x1, Pallas kernels, on_device(): pl.pallas_call(second_kernel, out_shape=[jax.ShapeDtypeStruct((width, pos...  3.67 us
    ppermute x1, starting transfers between devices, on_device(): low = lax.ppermute(edge_low, 'pos', [(i, i + 1) for i in range(n - 1)])  3.53 us
    ppermute x1, waiting for transfers between devices, on_device(): high = lax.ppermute(edge_high, 'pos', [(i + 1, i) for i in range(n - 1)])  2.64 us
    pallas_call x1, Pallas kernels, on_device(): pl.pallas_call(functools.partial(body_kernel, rows), out_shape=[jax.Shape...  1.63 us
  transfers between devices with their start and end apart: 17, of which 7 were waited for; matrix products, arithmetic and copies ran while one was open for 7% of the time, Pallas kernels for 18%

profile of v7, /device:TPU:9, one launch (start us, length us, event | category | flops | bytes accessed | tf_op | source)
XLA Modules:
  0.0 58.8 jit_solution(3640368507341998518)
XLA Ops:
  0.7 2.5 %collective-permute-start = (bf16[5,32,608]{2,1,0:T(8,128)(2,1)}, bf16[5,32,608]{2,1,0:T(8,128)(2,1)}, u32[]{:S(2)}, u32[]{:S(2)}) collective-permute-start(bf16[5,32,608]{2,1,0:T(8,128)(2,1)} %bitcast.11), channel_id=1, source_target_pairs={{0,8},{1,9},{2,10},{3,11},{4,12},{5,13},{6,14},{7,15},{8,0},{9,1},... | collective-permute-start | bytes 583688 | tf_op jit(solution)/shard_map/ppermute | solution.py:213
  3.2 1.2 %collective-permute-start.7 = (bf16[608,512]{1,0:T(8,128)(2,1)}, bf16[608,512]{1,0:T(8,128)(2,1)S(1)}, u32[]{:S(2)}, u32[]{:S(2)}) collective-permute-start(bf16[608,512]{1,0:T(8,128)(2,1)} %bitcast.7), channel_id=1, source_target_pairs={{0,2},{1,3},{2,0},{3,1},{4,6},{5,7},{6,4},{7,5},{8,10},{9,11},{10,... | collective-permute-start | bytes 1867784 | tf_op jit(solution)/shard_map/ppermute | solution.py:213
  4.4 1.4 %copy.6.cot = bf16[512,608]{1,0:T(8,128)(2,1)S(1)} copy(bf16[512,608]{0,1:T(8,128)(2,1)} %param.5) | data formatting | bytes 1245184 | tf_op args[2]
  6.6 3.5 %collective-permute-start.3 = (bf16[16,1120]{1,0:T(8,128)(2,1)S(1)}, bf16[16,1120]{1,0:T(8,128)(2,1)S(1)}, u32[]{:S(2)}, u32[]{:S(2)}) collective-permute-start(bf16[16,1120]{1,0:T(8,128)(2,1)S(1)} %pad_maximum_fusion), channel_id=1, source_target_pairs={{0,1},{1,2},{2,3},{3,4},{4,5},{5,6},{6,7},{7,8},{8,9},{9,10},{10,1... | collective-permute-start | bytes 107528 | tf_op jit(solution)/shard_map/ppermute | solution.py:250
  10.2 1.6 %body.1 = (bf16[512,512]{1,0:T(8,128)(2,1)S(1)}, bf16[512,128]{1,0:T(8,128)(2,1)S(1)}, bf16[512,128]{1,0:T(8,128)(2,1)S(1)}, bf16[512,128]{1,0:T(8,128)(2,1)S(1)}, bf16[512,128]{1,0:T(8,128)(2,1)S(1)}) custom-call(s32[2]{0:T(128)S(1)} %pad_add_fusion.place, bf16[1024,512]{1,0:T(8,128)(2,1)S(1)} %copy-done), custom_call_target="tpu_custom_call" | custom-call | tf_op jit(solution)/shard_map/body/pallas_call | solution.py:230
  12.4 0.8 %collective-permute-start.2 = (bf16[5,32,608]{2,1,0:T(8,128)(2,1)}, bf16[5,32,608]{2,1,0:T(8,128)(2,1)S(1)}, u32[]{:S(2)}, u32[]{:S(2)}) collective-permute-start(bf16[5,32,608]{2,1,0:T(8,128)(2,1)} %collective-permute-done), channel_id=1, source_target_pairs={{0,4},{1,5},{2,6},{3,7},{4,0},{5,1},{6,2},{7,3},{8,12},{9,13},{10,... | collective-permute-start | bytes 583688 | tf_op jit(solution)/shard_map/ppermute | solution.py:213
  13.3 4.3 %collective-permute-start.4 = (bf16[16,1120]{1,0:T(8,128)(2,1)S(1)}, bf16[16,1120]{1,0:T(8,128)(2,1)S(1)}, u32[]{:S(2)}, u32[]{:S(2)}) collective-permute-start(bf16[16,1120]{1,0:T(8,128)(2,1)S(1)} %pad_maximum_fusion.1), channel_id=1, source_target_pairs={{1,0},{2,1},{3,2},{4,3},{5,4},{6,5},{7,6},{8,7},{9,8},{10,9},{11,1... | collective-permute-start | bytes 107528 | tf_op jit(solution)/shard_map/ppermute | solution.py:251
  17.6 2.6 %collective-permute-done.4 = bf16[16,1120]{1,0:T(8,128)(2,1)S(1)} collective-permute-done((bf16[16,1120]{1,0:T(8,128)(2,1)S(1)}, bf16[16,1120]{1,0:T(8,128)(2,1)S(1)}, u32[]{:S(2)}, u32[]{:S(2)}) %collective-permute-start.4) | collective-permute-done | bytes 35872 | tf_op jit(solution)/shard_map/ppermute | solution.py:251
  21.3 1.3 %collective-permute-start.8 = (bf16[528,128]{1,0:T(8,128)(2,1)S(1)}, bf16[528,128]{1,0:T(8,128)(2,1)S(1)}, u32[]{:S(2)}, u32[]{:S(2)}) collective-permute-start(bf16[528,128]{1,0:T(8,128)(2,1)S(1)} %get-tuple-element.44.s2), channel_id=1, source_target_pairs={{0,2},{1,3},{2,0},{3,1},{4,6},{5,7},{6,4},{7,5},{8,10},{9,11},{10,... | collective-permute-start | bytes 405512 | tf_op jit(solution)/shard_map/ppermute | solution.py:213
  23.0 1.0 %fusion.6.k0 = bf16[5,128,640]{2,1,0:T(8,128)(2,1)S(1)} fusion(bf16[5,32,608]{2,1,0:T(8,128)(2,1)S(1)} %collective-permute-done.2, bf16[5,32,608]{2,1,0:T(8,128)(2,1)S(1)} %collective-permute-done.1, bf16[5,32,608]{2,1,0:T(8,128)(2,1)} %collective-permute-done, bf16[5,32,608]{2,1,0:T(8,128)(2,1)S(1)} %bitcast.12), kind=kLoop, calls=%fused_computation.7 | loop fusion | flops 5324800 | bytes 1597440 | tf_op jit(solution)/shard_map/concatenate | solution.py:246
  24.1 1.2 %near.1.start = f32[640,608]{1,0:T(8,128)S(1)} custom-call(bf16[528,128]{1,0:T(8,128)(2,1)S(1)} %get-tuple-element.39.s0, bf16[528,128]{1,0:T(8,128)(2,1)S(1)} %collective-permute-done.5.s1, bf16[608,512]{1,0:T(8,128)(2,1)S(1)} %bitcast.9, bf16[608,512]{1,0:T(8,128)(2,1)S(1)} %collective-permute-done.6.c1), custom_call_target="tpu_custom_call" | custom-call | tf_op jit(solution)/shard_map/near/pallas_call | solution.py:277
  25.5 0.9 %collective-permute-done.8.s2 = bf16[528,128]{1,0:T(8,128)(2,1)S(1)} collective-permute-done((bf16[528,128]{1,0:T(8,128)(2,1)S(1)}, bf16[528,128]{1,0:T(8,128)(2,1)S(1)}, u32[]{:S(2)}, u32[]{:S(2)}) %collective-permute-start.8) | collective-permute-done | bytes 135200 | tf_op jit(solution)/shard_map/ppermute | solution.py:213
  26.4 3.1 %collective-permute-done.9.s3 = bf16[528,128]{1,0:T(8,128)(2,1)S(1)} collective-permute-done((bf16[528,128]{1,0:T(8,128)(2,1)S(1)}, bf16[528,128]{1,0:T(8,128)(2,1)S(1)}, u32[]{:S(2)}, u32[]{:S(2)}) %collective-permute-start.9) | collective-permute-done | bytes 135200 | tf_op jit(solution)/shard_map/ppermute | solution.py:213
  29.5 1.3 %collective-permute-start.11 = (bf16[5,128,640]{2,1,0:T(8,128)(2,1)S(1)}, bf16[5,128,640]{2,1,0:T(8,128)(2,1)S(1)}, u32[]{:S(2)}, u32[]{:S(2)}) collective-permute-start(bf16[5,128,640]{2,1,0:T(8,128)(2,1)S(1)} %fusion.6.k0), channel_id=1, source_target_pairs={{0,2},{1,3},{2,0},{3,1},{4,6},{5,7},{6,4},{7,5},{8,10},{9,11},{10,... | collective-permute-start | bytes 2457608 | tf_op jit(solution)/shard_map/ppermute | solution.py:213
  30.8 1.2 %wgrad.1 = (f32[5,32,608]{2,1,0:T(8,128)S(1)}, bf16[5,32,608]{2,1,0:T(8,128)(2,1)S(1)}, bf16[5,32,608]{2,1,0:T(8,128)(2,1)S(1)}, bf16[5,32,608]{2,1,0:T(8,128)(2,1)S(1)}) custom-call(f32[640,608]{1,0:T(8,128)S(1)} %near.1.start, bf16[528,128]{1,0:T(8,128)(2,1)S(1)} %collective-permute-done.8.s2, bf16[528,128]{1,0:T(8,128)(2,1)S(1)} %collective-permute-done.9.s3, ...), custom_call_target="tpu_custom_call" | custom-call | tf_op jit(solution)/shard_map/wgrad/pallas_call | solution.py:286
  32.0 1.5 %collective-permute-start.13 = (bf16[5,32,608]{2,1,0:T(8,128)(2,1)S(1)}, bf16[5,32,608]{2,1,0:T(8,128)(2,1)S(1)}, u32[]{:S(2)}, u32[]{:S(2)}) collective-permute-start(bf16[5,32,608]{2,1,0:T(8,128)(2,1)S(1)} %get-tuple-element.49), channel_id=1, source_target_pairs={{0,8},{1,9},{2,10},{3,11},{4,12},{5,13},{6,14},{7,15},{8,0},{9,1},... | collective-permute-start | bytes 583688 | tf_op jit(solution)/shard_map/ppermute | solution.py:213
  33.8 1.0 %collective-permute-start.15 = (bf16[5,32,608]{2,1,0:T(8,128)(2,1)S(1)}, bf16[5,32,608]{2,1,0:T(8,128)(2,1)S(1)}, u32[]{:S(2)}, u32[]{:S(2)}) collective-permute-start(bf16[5,32,608]{2,1,0:T(8,128)(2,1)S(1)} %get-tuple-element.51), channel_id=1, source_target_pairs={{0,12},{1,13},{2,14},{3,15},{4,8},{5,9},{6,10},{7,11},{8,4},{9,5},... | collective-permute-start | bytes 583688 | tf_op jit(solution)/shard_map/ppermute | solution.py:213
  34.7 5.9 %first.1 = (f32[512,608]{1,0:T(8,128)S(1)}, bf16[1024,512]{1,0:T(8,128)(2,1)S(1)}, f32[1024,256]{1,0:T(8,128)S(1)}, bf16[256,512]{1,0:T(8,128)(2,1)S(1)}, bf16[5...) custom-call(s32[2]{0:T(128)S(1)} %pad_add_fusion.place, bf16[528,128]{1,0:T(8,128)(2,1)S(1)} %get-tuple-element.39.s0, ...), custom_call_target="tpu_custom_call" | custom-call | tf_op jit(solution)/shard_map/first/pallas_call | solution.py:308
  40.6 2.4 %collective-permute-done.13 = bf16[5,32,608]{2,1,0:T(8,128)(2,1)S(1)} collective-permute-done((bf16[5,32,608]{2,1,0:T(8,128)(2,1)S(1)}, bf16[5,32,608]{2,1,0:T(8,128)(2,1)S(1)}, u32[]{:S(2)}, u32[]{:S(2)}) %collective-permute-start.13) | collective-permute-done | bytes 194592 | tf_op jit(solution)/shard_map/ppermute | solution.py:213
  43.0 9.2 %collective-permute-done.15 = bf16[5,32,608]{2,1,0:T(8,128)(2,1)S(1)} collective-permute-done((bf16[5,32,608]{2,1,0:T(8,128)(2,1)S(1)}, bf16[5,32,608]{2,1,0:T(8,128)(2,1)S(1)}, u32[]{:S(2)}, u32[]{:S(2)}) %collective-permute-start.15) | collective-permute-done | bytes 194592 | tf_op jit(solution)/shard_map/ppermute | solution.py:213
  52.3 0.9 %collective-permute-start.16 = (bf16[5,128,640]{2,1,0:T(8,128)(2,1)S(1)}, bf16[5,128,640]{2,1,0:T(8,128)(2,1)S(1)}, u32[]{:S(2)}, u32[]{:S(2)}) collective-permute-start(bf16[5,128,640]{2,1,0:T(8,128)(2,1)S(1)} %collective-permute-done.11.k2), channel_id=1, source_target_pairs={{0,1},{1,0},{2,3},{3,2},{4,5},{5,4},{6,7},{7,6},{8,9},{9,8},{10,11... | collective-permute-start | bytes 2457608 | tf_op jit(solution)/shard_map/ppermute | solution.py:213
  53.2 0.9 %add_bitcast_fusion = f32[32,5,608]{2,0,1:T(8,128)} fusion(bf16[5,32,608]{2,1,0:T(8,128)(2,1)S(1)} %collective-permute-done.15, bf16[5,32,608]{2,1,0:T(8,128)(2,1)S(1)} %collective-permute-done.14, f32[5,32,608]{2,1,0:T(8,128)S(1)} %get-tuple-element.60, bf16[5,32,608]{2,1,0:T(8,128)(2,1)S(1)} %collective-permute-done.13), kind=kLoop, calls=%fused_computation.8 | loop fusion | flops 583680 | bytes 1361920 | tf_op jit(solution)/shard_map/transpose | solution.py:346
  54.0 1.1 %collective-permute-done.16.k3 = bf16[5,128,640]{2,1,0:T(8,128)(2,1)S(1)} collective-permute-done((bf16[5,128,640]{2,1,0:T(8,128)(2,1)S(1)}, bf16[5,128,640]{2,1,0:T(8,128)(2,1)S(1)}, u32[]{:S(2)}, u32[]{:S(2)}) %collective-permute-start.16) | collective-permute-done | bytes 819232 | tf_op jit(solution)/shard_map/ppermute | solution.py:213
  55.1 3.7 %second.1 = (bf16[608,512]{1,0:T(8,128)(2,1)}, bf16[1024,512]{1,0:T(8,128)(2,1)}) custom-call(bf16[5,128,640]{2,1,0:T(8,128)(2,1)S(1)} %collective-permute-done.11.k2, bf16[5,128,640]{2,1,0:T(8,128)(2,1)S(1)} %collective-permute-done.16.k3, bf16[512,1280]{1,0:T(8,128)(2,1)S(1)} %get-tuple-element.53.columns, ...), custom_call_target="tpu_custom_call" | custom-call | tf_op jit(solution)/shard_map/second/pallas_call | solution.py:331
  (34 shorter events, 3.4 us)
Async XLA Ops:
  0.6 9.6 %copy-start = (bf16[1024,512]{1,0:T(8,128)(2,1)S(1)}, bf16[1024,512]{1,0:T(8,128)(2,1)}, u32[]{:S(2)}) copy-start(bf16[1024,512]{1,0:T(8,128)(2,1)} %act.3) | copy-start | bytes 3145732
  0.6 16.9 %copy-start.1 = (bf16[512,608]{0,1:T(8,128)(2,1)S(1)}, bf16[512,608]{0,1:T(8,128)(2,1)}, u32[]{:S(2)}) copy-start(bf16[512,608]{0,1:T(8,128)(2,1)} %param.5) | copy-start | bytes 1867780
  0.7 19.6 %collective-permute-start.1 = (bf16[5,32,608]{2,1,0:T(8,128)(2,1)}, bf16[5,32,608]{2,1,0:T(8,128)(2,1)S(1)}, u32[]{:S(2)}, u32[]{:S(2)}) collective-permute-start(bf16[5,32,608]{2,1,0:T(8,128)(2,1)} %bitcast.10), channel_id=1, source_target_pairs={{0,4},{1,5},{2,6},{3,7},{4,0},{5,1},{6,2},{7,3},{8,12},{9,13},{10,... | collective-permute-start | bytes 583688 | tf_op jit(solution)/shard_map/ppermute | solution.py:213
  0.7 11.7 %collective-permute-start = (bf16[5,32,608]{2,1,0:T(8,128)(2,1)}, bf16[5,32,608]{2,1,0:T(8,128)(2,1)}, u32[]{:S(2)}, u32[]{:S(2)}) collective-permute-start(bf16[5,32,608]{2,1,0:T(8,128)(2,1)} %bitcast.11), channel_id=1, source_target_pairs={{0,8},{1,9},{2,10},{3,11},{4,12},{5,13},{6,14},{7,15},{8,0},{9,1},... | collective-permute-start | bytes 583688 | tf_op jit(solution)/shard_map/ppermute | solution.py:213
  3.2 19.8 %copy-start.2 = (bf16[32,5,608]{2,0,1:T(8,128)(2,1)S(1)}, bf16[32,5,608]{2,0,1:T(8,128)(2,1)}, u32[]{:S(2)}) copy-start(bf16[32,5,608]{2,0,1:T(8,128)(2,1)} %param.4) | copy-start | bytes 583684
  3.2 17.5 %collective-permute-start.7 = (bf16[608,512]{1,0:T(8,128)(2,1)}, bf16[608,512]{1,0:T(8,128)(2,1)S(1)}, u32[]{:S(2)}, u32[]{:S(2)}) collective-permute-start(bf16[608,512]{1,0:T(8,128)(2,1)} %bitcast.7), channel_id=1, source_target_pairs={{0,2},{1,3},{2,0},{3,1},{4,6},{5,7},{6,4},{7,5},{8,10},{9,11},{10,... | collective-permute-start | bytes 1867784 | tf_op jit(solution)/shard_map/ppermute | solution.py:213
  6.6 10.9 %collective-permute-start.3 = (bf16[16,1120]{1,0:T(8,128)(2,1)S(1)}, bf16[16,1120]{1,0:T(8,128)(2,1)S(1)}, u32[]{:S(2)}, u32[]{:S(2)}) collective-permute-start(bf16[16,1120]{1,0:T(8,128)(2,1)S(1)} %pad_maximum_fusion), channel_id=1, source_target_pairs={{0,1},{1,2},{2,3},{3,4},{4,5},{5,6},{6,7},{7,8},{8,9},{9,10},{10,1... | collective-permute-start | bytes 107528 | tf_op jit(solution)/shard_map/ppermute | solution.py:250
  12.4 8.3 %collective-permute-start.2 = (bf16[5,32,608]{2,1,0:T(8,128)(2,1)}, bf16[5,32,608]{2,1,0:T(8,128)(2,1)S(1)}, u32[]{:S(2)}, u32[]{:S(2)}) collective-permute-start(bf16[5,32,608]{2,1,0:T(8,128)(2,1)} %collective-permute-done), channel_id=1, source_target_pairs={{0,4},{1,5},{2,6},{3,7},{4,0},{5,1},{6,2},{7,3},{8,12},{9,13},{10,... | collective-permute-start | bytes 583688 | tf_op jit(solution)/shard_map/ppermute | solution.py:213
  13.3 7.0 %collective-permute-start.4 = (bf16[16,1120]{1,0:T(8,128)(2,1)S(1)}, bf16[16,1120]{1,0:T(8,128)(2,1)S(1)}, u32[]{:S(2)}, u32[]{:S(2)}) collective-permute-start(bf16[16,1120]{1,0:T(8,128)(2,1)S(1)} %pad_maximum_fusion.1), channel_id=1, source_target_pairs={{1,0},{2,1},{3,2},{4,3},{5,4},{6,5},{7,6},{8,7},{9,8},{10,9},{11,1... | collective-permute-start | bytes 107528 | tf_op jit(solution)/shard_map/ppermute | solution.py:251
  17.6 6.5 %collective-permute-start.6 = (bf16[608,512]{1,0:T(8,128)(2,1)S(1)}, bf16[608,512]{1,0:T(8,128)(2,1)S(1)}, u32[]{:S(2)}, u32[]{:S(2)}) collective-permute-start(bf16[608,512]{1,0:T(8,128)(2,1)S(1)} %bitcast.8), channel_id=1, source_target_pairs={{0,1},{1,0},{2,3},{3,2},{4,5},{5,4},{6,7},{7,6},{8,9},{9,8},{10,11... | collective-permute-start | bytes 1867784 | tf_op jit(solution)/shard_map/ppermute | solution.py:213
  20.7 8.8 %collective-permute-start.10 = (bf16[608,512]{1,0:T(8,128)(2,1)S(1)}, bf16[608,512]{1,0:T(8,128)(2,1)S(1)}, u32[]{:S(2)}, u32[]{:S(2)}) collective-permute-start(bf16[608,512]{1,0:T(8,128)(2,1)S(1)} %collective-permute-done.7.c2), channel_id=1, source_target_pairs={{0,1},{1,0},{2,3},{3,2},{4,5},{5,4},{6,7},{7,6},{8,9},{9,8},{10,11... | collective-permute-start | bytes 1867784 | tf_op jit(solution)/shard_map/ppermute | solution.py:213
  20.8 3.3 %collective-permute-start.5 = (bf16[528,128]{1,0:T(8,128)(2,1)S(1)}, bf16[528,128]{1,0:T(8,128)(2,1)S(1)}, u32[]{:S(2)}, u32[]{:S(2)}) collective-permute-start(bf16[528,128]{1,0:T(8,128)(2,1)S(1)} %get-tuple-element.40.s1), channel_id=1, source_target_pairs={{0,1},{1,0},{2,3},{3,2},{4,5},{5,4},{6,7},{7,6},{8,9},{9,8},{10,11... | collective-permute-start | bytes 405512 | tf_op jit(solution)/shard_map/ppermute | solution.py:213
  21.3 5.2 %collective-permute-start.8 = (bf16[528,128]{1,0:T(8,128)(2,1)S(1)}, bf16[528,128]{1,0:T(8,128)(2,1)S(1)}, u32[]{:S(2)}, u32[]{:S(2)}) collective-permute-start(bf16[528,128]{1,0:T(8,128)(2,1)S(1)} %get-tuple-element.44.s2), channel_id=1, source_target_pairs={{0,2},{1,3},{2,0},{3,1},{4,6},{5,7},{6,4},{7,5},{8,10},{9,11},{10,... | collective-permute-start | bytes 405512 | tf_op jit(solution)/shard_map/ppermute | solution.py:213
  22.6 6.9 %collective-permute-start.9 = (bf16[528,128]{1,0:T(8,128)(2,1)S(1)}, bf16[528,128]{1,0:T(8,128)(2,1)S(1)}, u32[]{:S(2)}, u32[]{:S(2)}) collective-permute-start(bf16[528,128]{1,0:T(8,128)(2,1)S(1)} %get-tuple-element.45.s3), channel_id=1, source_target_pairs={{0,3},{1,2},{2,1},{3,0},{4,7},{5,6},{6,5},{7,4},{8,11},{9,10},{10,... | collective-permute-start | bytes 405512 | tf_op jit(solution)/shard_map/ppermute | solution.py:213
  25.3 9.4 %collective-permute-start.12 = (bf16[5,128,640]{2,1,0:T(8,128)(2,1)S(1)}, bf16[5,128,640]{2,1,0:T(8,128)(2,1)S(1)}, u32[]{:S(2)}, u32[]{:S(2)}) collective-permute-start(bf16[5,128,640]{2,1,0:T(8,128)(2,1)S(1)} %fusion.6.k0), channel_id=1, source_target_pairs={{0,1},{1,0},{2,3},{3,2},{4,5},{5,4},{6,7},{7,6},{8,9},{9,8},{10,11... | collective-permute-start | bytes 2457608 | tf_op jit(solution)/shard_map/ppermute | solution.py:213
  29.5 22.8 %collective-permute-start.11 = (bf16[5,128,640]{2,1,0:T(8,128)(2,1)S(1)}, bf16[5,128,640]{2,1,0:T(8,128)(2,1)S(1)}, u32[]{:S(2)}, u32[]{:S(2)}) collective-permute-start(bf16[5,128,640]{2,1,0:T(8,128)(2,1)S(1)} %fusion.6.k0), channel_id=1, source_target_pairs={{0,2},{1,3},{2,0},{3,1},{4,6},{5,7},{6,4},{7,5},{8,10},{9,11},{10,... | collective-permute-start | bytes 2457608 | tf_op jit(solution)/shard_map/ppermute | solution.py:213
  32.0 11.0 %collective-permute-start.13 = (bf16[5,32,608]{2,1,0:T(8,128)(2,1)S(1)}, bf16[5,32,608]{2,1,0:T(8,128)(2,1)S(1)}, u32[]{:S(2)}, u32[]{:S(2)}) collective-permute-start(bf16[5,32,608]{2,1,0:T(8,128)(2,1)S(1)} %get-tuple-element.49), channel_id=1, source_target_pairs={{0,8},{1,9},{2,10},{3,11},{4,12},{5,13},{6,14},{7,15},{8,0},{9,1},... | collective-permute-start | bytes 583688 | tf_op jit(solution)/shard_map/ppermute | solution.py:213
  33.6 9.5 %collective-permute-start.14 = (bf16[5,32,608]{2,1,0:T(8,128)(2,1)S(1)}, bf16[5,32,608]{2,1,0:T(8,128)(2,1)S(1)}, u32[]{:S(2)}, u32[]{:S(2)}) collective-permute-start(bf16[5,32,608]{2,1,0:T(8,128)(2,1)S(1)} %get-tuple-element.50), channel_id=1, source_target_pairs={{0,4},{1,5},{2,6},{3,7},{4,0},{5,1},{6,2},{7,3},{8,12},{9,13},{10,... | collective-permute-start | bytes 583688 | tf_op jit(solution)/shard_map/ppermute | solution.py:213
  33.8 18.5 %collective-permute-start.15 = (bf16[5,32,608]{2,1,0:T(8,128)(2,1)S(1)}, bf16[5,32,608]{2,1,0:T(8,128)(2,1)S(1)}, u32[]{:S(2)}, u32[]{:S(2)}) collective-permute-start(bf16[5,32,608]{2,1,0:T(8,128)(2,1)S(1)} %get-tuple-element.51), channel_id=1, source_target_pairs={{0,12},{1,13},{2,14},{3,15},{4,8},{5,9},{6,10},{7,11},{8,4},{9,5},... | collective-permute-start | bytes 583688 | tf_op jit(solution)/shard_map/ppermute | solution.py:213
  52.3 2.9 %collective-permute-start.16 = (bf16[5,128,640]{2,1,0:T(8,128)(2,1)S(1)}, bf16[5,128,640]{2,1,0:T(8,128)(2,1)S(1)}, u32[]{:S(2)}, u32[]{:S(2)}) collective-permute-start(bf16[5,128,640]{2,1,0:T(8,128)(2,1)S(1)} %collective-permute-done.11.k2), channel_id=1, source_target_pairs={{0,1},{1,0},{2,3},{3,2},{4,5},{5,4},{6,7},{7,6},{8,9},{9,8},{10,11... | collective-permute-start | bytes 2457608 | tf_op jit(solution)/shard_map/ppermute | solution.py:213
